TPU v7x, 32 devices: a whole 2x2x4 slice. The times are simulated.
32 devices in a mesh: stream: 4 (over z), span: 8 (over y, x, core).
Axes of the slice: x: 2, y: 2, z: 4, core: 2. Of those that a mesh axis runs over, the one named last changes fastest.
Arguments:
- pre_pops: float32 [19, 32, 64, 128], P(None, 'stream', 'span'), may hold values from 0.7 to 1.3
- main_pops: float32 [19, 32, 64, 256], P(None, 'stream', 'span'), may hold values from 0.7 to 1.3
- tile_map: int32 [8], replicated, may hold values from 0 to 7, each once
- layer_phase: int32 [8], replicated, may hold values from 0 to 1
- wall_flags: int32 [256], replicated, may hold values 0 or 1
Outputs:
- pre_out: float32 [19, 32, 64, 128], P(None, 'stream', 'span')
- main_out: float32 [19, 32, 64, 256], P(None, 'stream', 'span')
Inputs may be any that keep to these rules, and one draw needn't show every extreme that they name: `tile_map`: each precursor tile feeds exactly one inlet tile.
All inputs are finite; a program needn't handle non-finite values.
Results may differ from a plain program's by a relative error of at most 0.0003.
Values sent between devices are 32-bit elements; how exact they have to be, the bound alone decides.
No kernel may reach another device: no remote copies, remote signals or barrier semaphores. Data moves between devices by JAX's collectives and lax.ppermute only.
A program may use at most 64 MiB of HBM per device.

v0:
```python
import jax
import jax.numpy as jnp
from jax import lax
from jax.sharding import PartitionSpec as P

STEPS = 2


velocities = (
    (0, 0, 0),
    (1, 0, 0),
    (-1, 0, 0),
    (0, 1, 0),
    (0, -1, 0),
    (0, 0, 1),
    (0, 0, -1),
    (1, 1, 0),
    (-1, -1, 0),
    (1, -1, 0),
    (-1, 1, 0),
    (1, 0, 1),
    (-1, 0, -1),
    (1, 0, -1),
    (-1, 0, 1),
    (0, 1, 1),
    (0, -1, -1),
    (0, 1, -1),
    (0, -1, 1),
)
opposite = (0, 2, 1, 4, 3, 6, 5, 8, 7, 10, 9, 12, 11, 14, 13, 16, 15, 18, 17)
lattice_weights = (1.0 / 3.0,) + (1.0 / 18.0,) * 6 + (1.0 / 36.0,) * 12
incoming = (1, 7, 9, 11, 13)
backward_x = (2, 8, 10, 12, 14)
forward_z = (5, 11, 14, 15, 18)
backward_z = (6, 12, 13, 16, 17)
relax_rate = 1.25


def from_behind(shard, axis, by):
    size = lax.axis_size(axis)
    return lax.ppermute(shard, axis, [(i, (i + by) % size) for i in range(size)])


def collide(pops):
    density = jnp.zeros_like(pops[0])
    moment = [jnp.zeros_like(pops[0]) for axis_num in range(3)]
    for which_pop in range(19):
        weighted = lattice_weights[which_pop] * pops[which_pop]
        density = density + weighted
        for axis_num in range(3):
            if velocities[which_pop][axis_num] != 0:
                moment[axis_num] = moment[axis_num] + velocities[which_pop][axis_num] * weighted
    speed = [component / density for component in moment]
    square = speed[0] * speed[0] + speed[1] * speed[1] + speed[2] * speed[2]
    result = []
    for which_pop in range(19):
        projected = jnp.zeros_like(density)
        for axis_num in range(3):
            if velocities[which_pop][axis_num] != 0:
                projected = projected + velocities[which_pop][axis_num] * speed[axis_num]
        balance = density * (1.0 + 3.0 * projected + 4.5 * projected * projected - 1.5 * square)
        result.append(pops[which_pop] - relax_rate * (pops[which_pop] - balance))
    return jnp.stack(result)


def stream(padded, collided, solid):
    row_len = collided.shape[1]
    span_len = collided.shape[2]
    layers = collided.shape[3]
    walled = jnp.concatenate([jnp.ones((1,), jnp.int32), solid, jnp.ones((1,), jnp.int32)])
    result = []
    for which_pop in range(19):
        step_x, step_y, step_z = velocities[which_pop]
        source = padded[
            which_pop, 1 - step_x : 1 - step_x + row_len, 1 - step_z : 1 - step_z + span_len, :
        ]
        if step_y == 1:
            source = jnp.concatenate([jnp.zeros_like(source[..., :1]), source[..., :-1]], axis=-1)
        elif step_y == -1:
            source = jnp.concatenate([source[..., 1:], jnp.zeros_like(source[..., :1])], axis=-1)
        blocked = walled[1 - step_y : 1 - step_y + layers] > 0
        result.append(jnp.where(blocked, collided[opposite[which_pop]], source))
    return jnp.stack(result)


def spread_matrix(coarse_len, fine_len, tile_phase):
    fine_pos = jnp.arange(fine_len, dtype=jnp.int32) + tile_phase
    lower = (fine_pos - 1) // 2
    upper_wt = jnp.where(fine_pos % 2 == 0, 0.75, 0.25).astype(jnp.float32)
    low_idx = jnp.clip(lower, 0, coarse_len - 1)
    high_idx = jnp.clip(lower + 1, 0, coarse_len - 1)
    coarse_rows = jnp.arange(coarse_len, dtype=jnp.int32)[:, None]
    return jnp.where(coarse_rows == low_idx[None, :], 1.0 - upper_wt[None, :], 0.0) + jnp.where(
        coarse_rows == high_idx[None, :], upper_wt[None, :], 0.0
    )


def refine(coarse, tile_phase, fine_len):
    matrix = spread_matrix(coarse.shape[-1], fine_len, tile_phase)
    return jnp.dot(
        coarse, matrix, precision=lax.Precision.HIGHEST, preferred_element_type=jnp.float32
    )


def select_tiles(targets, piece):
    shard_rows = jnp.arange(piece.shape[0], dtype=jnp.int32)

    def pick_one(target_tile, source):
        matches = (shard_rows == target_tile)[:, None, None, None]
        return jnp.sum(jnp.where(matches, source, 0.0), axis=0)

    return (
        pick_one(targets[0], piece[:, :, -1:, :]),
        pick_one(targets[1], piece),
        pick_one(targets[2], piece[:, :, :1, :]),
    )


def extend_rows(star, lower_rows, upper_rows):
    pieces = []
    zero_row = jnp.zeros_like(star[0, :1])
    for which_pop in range(19):
        low_part = lower_rows[incoming.index(which_pop)] if which_pop in incoming else zero_row
        high_part = upper_rows[backward_x.index(which_pop)] if which_pop in backward_x else zero_row
        pieces.append(jnp.concatenate([low_part, star[which_pop], high_part], axis=0))
    return jnp.stack(pieces)


def extend_columns(widened, left_cols, right_cols):
    pieces = []
    zero_col = jnp.zeros_like(widened[0, :, :1])
    for which_pop in range(19):
        left_part = left_cols[forward_z.index(which_pop)] if which_pop in forward_z else zero_col
        right_part = (
            right_cols[backward_z.index(which_pop)] if which_pop in backward_z else zero_col
        )
        pieces.append(jnp.concatenate([left_part, widened[which_pop], right_part], axis=1))
    return jnp.stack(pieces)


def crossing_faces(pre_star, main_star):

    def last_rows(star):
        return jnp.stack([star[which_pop, -1:] for which_pop in incoming])

    def first_rows(star):
        return jnp.stack([star[which_pop, :1] for which_pop in backward_x])

    pre_low, main_low = from_behind((last_rows(pre_star), last_rows(main_star)), "stream", 1)
    pre_high, main_high = from_behind((first_rows(pre_star), first_rows(main_star)), "stream", -1)
    pre_wide = extend_rows(pre_star, pre_low, pre_high)
    main_wide = extend_rows(main_star, main_low, main_high)

    def last_cols(widened):
        return jnp.stack([widened[which_pop, :, -1:] for which_pop in forward_z])

    def first_cols(widened):
        return jnp.stack([widened[which_pop, :, :1] for which_pop in backward_z])

    pre_left, main_left = from_behind((last_cols(pre_wide), last_cols(main_wide)), "span", 1)
    pre_right, main_right = from_behind((first_cols(pre_wide), first_cols(main_wide)), "span", -1)
    return (
        extend_columns(pre_wide, pre_left, pre_right),
        extend_columns(main_wide, main_left, main_right),
    )


def local(pre_pops, main_pops, tile_map, layer_phase, wall_flags):
    span_count = lax.axis_size("span")
    stream_count = lax.axis_size("stream")
    span_pos = lax.axis_index("span")
    stream_pos = lax.axis_index("stream")
    coarse_len = pre_pops.shape[3]
    fine_len = main_pops.shape[3]
    solid_coarse = jnp.max(wall_flags.reshape(coarse_len, 2), axis=1)
    left_pos = (span_pos + span_count - 1) % span_count
    right_pos = (span_pos + 1) % span_count
    targets = (tile_map[left_pos], tile_map[span_pos], tile_map[right_pos])
    own_phase = jnp.sum(jnp.where(tile_map == span_pos, layer_phase, 0))
    for step_num in range(STEPS):
        pre_star = collide(pre_pops)
        main_star = collide(main_pops)
        outflow = jnp.stack([pre_star[which_pop, -1] for which_pop in incoming])
        fine_out = refine(outflow, own_phase, fine_len)
        picked = select_tiles(targets, lax.all_gather(fine_out[None], "span", axis=0, tiled=True))
        inflow = jnp.concatenate([picked[0], picked[1], picked[2]], axis=1)
        pre_pad, main_pad = crossing_faces(pre_star, main_star)
        ghost_plane = main_pad[:, 0]
        inlet_rows = []
        for which_pop in range(19):
            if which_pop in incoming:
                inlet_rows.append(inflow[incoming.index(which_pop)])
            else:
                inlet_rows.append(ghost_plane[which_pop])
        inlet_plane = jnp.stack(inlet_rows)
        first_plane = jnp.where(stream_pos == 0, inlet_plane, ghost_plane)
        last_plane = jnp.where(stream_pos == stream_count - 1, main_pad[:, -2], main_pad[:, -1])
        main_pad = jnp.concatenate(
            [first_plane[:, None], main_pad[:, 1:-1], last_plane[:, None]], axis=1
        )
        pre_pops = stream(pre_pad, pre_star, solid_coarse)
        main_pops = stream(main_pad, main_star, wall_flags)
    return (pre_pops, main_pops)


def solution(mesh):
    return jax.shard_map(
        local,
        mesh=mesh,
        in_specs=(P(None, "stream", "span", None), P(None, "stream", "span", None), P(), P(), P()),
        out_specs=(P(None, "stream", "span", None), P(None, "stream", "span", None)),
        check_vma=False,
    )
```

profile of v0, /device:TPU:0, one launch (start us, length us, event | category | flops | bytes accessed | tf_op | source)
XLA Modules:
  0.0 91.7 jit_solution(3518954262550217660)
XLA Ops:
  0.6 1.2 %multiply_add_fusion.21 = (f32[1,8,8,128]{3,2,1,0:T(8,128)S(1)}, f32[1,8,8,128]{3,2,1,0:T(8,128)S(1)}, f32[1,8,8,128]{3,2,1,0:T(8,128)S(1)}, f32[1,8,8,128]{3,2,1,0:T(8,128)S(1)}) fusion(f32[19,8,8,128]{3,2,1,0:T(8,128)} %param.5), kind=kLoop, calls=%fused_computation.1530 | loop fusion | flops 573440 | bytes 753664 | tf_op jit(solution)/shard_map/add | solution.py:61
  1.9 0.9 %multiply_add_fusion.23 = (f32[1,8,8,128]{3,2,1,0:T(8,128)S(1)}, f32[1,8,8,128]{3,2,1,0:T(8,128)S(1)}) fusion(f32[1,8,8,128]{3,2,1,0:T(8,128)S(1)} %get-tuple-element.96, f32[1,8,8,128]{3,2,1,0:T(8,128)S(1)} %get-tuple-element.97, f32[19,8,8,128]{3,2,1,0:T(8,128)} %param.5), kind=kLoop, calls=%fused_computation.1532 | loop fusion | flops 196608 | bytes 458752 | tf_op jit(solution)/shard_map/add | solution.py:61
  2.8 1.0 %multiply_multiply_fusion.74 = (f32[1,8,8,128]{3,2,1,0:T(8,128)S(1)}, f32[1,8,8,128]{3,2,1,0:T(8,128)S(1)}, f32[1,8,8,128]{3,2,1,0:T(8,128)S(1)}, f32[1,8,8,128]...) fusion(f32[1,8,8,128]{3,2,1,0:T(8,128)S(1)} %get-tuple-element., ...), kind=kLoop, calls=%fused_computation.1136 | loop fusion | flops 434176 | bytes 1376256 | tf_op jit(solution)/shard_map/mul | solution.py:61
  4.5 0.6 constant_dynamic-update-slice_fusion.3
  5.1 0.6 constant_dynamic-update-slice_fusion.2
  5.7 0.6 constant_dynamic-update-slice_fusion.1
  6.3 0.6 constant_dynamic-update-slice_fusion
  6.9 3.0 %collective-permute-start = (f32[5,1,8,128]{3,2,1,0:T(8,128)}, f32[5,1,8,128]{3,2,1,0:T(8,128)}, u32[]{:S(2)}, u32[]{:S(2)}) collective-permute-start(f32[5,1,8,128]{3,2,1,0:T(8,128)} %constant_dynamic-update-slice_fusion), channel_id=1, source_target_pairs={{0,8},{8,16},{16,24},{24,0},{1,9},{9,17},{17,25},{25,1},{2,10},{10... | collective-permute-start | bytes 61448 | tf_op jit(solution)/shard_map/ppermute | solution.py:41
  9.9 0.6 constant_dynamic-update-slice_fusion.9
  10.5 0.6 constant_dynamic-update-slice_fusion.8
  11.1 0.6 constant_dynamic-update-slice_fusion.7
  11.7 0.6 constant_dynamic-update-slice_fusion.6
  12.9 2.0 %collective-permute-start.1 = (f32[5,1,8,128]{3,2,1,0:T(8,128)}, f32[5,1,8,128]{3,2,1,0:T(8,128)}, u32[]{:S(2)}, u32[]{:S(2)}) collective-permute-start(f32[5,1,8,128]{3,2,1,0:T(8,128)} %constant_dynamic-update-slice_fusion.5), channel_id=1, source_target_pairs={{0,24},{8,0},{16,8},{24,16},{1,25},{9,1},{17,9},{25,17},{2,26},{10... | collective-permute-start | bytes 61448 | tf_op jit(solution)/shard_map/ppermute | solution.py:41
  15.4 0.6 constant_dynamic-update-slice_fusion.73
  16.0 0.6 constant_dynamic-update-slice_fusion.72
  16.6 0.6 constant_dynamic-update-slice_fusion.71
  17.2 0.6 constant_dynamic-update-slice_fusion.70
  17.8 0.6 constant_dynamic-update-slice_fusion.67
  18.4 0.6 constant_dynamic-update-slice_fusion.66
  19.0 0.6 constant_dynamic-update-slice_fusion.69
  19.6 0.6 constant_dynamic-update-slice_fusion.64
  20.2 2.0 %collective-permute-start.8 = (f32[5,1,8,256]{3,2,1,0:T(8,128)}, f32[5,1,8,256]{3,2,1,0:T(8,128)}, u32[]{:S(2)}, u32[]{:S(2)}) collective-permute-start(f32[5,1,8,256]{3,2,1,0:T(8,128)} %constant_dynamic-update-slice_fusion.64), channel_id=1, source_target_pairs={{0,24},{8,0},{16,8},{24,16},{1,25},{9,1},{17,9},{25,17},{2,26},{10... | collective-permute-start | bytes 122888 | tf_op jit(solution)/shard_map/ppermute | solution.py:41
  23.5 0.6 fusion.825
  24.2 0.7 compare_select_fusion.2
  24.9 0.7 add_clamp_fusion
  25.6 0.7 fusion.861
  26.2 1.2 %iota_compare_fusion.7 = pred[8]{0:T(512)(128)(4,1)} fusion(s32[]{:T(128)} %bitcast.213), kind=kLoop, calls=%fused_computation.1777 | loop fusion | flops 8 | bytes 12 | tf_op jit(solution)/shard_map/eq | solution.py:109
  27.4 0.7 slice_compare_fusion.2
  28.1 0.6 slice_compare_fusion
  28.7 1.9 %iota_compare_fusion.6 = (pred[8]{0:T(512)(128)(4,1)}, pred[8]{0:T(512)(128)(4,1)}) fusion(s32[]{:T(128)} %bitcast.214, s32[]{:T(128)} %bitcast.205), kind=kLoop, calls=%fused_computation.1776 | loop fusion | flops 16 | bytes 24 | tf_op jit(solution)/shard_map/eq | solution.py:109
  30.6 0.7 fusion.136
  31.8 9.7 %all-gather = f32[40,8,256]{2,1,0:T(8,128)S(1)} all-gather(f32[5,8,256]{2,1,0:T(8,128)S(1)} %fusion.70), channel_id=2, replica_groups=mesh['stream'=4,'span'=8] {'span'}, dimensions={0}, use_global_device_ids=true | all-gather | bytes 368640 | tf_op jit(solution)/shard_map/all_gather | solution.py:185
  41.5 0.7 slice_bitcast_fusion.137
  42.2 0.7 slice_bitcast_fusion.138
  43.0 1.5 %collective-permute-start.3 = (f32[5,10,1,128]{3,2,1,0:T(1,128)S(1)}, f32[5,10,1,128]{3,2,1,0:T(1,128)S(1)}, u32[]{:S(2)}, u32[]{:S(2)}) collective-permute-start(f32[5,10,1,128]{3,2,1,0:T(1,128)S(1)} %constant_dynamic-update-slice_fusion.15), channel_id=1, source_target_pairs={{0,7},{1,0},{2,1},{3,2},{4,3},{5,4},{6,5},{7,6},{8,15},{9,8},{10,9... | collective-permute-start | bytes 76808 | tf_op jit(solution)/shard_map/ppermute | solution.py:41
  44.5 0.8 slice_bitcast_fusion.99
  45.3 0.8 slice_bitcast_fusion.96
  46.4 0.9 fusion.554
  48.2 3.4 %collective-permute-done.2 = f32[5,10,1,128]{3,2,1,0:T(1,128)S(1)} collective-permute-done((f32[5,10,1,128]{3,2,1,0:T(1,128)S(1)}, f32[5,10,1,128]{3,2,1,0:T(1,128)S(1)}, u32[]{:S(2)}, u32[]{:S(2)}) %collective-permute-start.2) | collective-permute-done | bytes 25632 | tf_op jit(solution)/shard_map/ppermute | solution.py:41
  52.9 9.4 %all-gather.1 = f32[40,8,256]{2,1,0:T(8,128)S(1)} all-gather(f32[5,8,256]{2,1,0:T(8,128)S(1)} %fusion.68), channel_id=3, replica_groups=mesh['stream'=4,'span'=8] {'span'}, dimensions={0}, use_global_device_ids=true | all-gather | bytes 368640 | tf_op jit(solution)/shard_map/all_gather | solution.py:185
  63.0 3.8 %collective-permute-start.5 = (f32[5,1,8,128]{3,2,1,0:T(8,128)S(1)}, f32[5,1,8,128]{3,2,1,0:T(8,128)S(1)}, u32[]{:S(2)}, u32[]{:S(2)}) collective-permute-start(f32[5,1,8,128]{3,2,1,0:T(8,128)S(1)} %constant_dynamic-update-slice_fusion.25), channel_id=1, source_target_pairs={{0,24},{8,0},{16,8},{24,16},{1,25},{9,1},{17,9},{25,17},{2,26},{10... | collective-permute-start | bytes 61448 | tf_op jit(solution)/shard_map/ppermute | solution.py:41
  68.7 4.0 %collective-permute-done.6 = f32[5,10,1,128]{3,2,1,0:T(1,128)S(1)} collective-permute-done((f32[5,10,1,128]{3,2,1,0:T(1,128)S(1)}, f32[5,10,1,128]{3,2,1,0:T(1,128)S(1)}, u32[]{:S(2)}, u32[]{:S(2)}) %collective-permute-start.6) | collective-permute-done | bytes 25632 | tf_op jit(solution)/shard_map/ppermute | solution.py:41
  76.4 1.2 %collective-permute-start.13 = (f32[5,1,8,256]{3,2,1,0:T(8,128)S(1)}, f32[5,1,8,256]{3,2,1,0:T(8,128)S(1)}, u32[]{:S(2)}, u32[]{:S(2)}) collective-permute-start(f32[5,1,8,256]{3,2,1,0:T(8,128)S(1)} %constant_dynamic-update-slice_fusion.132), channel_id=1, source_target_pairs={{0,8},{8,16},{16,24},{24,0},{1,9},{9,17},{17,25},{25,1},{2,10},{10... | collective-permute-start | bytes 122888 | tf_op jit(solution)/shard_map/ppermute | solution.py:41
  77.7 3.0 %collective-permute-start.12 = (f32[5,1,8,256]{3,2,1,0:T(8,128)S(1)}, f32[5,1,8,256]{3,2,1,0:T(8,128)S(1)}, u32[]{:S(2)}, u32[]{:S(2)}) collective-permute-start(f32[5,1,8,256]{3,2,1,0:T(8,128)S(1)} %constant_dynamic-update-slice_fusion.127), channel_id=1, source_target_pairs={{0,24},{8,0},{16,8},{24,16},{1,25},{9,1},{17,9},{25,17},{2,26},{10... | collective-permute-start | bytes 122888 | tf_op jit(solution)/shard_map/ppermute | solution.py:41
  81.4 1.4 %collective-permute-done.13 = f32[5,1,8,256]{3,2,1,0:T(8,128)S(1)} collective-permute-done((f32[5,1,8,256]{3,2,1,0:T(8,128)S(1)}, f32[5,1,8,256]{3,2,1,0:T(8,128)S(1)}, u32[]{:S(2)}, u32[]{:S(2)}) %collective-permute-start.13) | collective-permute-done | bytes 40992 | tf_op jit(solution)/shard_map/ppermute | solution.py:41
  83.2 2.7 %collective-permute-start.15 = (f32[5,10,1,256]{3,2,1,0:T(1,128)S(1)}, f32[5,10,1,256]{3,2,1,0:T(1,128)S(1)}, u32[]{:S(2)}, u32[]{:S(2)}) collective-permute-start(f32[5,10,1,256]{3,2,1,0:T(1,128)S(1)} %constant_dynamic-update-slice_fusion.142), channel_id=1, source_target_pairs={{0,7},{1,0},{2,1},{3,2},{4,3},{5,4},{6,5},{7,6},{8,15},{9,8},{10,9... | collective-permute-start | bytes 153608 | tf_op jit(solution)/shard_map/ppermute | solution.py:41
  86.1 1.6 %collective-permute-done.15 = f32[5,10,1,256]{3,2,1,0:T(1,128)S(1)} collective-permute-done((f32[5,10,1,256]{3,2,1,0:T(1,128)S(1)}, f32[5,10,1,256]{3,2,1,0:T(1,128)S(1)}, u32[]{:S(2)}, u32[]{:S(2)}) %collective-permute-start.15) | collective-permute-done | bytes 51232 | tf_op jit(solution)/shard_map/ppermute | solution.py:41
  90.7 1.0 %copy-done.11 = f32[19,8,8,256]{3,2,1,0:T(8,128)} copy-done((f32[19,8,8,256]{3,2,1,0:T(8,128)}, f32[19,8,8,256]{3,2,1,0:T(8,128)S(1)}, u32[]{:S(2)}) %copy-start.11) | copy-done | bytes 1245208
  (389 shorter events, 14.9 us)
Async XLA Ops:
  0.6 14.3 %copy-start = (f32[19,8,8,256]{3,2,1,0:T(8,128)S(1)}, f32[19,8,8,256]{3,2,1,0:T(8,128)}, u32[]{:S(2)}) copy-start(f32[19,8,8,256]{3,2,1,0:T(8,128)} %param.6) | copy-start | bytes 3735556
  3.8 18.4 %copy-start.1 = (f32[19,8,8,128]{3,2,1,0:T(8,128)S(1)}, f32[19,8,8,128]{3,2,1,0:T(8,128)}, u32[]{:S(2)}) copy-start(f32[19,8,8,128]{3,2,1,0:T(8,128)} %param.5) | copy-start | bytes 1867780
  6.9 34.6 %collective-permute-start = (f32[5,1,8,128]{3,2,1,0:T(8,128)}, f32[5,1,8,128]{3,2,1,0:T(8,128)}, u32[]{:S(2)}, u32[]{:S(2)}) collective-permute-start(f32[5,1,8,128]{3,2,1,0:T(8,128)} %constant_dynamic-update-slice_fusion), channel_id=1, source_target_pairs={{0,8},{8,16},{16,24},{24,0},{1,9},{9,17},{17,25},{25,1},{2,10},{10... | collective-permute-start | bytes 61448 | tf_op jit(solution)/shard_map/ppermute | solution.py:41
  12.9 29.3 %collective-permute-start.1 = (f32[5,1,8,128]{3,2,1,0:T(8,128)}, f32[5,1,8,128]{3,2,1,0:T(8,128)}, u32[]{:S(2)}, u32[]{:S(2)}) collective-permute-start(f32[5,1,8,128]{3,2,1,0:T(8,128)} %constant_dynamic-update-slice_fusion.5), channel_id=1, source_target_pairs={{0,24},{8,0},{16,8},{24,16},{1,25},{9,1},{17,9},{25,17},{2,26},{10... | collective-permute-start | bytes 61448 | tf_op jit(solution)/shard_map/ppermute | solution.py:41
  15.1 7.5 %copy-start.10 = (s32[256]{0:T(256)S(1)}, s32[256]{0:T(256)}, u32[]{:S(2)}) copy-start(s32[256]{0:T(256)} %param.9) | copy-start | bytes 3076
  15.2 8.4 %copy-start.9 = (s32[8]{0:T(128)S(1)}, s32[8]{0:T(128)}, u32[]{:S(2)}) copy-start(s32[8]{0:T(128)} %param.7) | copy-start | bytes 100
  15.2 8.4 %copy-start.24 = (s32[8]{0:T(128)S(1)}, s32[8]{0:T(128)}, u32[]{:S(2)}) copy-start(s32[8]{0:T(128)} %param.8) | copy-start | bytes 100
  20.2 24.2 %collective-permute-start.8 = (f32[5,1,8,256]{3,2,1,0:T(8,128)}, f32[5,1,8,256]{3,2,1,0:T(8,128)}, u32[]{:S(2)}, u32[]{:S(2)}) collective-permute-start(f32[5,1,8,256]{3,2,1,0:T(8,128)} %constant_dynamic-update-slice_fusion.64), channel_id=1, source_target_pairs={{0,24},{8,0},{16,8},{24,16},{1,25},{9,1},{17,9},{25,17},{2,26},{10... | collective-permute-start | bytes 122888 | tf_op jit(solution)/shard_map/ppermute | solution.py:41
  22.3 23.0 %collective-permute-start.9 = (f32[5,1,8,256]{3,2,1,0:T(8,128)}, f32[5,1,8,256]{3,2,1,0:T(8,128)}, u32[]{:S(2)}, u32[]{:S(2)}) collective-permute-start(f32[5,1,8,256]{3,2,1,0:T(8,128)} %get-tuple-element.208), channel_id=1, source_target_pairs={{0,8},{8,16},{16,24},{24,0},{1,9},{9,17},{17,25},{25,1},{2,10},{10... | collective-permute-start | bytes 122888 | tf_op jit(solution)/shard_map/ppermute | solution.py:41
  22.4 9.2 %copy-start.2 = (f32[8,8,128]{2,1,0:T(8,128)}, f32[8,8,128]{2,1,0:T(8,128)S(1)}, u32[]{:S(2)}) copy-start(f32[8,8,128]{2,1,0:T(8,128)S(1)} %get-tuple-element.91) | copy-start | bytes 98308
  24.8 6.7 %copy-start.15 = (f32[256]{0:T(256)}, f32[256]{0:T(256)S(1)}, u32[]{:S(2)}) copy-start(f32[256]{0:T(256)S(1)} %get-tuple-element.488) | copy-start | bytes 3076
  24.8 6.7 %copy-start.17 = (f32[256]{0:T(256)}, f32[256]{0:T(256)S(1)}, u32[]{:S(2)}) copy-start(f32[256]{0:T(256)S(1)} %get-tuple-element.489) | copy-start | bytes 3076
  25.5 6.0 %copy-start.19 = (s32[256]{0:T(256)}, s32[256]{0:T(256)S(1)}, u32[]{:S(2)}) copy-start(s32[256]{0:T(256)S(1)} %get-tuple-element.490) | copy-start | bytes 3076
  25.5 6.0 %copy-start.21 = (s32[256]{0:T(256)}, s32[256]{0:T(256)S(1)}, u32[]{:S(2)}) copy-start(s32[256]{0:T(256)S(1)} %get-tuple-element.491) | copy-start | bytes 3076
  42.9 9.1 %copy-start.3 = (f32[1,10,10,128]{3,2,1,0:T(8,128)S(1)}, f32[1,10,10,128]{3,2,1,0:T(8,128)}, u32[]{:S(2)}) copy-start(f32[1,10,10,128]{3,2,1,0:T(8,128)} %fusion.136) | copy-start | bytes 153604
  42.9 9.1 %copy-start.4 = (pred[128]{0:T(512)(128)(4,1)S(1)}, pred[128]{0:T(512)(128)(4,1)}, u32[]{:S(2)}) copy-start(pred[128]{0:T(512)(128)(4,1)} %broadcast_compare_fusion.1) | copy-start | bytes 388
  42.9 9.1 %copy-start.6 = (pred[128]{0:T(512)(128)(4,1)S(1)}, pred[128]{0:T(512)(128)(4,1)}, u32[]{:S(2)}) copy-start(pred[128]{0:T(512)(128)(4,1)} %get-tuple-element.475) | copy-start | bytes 388
  42.9 9.1 %copy-start.8 = (pred[128]{0:T(512)(128)(4,1)S(1)}, pred[128]{0:T(512)(128)(4,1)}, u32[]{:S(2)}) copy-start(pred[128]{0:T(512)(128)(4,1)} %get-tuple-element.474) | copy-start | bytes 388
  43.0 3.4 %collective-permute-start.3 = (f32[5,10,1,128]{3,2,1,0:T(1,128)S(1)}, f32[5,10,1,128]{3,2,1,0:T(1,128)S(1)}, u32[]{:S(2)}, u32[]{:S(2)}) collective-permute-start(f32[5,10,1,128]{3,2,1,0:T(1,128)S(1)} %constant_dynamic-update-slice_fusion.15), channel_id=1, source_target_pairs={{0,7},{1,0},{2,1},{3,2},{4,3},{5,4},{6,5},{7,6},{8,15},{9,8},{10,9... | collective-permute-start | bytes 76808 | tf_op jit(solution)/shard_map/ppermute | solution.py:41
  46.2 20.7 %collective-permute-start.11 = (f32[5,10,1,256]{3,2,1,0:T(1,128)S(1)}, f32[5,10,1,256]{3,2,1,0:T(1,128)S(1)}, u32[]{:S(2)}, u32[]{:S(2)}) collective-permute-start(f32[5,10,1,256]{3,2,1,0:T(1,128)S(1)} %constant_dynamic-update-slice_fusion.79), channel_id=1, source_target_pairs={{0,7},{1,0},{2,1},{3,2},{4,3},{5,4},{6,5},{7,6},{8,15},{9,8},{10,9... | collective-permute-start | bytes 153608 | tf_op jit(solution)/shard_map/ppermute | solution.py:41
  47.4 4.2 %collective-permute-start.2 = (f32[5,10,1,128]{3,2,1,0:T(1,128)S(1)}, f32[5,10,1,128]{3,2,1,0:T(1,128)S(1)}, u32[]{:S(2)}, u32[]{:S(2)}) collective-permute-start(f32[5,10,1,128]{3,2,1,0:T(1,128)S(1)} %constant_dynamic-update-slice_fusion.10), channel_id=1, source_target_pairs={{0,1},{1,2},{2,3},{3,4},{4,5},{5,6},{6,7},{7,0},{8,9},{9,10},{10,1... | collective-permute-start | bytes 76808 | tf_op jit(solution)/shard_map/ppermute | solution.py:41
  47.8 4.8 %copy-start.16 = (f32[256]{0:T(256)S(1)}, f32[256]{0:T(256)}, u32[]{:S(2)}) copy-start(f32[256]{0:T(256)} %copy-done.15) | copy-start | bytes 3076
  47.8 4.9 %copy-start.18 = (f32[256]{0:T(256)S(1)}, f32[256]{0:T(256)}, u32[]{:S(2)}) copy-start(f32[256]{0:T(256)} %copy-done.17) | copy-start | bytes 3076
  47.8 4.9 %copy-start.20 = (s32[256]{0:T(256)S(1)}, s32[256]{0:T(256)}, u32[]{:S(2)}) copy-start(s32[256]{0:T(256)} %copy-done.19) | copy-start | bytes 3076
  47.8 4.9 %copy-start.22 = (s32[256]{0:T(256)S(1)}, s32[256]{0:T(256)}, u32[]{:S(2)}) copy-start(s32[256]{0:T(256)} %copy-done.21) | copy-start | bytes 3076
  47.9 14.4 %copy-start.12 = (pred[8]{0:T(512)(128)(4,1)S(1)}, pred[8]{0:T(512)(128)(4,1)}, u32[]{:S(2)}) copy-start(pred[8]{0:T(512)(128)(4,1)} %get-tuple-element.492) | copy-start | bytes 28
  48.0 14.4 %copy-start.13 = (pred[8]{0:T(512)(128)(4,1)S(1)}, pred[8]{0:T(512)(128)(4,1)}, u32[]{:S(2)}) copy-start(pred[8]{0:T(512)(128)(4,1)} %get-tuple-element.493) | copy-start | bytes 28
  48.0 14.7 %copy-start.23 = (pred[8]{0:T(512)(128)(4,1)S(1)}, pred[8]{0:T(512)(128)(4,1)}, u32[]{:S(2)}) copy-start(pred[8]{0:T(512)(128)(4,1)} %iota_compare_fusion.7) | copy-start | bytes 28
  52.0 15.0 %copy-start.5 = (pred[256]{0:T(512)(128)(4,1)S(1)}, pred[256]{0:T(512)(128)(4,1)}, u32[]{:S(2)}) copy-start(pred[256]{0:T(512)(128)(4,1)} %get-tuple-element.487) | copy-start | bytes 772
  52.6 10.3 %collective-permute-start.4 = (f32[5,1,8,128]{3,2,1,0:T(8,128)S(1)}, f32[5,1,8,128]{3,2,1,0:T(8,128)S(1)}, u32[]{:S(2)}, u32[]{:S(2)}) collective-permute-start(f32[5,1,8,128]{3,2,1,0:T(8,128)S(1)} %constant_dynamic-update-slice_fusion.20), channel_id=1, source_target_pairs={{0,8},{8,16},{16,24},{24,0},{1,9},{9,17},{17,25},{25,1},{2,10},{10... | collective-permute-start | bytes 61448 | tf_op jit(solution)/shard_map/ppermute | solution.py:41
  63.0 5.3 %collective-permute-start.5 = (f32[5,1,8,128]{3,2,1,0:T(8,128)S(1)}, f32[5,1,8,128]{3,2,1,0:T(8,128)S(1)}, u32[]{:S(2)}, u32[]{:S(2)}) collective-permute-start(f32[5,1,8,128]{3,2,1,0:T(8,128)S(1)} %constant_dynamic-update-slice_fusion.25), channel_id=1, source_target_pairs={{0,24},{8,0},{16,8},{24,16},{1,25},{9,1},{17,9},{25,17},{2,26},{10... | collective-permute-start | bytes 61448 | tf_op jit(solution)/shard_map/ppermute | solution.py:41
  67.4 5.9 %collective-permute-start.10 = (f32[5,10,1,256]{3,2,1,0:T(1,128)S(1)}, f32[5,10,1,256]{3,2,1,0:T(1,128)S(1)}, u32[]{:S(2)}, u32[]{:S(2)}) collective-permute-start(f32[5,10,1,256]{3,2,1,0:T(1,128)S(1)} %constant_dynamic-update-slice_fusion.74), channel_id=1, source_target_pairs={{0,1},{1,2},{2,3},{3,4},{4,5},{5,6},{6,7},{7,0},{8,9},{9,10},{10,1... | collective-permute-start | bytes 153608 | tf_op jit(solution)/shard_map/ppermute | solution.py:41
  68.5 4.2 %collective-permute-start.6 = (f32[5,10,1,128]{3,2,1,0:T(1,128)S(1)}, f32[5,10,1,128]{3,2,1,0:T(1,128)S(1)}, u32[]{:S(2)}, u32[]{:S(2)}) collective-permute-start(f32[5,10,1,128]{3,2,1,0:T(1,128)S(1)} %constant_dynamic-update-slice_fusion.30), channel_id=1, source_target_pairs={{0,1},{1,2},{2,3},{3,4},{4,5},{5,6},{6,7},{7,0},{8,9},{9,10},{10,1... | collective-permute-start | bytes 76808 | tf_op jit(solution)/shard_map/ppermute | solution.py:41
  73.1 7.6 %collective-permute-start.7 = (f32[5,10,1,128]{3,2,1,0:T(1,128)S(1)}, f32[5,10,1,128]{3,2,1,0:T(1,128)S(1)}, u32[]{:S(2)}, u32[]{:S(2)}) collective-permute-start(f32[5,10,1,128]{3,2,1,0:T(1,128)S(1)} %constant_dynamic-update-slice_fusion.35), channel_id=1, source_target_pairs={{0,7},{1,0},{2,1},{3,2},{4,3},{5,4},{6,5},{7,6},{8,15},{9,8},{10,9... | collective-permute-start | bytes 76808 | tf_op jit(solution)/shard_map/ppermute | solution.py:41
  74.8 0.7 copy-start.7
  76.4 6.4 %collective-permute-start.13 = (f32[5,1,8,256]{3,2,1,0:T(8,128)S(1)}, f32[5,1,8,256]{3,2,1,0:T(8,128)S(1)}, u32[]{:S(2)}, u32[]{:S(2)}) collective-permute-start(f32[5,1,8,256]{3,2,1,0:T(8,128)S(1)} %constant_dynamic-update-slice_fusion.132), channel_id=1, source_target_pairs={{0,8},{8,16},{16,24},{24,0},{1,9},{9,17},{17,25},{25,1},{2,10},{10... | collective-permute-start | bytes 122888 | tf_op jit(solution)/shard_map/ppermute | solution.py:41
  77.7 5.2 %collective-permute-start.12 = (f32[5,1,8,256]{3,2,1,0:T(8,128)S(1)}, f32[5,1,8,256]{3,2,1,0:T(8,128)S(1)}, u32[]{:S(2)}, u32[]{:S(2)}) collective-permute-start(f32[5,1,8,256]{3,2,1,0:T(8,128)S(1)} %constant_dynamic-update-slice_fusion.127), channel_id=1, source_target_pairs={{0,24},{8,0},{16,8},{24,16},{1,25},{9,1},{17,9},{25,17},{2,26},{10... | collective-permute-start | bytes 122888 | tf_op jit(solution)/shard_map/ppermute | solution.py:41
  81.4 6.8 %copy-start.14 = (f32[19,8,8,128]{3,2,1,0:T(8,128)}, f32[19,8,8,128]{3,2,1,0:T(8,128)S(1)}, u32[]{:S(2)}) copy-start(f32[19,8,8,128]{3,2,1,0:T(8,128)S(1)} %constant_dynamic-update-slice_fusion.40) | copy-start | bytes 1867780
  83.0 4.9 %collective-permute-start.14 = (f32[5,10,1,256]{3,2,1,0:T(1,128)S(1)}, f32[5,10,1,256]{3,2,1,0:T(1,128)S(1)}, u32[]{:S(2)}, u32[]{:S(2)}) collective-permute-start(f32[5,10,1,256]{3,2,1,0:T(1,128)S(1)} %constant_dynamic-update-slice_fusion.137), channel_id=1, source_target_pairs={{0,1},{1,2},{2,3},{3,4},{4,5},{5,6},{6,7},{7,0},{8,9},{9,10},{10,1... | collective-permute-start | bytes 153608 | tf_op jit(solution)/shard_map/ppermute | solution.py:41
  83.2 4.5 %collective-permute-start.15 = (f32[5,10,1,256]{3,2,1,0:T(1,128)S(1)}, f32[5,10,1,256]{3,2,1,0:T(1,128)S(1)}, u32[]{:S(2)}, u32[]{:S(2)}) collective-permute-start(f32[5,10,1,256]{3,2,1,0:T(1,128)S(1)} %constant_dynamic-update-slice_fusion.142), channel_id=1, source_target_pairs={{0,7},{1,0},{2,1},{3,2},{4,3},{5,4},{6,5},{7,6},{8,15},{9,8},{10,9... | collective-permute-start | bytes 153608 | tf_op jit(solution)/shard_map/ppermute | solution.py:41
  90.7 1.0 %copy-start.11 = (f32[19,8,8,256]{3,2,1,0:T(8,128)}, f32[19,8,8,256]{3,2,1,0:T(8,128)S(1)}, u32[]{:S(2)}) copy-start(f32[19,8,8,256]{3,2,1,0:T(8,128)S(1)} %constant_dynamic-update-slice_fusion.185) | copy-start | bytes 3735556
where the time goes:
time: 92.3 us; the launch traced here: 91.7 us
  other arithmetic  26.9 us (29%)
  starting transfers between devices  20.3 us (22%)
  blocking collectives  19.1 us (21%)
  local copies, waits for them, and re-layouts  11.1 us (12%)
  waiting for transfers between devices  11.1 us (12%)
  between operations  2.81 us (3%)
    ppermute x16, starting transfers between devices, from_behind(): lax.ppermute(shard, axis, [(i, (i + by) % size) for i in range(size)])  20.3 us
    all_gather x2, blocking collectives, local(): lax.all_gather(fine_out[None], 'span', axis=0, tiled=True)  19.1 us
    ppermute x16, waiting for transfers between devices, from_behind(): lax.ppermute(shard, axis, [(i, (i + by) % size) for i in range(size)])  11.1 us
    unnamed x84, other arithmetic  8.43 us
    unnamed x142, local copies, waits for them, and re-layouts  4.16 us
    sub x12, other arithmetic, collide(): result.append(pops[which_pop] - relax_rate * (pops[which_pop] - balance))  3.07 us
    eq x2, other arithmetic, pick_one(): matches = (shard_rows == target_tile)[:, None, None, None]  3.04 us
    add x4, other arithmetic, collide(): 1.0 + 3.0 * projected + 4.5 * projected * projected - 1.5 * square  2.4 us
  transfers between devices with their start and end apart: 16, of which 6 were waited for; matrix products, arithmetic and copies ran while one was open for 31% of the time, Pallas kernels for 0%

commit v1 on v0

v1 whole, which is shorter than its diff:
```python
import jax
import jax.numpy as jnp
from jax import lax
from jax.experimental import pallas as pl
from jax.experimental.pallas import tpu as pltpu
from jax.sharding import PartitionSpec as P

velocities = (
    (0, 0, 0),
    (1, 0, 0),
    (-1, 0, 0),
    (0, 1, 0),
    (0, -1, 0),
    (0, 0, 1),
    (0, 0, -1),
    (1, 1, 0),
    (-1, -1, 0),
    (1, -1, 0),
    (-1, 1, 0),
    (1, 0, 1),
    (-1, 0, -1),
    (1, 0, -1),
    (-1, 0, 1),
    (0, 1, 1),
    (0, -1, -1),
    (0, 1, -1),
    (0, -1, 1),
)
opposite = (0, 2, 1, 4, 3, 6, 5, 8, 7, 10, 9, 12, 11, 14, 13, 16, 15, 18, 17)
pairs = tuple((k, k + 1) for k in range(1, 19, 2))
incoming = (1, 7, 9, 11, 13)
backward_x = (2, 8, 10, 12, 14)
forward_z = (5, 11, 14, 15, 18)
backward_z = (6, 12, 13, 16, 17)
POPS = 19
KEPT = POPS + 5
VMEM_BYTES = 56 * 1024 * 1024


def collide(pops, wanted=range(POPS)):
    sums = [pops[a] + pops[b] for a, b in pairs]
    difs = [pops[a] - pops[b] for a, b in pairs]
    density = (
        pops[0] * (1.0 / 3.0)
        + (sums[0] + sums[1] + sums[2]) * (1.0 / 18.0)
        + ((sums[3] + sums[4]) + (sums[5] + sums[6]) + (sums[7] + sums[8])) * (1.0 / 36.0)
    )
    moment = [
        difs[0] * (1.0 / 18.0) + ((difs[3] + difs[4]) + (difs[5] + difs[6])) * (1.0 / 36.0),
        difs[1] * (1.0 / 18.0) + ((difs[3] - difs[4]) + (difs[7] + difs[8])) * (1.0 / 36.0),
        difs[2] * (1.0 / 18.0) + ((difs[5] - difs[6]) + (difs[7] - difs[8])) * (1.0 / 36.0),
    ]
    inverse = 1.0 / density
    speed = [component * inverse for component in moment]
    kinetic = moment[0] * speed[0] + moment[1] * speed[1] + moment[2] * speed[2]
    base = 1.25 * density - 1.875 * kinetic
    result = [None] * POPS
    if 0 in wanted:
        result[0] = base - 0.25 * pops[0]
    for a, b in pairs:
        if a not in wanted and b not in wanted:
            continue
        flux = None
        along = None
        for axis_num, step in enumerate(velocities[a]):
            if step == 0:
                continue
            if flux is None:
                flux, along = moment[axis_num], speed[axis_num]
            elif step == 1:
                flux, along = flux + moment[axis_num], along + speed[axis_num]
            else:
                flux, along = flux - moment[axis_num], along - speed[axis_num]
        even = base + 5.625 * (flux * along)
        odd = 3.75 * flux
        if a in wanted:
            result[a] = even + odd - 0.25 * pops[a]
        if b in wanted:
            result[b] = even - odd - 0.25 * pops[b]
    return result


def shift_layers(value, step_y):
    if step_y == 0:
        return value
    size = value.shape[-1]
    return pltpu.roll(value, step_y % size, value.ndim - 1)


def moved_row(base, left, right, masks, x_at):
    result = []
    sub = None
    for which_pop in range(POPS):
        step_x, step_y, step_z = velocities[which_pop]
        source = base(which_pop, x_at - step_x)
        if step_z != 0 and sub is None:
            sub = lax.broadcasted_iota(jnp.int32, source.shape, 0)
        width = source.shape[0]
        if step_z == 1:
            source = jnp.where(
                sub == 0, left(which_pop, x_at - step_x), pltpu.roll(source, 1, 0)
            )
        elif step_z == -1:
            source = jnp.where(
                sub == width - 1,
                right(which_pop, x_at - step_x),
                pltpu.roll(source, width - 1, 0),
            )
        source = shift_layers(source, step_y)
        result.append(
            jnp.where(masks[step_y] != 0, base(opposite[which_pop], x_at), source)
        )
    return result


def first_kernel(pre, main, star_pre, star_main, x_hi, x_lo, z_same, z_cross, x_small):
    rows = pre.shape[1]
    coarse = pre.shape[3]
    parity = lax.rem(lax.axis_index("span"), 2)
    domains = ((pre, star_pre, slice(0, coarse)), (main, star_main, slice(coarse, None)))
    for x_at in range(rows):
        for pops, star, lanes in domains:
            out = collide([pops[which_pop, x_at] for which_pop in range(POPS)])
            for which_pop in range(POPS):
                star[which_pop, x_at] = out[which_pop]
                if x_at == 0:
                    x_lo[which_pop, :, lanes] = out[which_pop]
                if x_at == rows - 1:
                    x_hi[which_pop, :, lanes] = out[which_pop]
            for k in range(5):
                if x_at == 1:
                    x_lo[POPS + k, :, lanes] = out[backward_x[k]]
                if x_at == rows - 2:
                    x_hi[POPS + k, :, lanes] = out[incoming[k]]
                if x_at == 0 and star is star_pre:
                    x_small[k] = out[backward_x[k]]

    def edges(hi, lo):
        for _, star, lanes in domains:
            width = star.shape[2]
            for which_pop in range(POPS):
                hi[which_pop, :, lanes] = star[which_pop, :, width - 1, :]
                lo[which_pop, :, lanes] = star[which_pop, :, 0, :]
            for k in range(5):
                hi[POPS + k, :, lanes] = star[forward_z[k], :, width - 2, :]
                lo[POPS + k, :, lanes] = star[backward_z[k], :, 1, :]

    @pl.when(parity == 0)
    def _():
        edges(z_same, z_cross)

    @pl.when(parity == 1)
    def _():
        edges(z_cross, z_same)


def corner_kernel(same, cross, c_hi, c_lo):
    last = same.shape[1] - 1
    for side, halo in enumerate((same, cross)):
        for k in range(KEPT):
            c_hi[side, k : k + 1, :] = halo[k, last : last + 1, :]
            c_lo[side, k : k + 1, :] = halo[k, 0:1, :]
        for k in range(5):
            at = KEPT + k
            c_hi[side, at : at + 1, :] = halo[incoming[k], last - 1 : last, :]
            c_lo[side, at : at + 1, :] = halo[backward_x[k], 1:2, :]
        for k in (1, 2):
            at = KEPT + 4 + k
            c_hi[side, at : at + 1, :] = halo[POPS + k, last - 1 : last, :]
            c_lo[side, at : at + 1, :] = halo[POPS + k, 1:2, :]


def build_columns(is_left, col, halo, edge, side, x_low, x_high, c_low, c_high):
    inward = backward_z if is_left else forward_z
    rim = 0 if is_left else x_low.shape[1] - 1
    for k in range(KEPT):
        col[k, 8:16, :] = halo[k]
        col[k, 7:8, :] = c_low[side, k : k + 1, :]
        col[k, 16:17, :] = c_high[side, k : k + 1, :]
    for k in range(5):
        col[incoming[k], 6:7, :] = c_low[side, KEPT + k : KEPT + k + 1, :]
        col[backward_x[k], 17:18, :] = c_high[side, KEPT + k : KEPT + k + 1, :]
    hi_k, lo_k = (1, 2) if is_left else (2, 1)
    col[POPS + hi_k, 6:7, :] = c_low[side, KEPT + 4 + hi_k : KEPT + 5 + hi_k, :]
    col[POPS + lo_k, 17:18, :] = c_high[side, KEPT + 4 + lo_k : KEPT + 5 + lo_k, :]
    for k in range(5):
        pop = inward[k]
        at = KEPT + k
        col[at, 8:16, :] = edge[pop]
        col[at, 7:8, :] = x_low[pop, rim : rim + 1, :]
        col[at, 16:17, :] = x_high[pop, rim : rim + 1, :]
        if pop in incoming:
            second = POPS + incoming.index(pop)
            col[at, 6:7, :] = x_low[second, rim : rim + 1, :]
        if pop in backward_x:
            second = POPS + backward_x.index(pop)
            col[at, 17:18, :] = x_high[second, rim : rim + 1, :]


def refine(coarse, phases, fine_len):
    coarse_len = coarse.shape[1]
    count = coarse.shape[0] // 3
    rows = lax.broadcasted_iota(jnp.int32, (coarse_len, fine_len), 0)
    fine = lax.broadcasted_iota(jnp.int32, (coarse_len, fine_len), 1)
    outs = []
    for phase in (0, 1):
        position = fine + phase
        lower = lax.shift_right_arithmetic(position - 1, 1)
        upper_wt = jnp.where(position % 2 == 0, 0.75, 0.25)
        low_idx = jnp.clip(lower, 0, coarse_len - 1)
        high_idx = jnp.clip(lower + 1, 0, coarse_len - 1)
        matrix = jnp.where(rows == low_idx, 1.0 - upper_wt, 0.0) + jnp.where(
            rows == high_idx, upper_wt, 0.0
        )
        outs.append(
            jnp.dot(
                coarse,
                matrix,
                precision=lax.Precision.HIGHEST,
                preferred_element_type=jnp.float32,
            )
        )
    return [
        jnp.where(
            phases[tile] > 0,
            outs[1][tile * count : (tile + 1) * count],
            outs[0][tile * count : (tile + 1) * count],
        )
        for tile in range(3)
    ]


def second_kernel(
    tile_map,
    layer_phase,
    walls,
    star_pre,
    star_main,
    x_low,
    x_high,
    same,
    cross,
    edge_same,
    edge_cross,
    c_low,
    c_high,
    tiles,
    out_pre,
    out_main,
    col_left,
    col_right,
    in_low,
    in_high,
    mask_pre,
    mask_main,
    inflow,
    next_pre,
    next_main,
    rim_left,
    rim_right,
):
    rows, width, coarse = star_pre.shape[1:]
    fine = star_main.shape[3]
    pre_lanes, main_lanes = slice(0, coarse), slice(coarse, coarse + fine)
    span_pos = lax.axis_index("span")
    stream_pos = lax.axis_index("stream")
    span_count = lax.axis_size("span")
    is_first = stream_pos == 0
    is_last = stream_pos == lax.axis_size("stream") - 1
    parity = lax.rem(span_pos, 2)

    def masks_of(solid, ref):
        layers = solid.shape[1]
        lane = lax.broadcasted_iota(jnp.int32, solid.shape, 1)
        ref[0] = solid
        ref[1] = jnp.where(lane == 0, 1.0, pltpu.roll(solid, 1, 1))
        ref[2] = jnp.where(lane == layers - 1, 1.0, pltpu.roll(solid, layers - 1, 1))

    solid = jnp.broadcast_to(jnp.where(walls[...] > 0, 1.0, 0.0), (8, fine))
    fine_at = lax.broadcasted_iota(jnp.int32, (fine, coarse), 0)
    coarse_at = lax.broadcasted_iota(jnp.int32, (fine, coarse), 1)
    halves = jnp.where(lax.shift_right_logical(fine_at, 1) == coarse_at, 1.0, 0.0)
    hits = jnp.dot(solid, halves, preferred_element_type=jnp.float32)
    masks_of(solid, mask_main)
    masks_of(jnp.where(hits > 0.5, 1.0, 0.0), mask_pre)
    masks = {step: (mask_pre[step % 3], mask_main[step % 3]) for step in (0, 1, -1)}

    def masks_for(domain, height=8):
        if height == 8:
            return {step: masks[step][domain] for step in masks}
        return {
            step: jnp.broadcast_to(masks[step][domain][:1], (height, masks[step][domain].shape[1]))
            for step in masks
        }

    @pl.when(parity == 0)
    def _():
        build_columns(True, col_left, cross, edge_cross, 1, x_low, x_high, c_low, c_high)
        build_columns(False, col_right, same, edge_same, 0, x_low, x_high, c_low, c_high)

    @pl.when(parity == 1)
    def _():
        build_columns(True, col_left, same, edge_same, 0, x_low, x_high, c_low, c_high)
        build_columns(False, col_right, cross, edge_cross, 1, x_low, x_high, c_low, c_high)

    for k in range(5):
        in_low[k] = x_low[incoming[k], :, main_lanes]
        in_high[k] = x_high[backward_x[k], :, main_lanes]

    @pl.when(is_last)
    def _():
        for k in range(5):
            in_high[k] = star_main[backward_x[k], rows - 1]
        for col in (col_left, col_right):
            for k in range(KEPT + 5):
                col[k, 16:17, main_lanes] = col[k, 15:16, main_lanes]

    @pl.when(is_first)
    def _():
        chosen, phases = [], []
        for offset in (span_count - 1, 0, 1):
            at = lax.rem(span_pos + offset, span_count)
            chosen.append(tile_map[at])
            phases.append(layer_phase[at])

        planes = [[tiles[tile, pop] for pop in incoming] for tile in chosen]
        planes_next = []
        for tile in chosen:
            before = lax.rem(tile + span_count - 1, span_count)
            after = lax.rem(tile + 1, span_count)

            def slot(pop, x_at):
                if x_at == 0:
                    return pop
                if x_at == -1:
                    return POPS + incoming.index(pop)
                return KEPT + backward_x.index(pop)

            new = moved_row(
                lambda pop, x_at: tiles[tile, slot(pop, x_at)],
                lambda pop, x_at: tiles[before, slot(pop, x_at), width - 1 : width, :],
                lambda pop, x_at: tiles[after, slot(pop, x_at), 0:1, :],
                masks_for(0),
                0,
            )
            out = collide(new, incoming)
            planes_next.append([out[pop] for pop in incoming])
        for step_num, found in enumerate((planes, planes_next)):
            stacked = jnp.concatenate([plane for group in found for plane in group], axis=0)
            for tile, value in enumerate(refine(stacked, phases, fine)):
                inflow[step_num, tile] = value.reshape(5, width, fine)
        before, own, after = (inflow.at[0, tile] for tile in range(3))
        for k in range(5):
            in_low[k] = own[k]
            col_left[incoming[k], 7:8, main_lanes] = before[k, width - 1 : width]
            col_right[incoming[k], 7:8, main_lanes] = after[k, 0:1]
        col_left[POPS + 1, 7:8, main_lanes] = before[3, width - 2 : width - 1]
        col_left[KEPT + 2, 7:8, main_lanes] = own[4, 0:1]
        col_right[POPS + 2, 7:8, main_lanes] = after[4, 1:2]
        col_right[KEPT + 1, 7:8, main_lanes] = own[3, width - 1 : width]

    for is_left, col, rim in ((True, col_left, rim_left), (False, col_right, rim_right)):
        moving = forward_z if is_left else backward_z
        for domain, lanes in enumerate((pre_lanes, main_lanes)):
            tall = masks_for(domain, 16)
            new = []
            for pop in range(POPS):
                step_x, step_y, step_z = velocities[pop]
                if step_z == 0:
                    at = pop
                elif pop in moving:
                    at = POPS + moving.index(pop)
                else:
                    at = KEPT + (backward_z if is_left else forward_z).index(pop)
                source = shift_layers(col[at, 7 - step_x : 23 - step_x, lanes], step_y)
                new.append(
                    jnp.where(tall[step_y] != 0, col[opposite[pop], 7:23, lanes], source)
                )
            out = collide(new, moving)
            for k in range(5):
                rim[k, :, lanes] = out[moving[k]]

    stars = (star_pre, star_main)
    nexts = (next_pre, next_main)

    def base_of(domain, lanes):
        def base(pop, x_at):
            if 0 <= x_at < rows:
                return stars[domain][pop, x_at]
            if x_at == -1:
                if domain == 1 and pop in incoming:
                    return in_low[incoming.index(pop)]
                return x_low[pop, :, lanes]
            if x_at == rows:
                if domain == 1 and pop in backward_x:
                    return in_high[backward_x.index(pop)]
                return x_high[pop, :, lanes]
            if x_at < 0:
                return x_low[POPS + incoming.index(pop), :, lanes]
            return x_high[POPS + backward_x.index(pop), :, lanes]

        return base

    for x_at in range(-1, rows + 1):
        for domain, lanes in enumerate((pre_lanes, main_lanes)):
            new = moved_row(
                base_of(domain, lanes),
                lambda pop, at: col_left[pop, 8 + at : 9 + at, lanes],
                lambda pop, at: col_right[pop, 8 + at : 9 + at, lanes],
                masks_for(domain),
                x_at,
            )
            wanted = range(POPS)
            if x_at == -1:
                wanted = incoming
            elif x_at == rows:
                wanted = backward_x
            out = collide(new, wanted)
            for pop in wanted:
                nexts[domain][pop, x_at + 1] = out[pop]

    @pl.when(is_first)
    def _():
        for k in range(5):
            next_main[incoming[k], 0] = inflow[1, 1, k]
        rim_left[1, 0:1, main_lanes] = inflow[1, 0, 3, width - 1 : width]
        rim_right[2, 0:1, main_lanes] = inflow[1, 2, 4, 0:1]

    @pl.when(is_last)
    def _():
        for k in range(5):
            next_main[backward_x[k], rows + 1] = next_main[backward_x[k], rows]
            for rim in (rim_left, rim_right):
                rim[k, rows + 1 : rows + 2, main_lanes] = rim[k, rows : rows + 1, main_lanes]

    for x_at in range(rows):
        for domain, lanes in enumerate((pre_lanes, main_lanes)):
            new = moved_row(
                lambda pop, at: nexts[domain][pop, at + 1],
                lambda pop, at: rim_left[forward_z.index(pop), at + 1 : at + 2, lanes],
                lambda pop, at: rim_right[backward_z.index(pop), at + 1 : at + 2, lanes],
                masks_for(domain),
                x_at,
            )
            for pop in range(POPS):
                (out_pre, out_main)[domain][pop, x_at] = new[pop]


def f32(*shape):
    return jax.ShapeDtypeStruct(shape, jnp.float32)


def local(pre_pops, main_pops, tile_map, layer_phase, wall_flags):
    span_count = lax.axis_size("span")
    stream_count = lax.axis_size("stream")
    _, rows, width, coarse = pre_pops.shape
    fine = main_pops.shape[3]
    lanes = coarse + fine

    def send(value, step_x, place, only=None):
        moves = []
        for s in range(stream_count):
            if only is not None and s != only:
                continue
            for j in range(span_count):
                target = (s + step_x) % stream_count * span_count + place(j) % span_count
                moves.append((s * span_count + j, target))
        return lax.ppermute(value, ("stream", "span"), moves)

    stay = lambda j: j
    sibling = lambda j: j + 1 if j % 2 == 0 else j - 1
    beyond = lambda j: j - 1 if j % 2 == 0 else j + 1
    params = pltpu.CompilerParams(vmem_limit_bytes=VMEM_BYTES)

    star_pre, star_main, x_hi, x_lo, z_same, z_cross, x_small = pl.pallas_call(
        first_kernel,
        out_shape=(
            f32(*pre_pops.shape),
            f32(*main_pops.shape),
            f32(KEPT, width, lanes),
            f32(KEPT, width, lanes),
            f32(KEPT, rows, lanes),
            f32(KEPT, rows, lanes),
            f32(5, width, coarse),
        ),
        compiler_params=params,
        name="collide_and_pack",
    )(pre_pops, main_pops)

    beside = send(x_small, -1, stay, only=1 % stream_count)
    same = send(z_same, 0, sibling)
    cross = send(z_cross, 0, beyond)
    x_low = send(x_hi, 1, stay)
    x_high = send(x_lo, -1, stay)
    c_hi, c_lo = pl.pallas_call(
        corner_kernel,
        out_shape=(f32(2, 32, lanes), f32(2, 32, lanes)),
        compiler_params=params,
        name="corners",
    )(same, cross)
    c_low = send(c_hi, 1, stay)
    c_high = send(c_lo, -1, stay)
    plane = jnp.concatenate([x_hi[:, :, :coarse], beside], axis=0)
    tiles = lax.all_gather(plane, "span", axis=0, tiled=False)

    whole = pl.BlockSpec(memory_space=pltpu.VMEM)
    scalars = pl.BlockSpec(memory_space=pltpu.SMEM)
    return pl.pallas_call(
        second_kernel,
        out_shape=(f32(*pre_pops.shape), f32(*main_pops.shape)),
        in_specs=[scalars, scalars] + [whole] * 12,
        scratch_shapes=[
            pltpu.VMEM((KEPT + 5, 24, lanes), jnp.float32),
            pltpu.VMEM((KEPT + 5, 24, lanes), jnp.float32),
            pltpu.VMEM((5, width, fine), jnp.float32),
            pltpu.VMEM((5, width, fine), jnp.float32),
            pltpu.VMEM((3, 8, coarse), jnp.float32),
            pltpu.VMEM((3, 8, fine), jnp.float32),
            pltpu.VMEM((2, 3, 5, width, fine), jnp.float32),
            pltpu.VMEM((POPS, rows + 2, width, coarse), jnp.float32),
            pltpu.VMEM((POPS, rows + 2, width, fine), jnp.float32),
            pltpu.VMEM((5, 16, lanes), jnp.float32),
            pltpu.VMEM((5, 16, lanes), jnp.float32),
        ],
        compiler_params=params,
        name="two_steps",
    )(
        tile_map,
        layer_phase,
        wall_flags.reshape(1, fine),
        star_pre,
        star_main,
        x_low,
        x_high,
        same,
        cross,
        z_same,
        z_cross,
        c_low,
        c_high,
        tiles,
    )


def solution(mesh):
    return jax.shard_map(
        local,
        mesh=mesh,
        in_specs=(P(None, "stream", "span", None), P(None, "stream", "span", None), P(), P(), P()),
        out_specs=(P(None, "stream", "span", None), P(None, "stream", "span", None)),
        check_vma=False,
    )
```

time: 92.3 us -> 41.3 us (0.45)
  other arithmetic: 26.9 us -> 0.01 us
  Pallas kernels: 0 us -> 11.9 us
  waiting for transfers between devices: 11.1 us -> 1.7 us
  local copies, waits for them, and re-layouts: 11.1 us -> 2.5 us
  starting transfers between devices: 20.3 us -> 12.1 us
  blocking collectives: 19.1 us -> 12.2 us
  between operations: 2.81 us -> 0.7 us
    pallas_call x0 -> x3, Pallas kernels: none -> 11.9 us  [the longest x1 6.09 us: local(): pl.pallas_call(second_kernel, out_shape=(f32(*pre_pops.shape), f32(*main_...]
    ppermute x16 -> x7, waiting for transfers between devices: 11.1 us -> 1.7 us  [send(): return lax.ppermute(value, ('stream', 'span'), moves)]
    unnamed x84 -> x0, other arithmetic: 8.43 us -> none
    ppermute x16 -> x7, starting transfers between devices: 20.3 us -> 12.1 us  [send(): return lax.ppermute(value, ('stream', 'span'), moves)]
    all_gather x2 -> x1, blocking collectives: 19.1 us -> 12.2 us  [local(): tiles = lax.all_gather(plane, 'span', axis=0, tiled=False)]
    another operation x40 -> x0, other arithmetic: 4 us -> none  [the longest x26 1.95 us: extend_columns(): return jnp.stack(pieces)]
    squeeze x48 -> x0, local copies, waits for them, and re-layouts: 3.22 us -> none  [the longest x4 1.48 us: extend_rows(): lower_rows[incoming.index(which_pop)]]
    sub x12 -> x0, other arithmetic: 3.07 us -> none  [collide(): result.append(pops[which_pop] - relax_rate * (pops[which_pop] - balance))]
  transfers between devices with their start and end apart: 16 -> 7, of which waited for: 6 -> 2; matrix products, arithmetic and copies ran while one was open for 31% -> 2% of each run, Pallas kernels for 0% -> 4%
where the time goes in v1:
time: 41.3 us; the launch traced here: 41.1 us
  blocking collectives  12.2 us (30%)
  starting transfers between devices  12.1 us (29%)
  Pallas kernels  11.9 us (29%)
  local copies, waits for them, and re-layouts  2.5 us (6%)
  waiting for transfers between devices  1.7 us (4%)
  between operations  0.7 us (2%)
    all_gather x1, blocking collectives, local(): tiles = lax.all_gather(plane, 'span', axis=0, tiled=False)  12.2 us
    ppermute x7, starting transfers between devices, send(): return lax.ppermute(value, ('stream', 'span'), moves)  12.1 us
    pallas_call x1, Pallas kernels, local(): pl.pallas_call(second_kernel, out_shape=(f32(*pre_pops.shape), f32(*main_...  6.09 us
    pallas_call x1, Pallas kernels, local(): pl.pallas_call(first_kernel, out_shape=(f32(*pre_pops.shape), f32(*main_p...  3.97 us
    pallas_call x1, Pallas kernels, local(): pl.pallas_call(corner_kernel, out_shape=(f32(2, 32, lanes), f32(2, 32, la...  1.79 us
    ppermute x7, waiting for transfers between devices, send(): return lax.ppermute(value, ('stream', 'span'), moves)  1.7 us
    unnamed x12, local copies, waits for them, and re-layouts  1.57 us
    slice x1, local copies, waits for them, and re-layouts, local(): plane = jnp.concatenate([x_hi[:, :, :coarse], beside], axis=0)  0.93 us
  transfers between devices with their start and end apart: 7, of which 2 were waited for; matrix products, arithmetic and copies ran while one was open for 2% of the time, Pallas kernels for 4%

profile of v1, /device:TPU:0, one launch (start us, length us, event | category | flops | bytes accessed | tf_op | source)
XLA Modules:
  0.0 41.1 jit_solution(4122500163366889917)
XLA Ops:
  0.6 4.0 %collide_and_pack.1 = (f32[19,8,8,128]{3,2,1,0:T(8,128)}, f32[19,8,8,256]{3,2,1,0:T(8,128)}, f32[24,8,384]{2,1,0:T(8,128)}, f32[24,8,384]{2,1,0:T(8,128)}, f32[2...) custom-call(f32[19,8,8,128]{3,2,1,0:T(8,128)} %pre.1, f32[19,8,8,256]{3,2,1,0:T(8,128)} %main.1), custom_call_target="tpu_custom_call" | custom-call | tf_op jit(solution)/shard_map/collide_and_pack/pallas_call | solution.py:475
  4.6 0.5 %collective-permute-start.2 = (f32[24,8,384]{2,1,0:T(8,128)}, f32[24,8,384]{2,1,0:T(8,128)S(1)}, u32[]{:S(2)}, u32[]{:S(2)}) collective-permute-start(f32[24,8,384]{2,1,0:T(8,128)} %get-tuple-element.15.edge_same), channel_id=1, source_target_pairs={{0,1},{1,0},{2,3},{3,2},{4,5},{5,4},{6,7},{7,6},{8,9},{9,8},{10,11... | collective-permute-start | bytes 884744 | tf_op jit(solution)/shard_map/ppermute | solution.py:468
  5.1 3.5 %collective-permute-start.3 = (f32[24,8,384]{2,1,0:T(8,128)}, f32[24,8,384]{2,1,0:T(8,128)S(1)}, u32[]{:S(2)}, u32[]{:S(2)}) collective-permute-start(f32[24,8,384]{2,1,0:T(8,128)} %get-tuple-element.16.edge_cross), channel_id=1, source_target_pairs={{0,7},{1,2},{2,1},{3,4},{4,3},{5,6},{6,5},{7,0},{8,15},{9,10},{10,... | collective-permute-start | bytes 884744 | tf_op jit(solution)/shard_map/ppermute | solution.py:468
  8.6 1.3 %collective-permute-start.6 = (f32[5,8,128]{2,1,0:T(8,128)}, f32[5,8,128]{2,1,0:T(8,128)S(1)}, u32[]{:S(2)}, u32[]{:S(2)}) collective-permute-start(f32[5,8,128]{2,1,0:T(8,128)} %get-tuple-element.19), channel_id=1, source_target_pairs={{8,0},{9,1},{10,2},{11,3},{12,4},{13,5},{14,6},{15,7}} | collective-permute-start | bytes 61448 | tf_op jit(solution)/shard_map/ppermute | solution.py:468
  9.9 3.0 %collective-permute-start.1 = (f32[24,8,384]{2,1,0:T(8,128)}, f32[24,8,384]{2,1,0:T(8,128)S(1)}, u32[]{:S(2)}, u32[]{:S(2)}) collective-permute-start(f32[24,8,384]{2,1,0:T(8,128)} %get-tuple-element.14), channel_id=1, source_target_pairs={{0,24},{1,25},{2,26},{3,27},{4,28},{5,29},{6,30},{7,31},{8,0},{9,1... | collective-permute-start | bytes 884744 | tf_op jit(solution)/shard_map/ppermute | solution.py:468
  12.9 0.0 collective-permute-start
  12.9 0.9 %slice.3 = f32[24,8,128]{2,1,0:T(8,128)S(1)} slice(f32[24,8,384]{2,1,0:T(8,128)} %get-tuple-element.13), slice={[0:24], [0:8], [0:128]} | slice | bytes 196608 | tf_op jit(solution)/shard_map/slice | solution.py:503
  13.9 0.9 %collective-permute-done.6 = f32[5,8,128]{2,1,0:T(8,128)S(1)} collective-permute-done((f32[5,8,128]{2,1,0:T(8,128)}, f32[5,8,128]{2,1,0:T(8,128)S(1)}, u32[]{:S(2)}, u32[]{:S(2)}) %collective-permute-start.6) | collective-permute-done | bytes 20512 | tf_op jit(solution)/shard_map/ppermute | solution.py:468
  14.8 0.0 collective-permute-done.2.same
  14.8 0.0 copy-start
  14.8 0.8 %collective-permute-done.3.cross = f32[24,8,384]{2,1,0:T(8,128)S(1)} collective-permute-done((f32[24,8,384]{2,1,0:T(8,128)}, f32[24,8,384]{2,1,0:T(8,128)S(1)}, u32[]{:S(2)}, u32[]{:S(2)}) %collective-permute-start.3) | collective-permute-done | bytes 294944 | tf_op jit(solution)/shard_map/ppermute | solution.py:468
  15.6 0.0 copy-done
  15.6 0.0 copy-start.1
  15.6 0.7 %copy-done.1 = f32[24,8,384]{2,1,0:T(8,128)} copy-done((f32[24,8,384]{2,1,0:T(8,128)}, f32[24,8,384]{2,1,0:T(8,128)S(1)}, u32[]{:S(2)}) %copy-start.1) | copy-done | bytes 294936
  16.3 1.8 %corners.1 = (f32[2,32,384]{2,1,0:T(8,128)}, f32[2,32,384]{2,1,0:T(8,128)}) custom-call(f32[24,8,384]{2,1,0:T(8,128)} %copy-done, f32[24,8,384]{2,1,0:T(8,128)} %copy-done.1), custom_call_target="tpu_custom_call" | custom-call | tf_op jit(solution)/shard_map/corners/pallas_call | solution.py:495
  18.1 1.8 %collective-permute-start.4 = (f32[2,32,384]{2,1,0:T(8,128)}, f32[2,32,384]{2,1,0:T(8,128)S(1)}, u32[]{:S(2)}, u32[]{:S(2)}) collective-permute-start(f32[2,32,384]{2,1,0:T(8,128)} %get-tuple-element.17), channel_id=1, source_target_pairs={{0,8},{1,9},{2,10},{3,11},{4,12},{5,13},{6,14},{7,15},{8,16},{9,17... | collective-permute-start | bytes 294920 | tf_op jit(solution)/shard_map/ppermute | solution.py:468
  19.9 2.1 %collective-permute-start.5 = (f32[2,32,384]{2,1,0:T(8,128)}, f32[2,32,384]{2,1,0:T(8,128)S(1)}, u32[]{:S(2)}, u32[]{:S(2)}) collective-permute-start(f32[2,32,384]{2,1,0:T(8,128)} %get-tuple-element.18), channel_id=1, source_target_pairs={{0,24},{1,25},{2,26},{3,27},{4,28},{5,29},{6,30},{7,31},{8,0},{9,1... | collective-permute-start | bytes 294920 | tf_op jit(solution)/shard_map/ppermute | solution.py:468
  21.9 12.2 %all-gather = f32[232,8,128]{2,1,0:T(8,128)} all-gather(f32[29,8,128]{2,1,0:T(8,128)S(1)} %pad_maximum_fusion), channel_id=2, replica_groups=mesh['stream'=4,'span'=8] {'span'}, dimensions={0}, use_global_device_ids=true | all-gather | bytes 1069056 | tf_op jit(solution)/shard_map/all_gather | solution.py:504
  34.1 0.0 collective-permute-done.1.x_high
  34.1 0.0 copy-start.2
  34.1 0.0 collective-permute-done.x_low
  34.1 0.0 copy-start.3
  34.1 0.0 collective-permute-done.4.c_low
  34.1 0.0 copy-start.4
  34.1 0.0 collective-permute-done.5.c_high
  34.1 0.0 copy-start.5
  34.2 0.7 %copy-done.2 = f32[24,8,384]{2,1,0:T(8,128)} copy-done((f32[24,8,384]{2,1,0:T(8,128)}, f32[24,8,384]{2,1,0:T(8,128)S(1)}, u32[]{:S(2)}) %copy-start.2) | copy-done | bytes 294936
  34.8 0.1 copy-done.3
  34.9 0.0 copy-done.4
  35.0 0.0 copy-done.5
  35.0 6.1 %two_steps.1 = (f32[19,8,8,128]{3,2,1,0:T(8,128)}, f32[19,8,8,256]{3,2,1,0:T(8,128)}) custom-call(s32[8]{0:T(128)} %tile_map.1, s32[8]{0:T(128)} %layer_phase.1, s32[1,256]{1,0:T(1,128)} %bitcast.3, f32[19,8,8,128]{3,2,1,0:T(8,128)} %get-tuple-element.11.star_pre, f32[19,8,8,256]{3,2,1,0:T(8,128)} %get-tuple-element.12.star_main, f32[24,8,384]{2,1,0:T(8,128)} %copy-done.3, ...), custom_call_target="tpu_custom_call" | custom-call | tf_op jit(solution)/shard_map/two_steps/pallas_call | solution.py:508
  (1 shorter events, 0.0 us)
Async XLA Ops:
  4.6 10.2 %collective-permute-start.2 = (f32[24,8,384]{2,1,0:T(8,128)}, f32[24,8,384]{2,1,0:T(8,128)S(1)}, u32[]{:S(2)}, u32[]{:S(2)}) collective-permute-start(f32[24,8,384]{2,1,0:T(8,128)} %get-tuple-element.15.edge_same), channel_id=1, source_target_pairs={{0,1},{1,0},{2,3},{3,2},{4,5},{5,4},{6,7},{7,6},{8,9},{9,8},{10,11... | collective-permute-start | bytes 884744 | tf_op jit(solution)/shard_map/ppermute | solution.py:468
  5.1 10.5 %collective-permute-start.3 = (f32[24,8,384]{2,1,0:T(8,128)}, f32[24,8,384]{2,1,0:T(8,128)S(1)}, u32[]{:S(2)}, u32[]{:S(2)}) collective-permute-start(f32[24,8,384]{2,1,0:T(8,128)} %get-tuple-element.16.edge_cross), channel_id=1, source_target_pairs={{0,7},{1,2},{2,1},{3,4},{4,3},{5,6},{6,5},{7,0},{8,15},{9,10},{10,... | collective-permute-start | bytes 884744 | tf_op jit(solution)/shard_map/ppermute | solution.py:468
  8.6 6.2 %collective-permute-start.6 = (f32[5,8,128]{2,1,0:T(8,128)}, f32[5,8,128]{2,1,0:T(8,128)S(1)}, u32[]{:S(2)}, u32[]{:S(2)}) collective-permute-start(f32[5,8,128]{2,1,0:T(8,128)} %get-tuple-element.19), channel_id=1, source_target_pairs={{8,0},{9,1},{10,2},{11,3},{12,4},{13,5},{14,6},{15,7}} | collective-permute-start | bytes 61448 | tf_op jit(solution)/shard_map/ppermute | solution.py:468
  9.9 24.2 %collective-permute-start.1 = (f32[24,8,384]{2,1,0:T(8,128)}, f32[24,8,384]{2,1,0:T(8,128)S(1)}, u32[]{:S(2)}, u32[]{:S(2)}) collective-permute-start(f32[24,8,384]{2,1,0:T(8,128)} %get-tuple-element.14), channel_id=1, source_target_pairs={{0,24},{1,25},{2,26},{3,27},{4,28},{5,29},{6,30},{7,31},{8,0},{9,1... | collective-permute-start | bytes 884744 | tf_op jit(solution)/shard_map/ppermute | solution.py:468
  12.9 21.2 %collective-permute-start = (f32[24,8,384]{2,1,0:T(8,128)}, f32[24,8,384]{2,1,0:T(8,128)S(1)}, u32[]{:S(2)}, u32[]{:S(2)}) collective-permute-start(f32[24,8,384]{2,1,0:T(8,128)} %get-tuple-element.13), channel_id=1, source_target_pairs={{0,8},{1,9},{2,10},{3,11},{4,12},{5,13},{6,14},{7,15},{8,16},{9,17... | collective-permute-start | bytes 884744 | tf_op jit(solution)/shard_map/ppermute | solution.py:468
  14.8 0.8 %copy-start = (f32[24,8,384]{2,1,0:T(8,128)}, f32[24,8,384]{2,1,0:T(8,128)S(1)}, u32[]{:S(2)}) copy-start(f32[24,8,384]{2,1,0:T(8,128)S(1)} %collective-permute-done.2.same) | copy-start | bytes 884740
  15.6 0.7 %copy-start.1 = (f32[24,8,384]{2,1,0:T(8,128)}, f32[24,8,384]{2,1,0:T(8,128)S(1)}, u32[]{:S(2)}) copy-start(f32[24,8,384]{2,1,0:T(8,128)S(1)} %collective-permute-done.3.cross) | copy-start | bytes 884740
  18.1 16.0 %collective-permute-start.4 = (f32[2,32,384]{2,1,0:T(8,128)}, f32[2,32,384]{2,1,0:T(8,128)S(1)}, u32[]{:S(2)}, u32[]{:S(2)}) collective-permute-start(f32[2,32,384]{2,1,0:T(8,128)} %get-tuple-element.17), channel_id=1, source_target_pairs={{0,8},{1,9},{2,10},{3,11},{4,12},{5,13},{6,14},{7,15},{8,16},{9,17... | collective-permute-start | bytes 294920 | tf_op jit(solution)/shard_map/ppermute | solution.py:468
  19.9 14.3 %collective-permute-start.5 = (f32[2,32,384]{2,1,0:T(8,128)}, f32[2,32,384]{2,1,0:T(8,128)S(1)}, u32[]{:S(2)}, u32[]{:S(2)}) collective-permute-start(f32[2,32,384]{2,1,0:T(8,128)} %get-tuple-element.18), channel_id=1, source_target_pairs={{0,24},{1,25},{2,26},{3,27},{4,28},{5,29},{6,30},{7,31},{8,0},{9,1... | collective-permute-start | bytes 294920 | tf_op jit(solution)/shard_map/ppermute | solution.py:468
  34.1 0.7 %copy-start.2 = (f32[24,8,384]{2,1,0:T(8,128)}, f32[24,8,384]{2,1,0:T(8,128)S(1)}, u32[]{:S(2)}) copy-start(f32[24,8,384]{2,1,0:T(8,128)S(1)} %collective-permute-done.1.x_high) | copy-start | bytes 884740
  34.1 0.8 %copy-start.3 = (f32[24,8,384]{2,1,0:T(8,128)}, f32[24,8,384]{2,1,0:T(8,128)S(1)}, u32[]{:S(2)}) copy-start(f32[24,8,384]{2,1,0:T(8,128)S(1)} %collective-permute-done.x_low) | copy-start | bytes 884740
  34.1 0.8 %copy-start.4 = (f32[2,32,384]{2,1,0:T(8,128)}, f32[2,32,384]{2,1,0:T(8,128)S(1)}, u32[]{:S(2)}) copy-start(f32[2,32,384]{2,1,0:T(8,128)S(1)} %collective-permute-done.4.c_low) | copy-start | bytes 294916
  34.1 0.9 %copy-start.5 = (f32[2,32,384]{2,1,0:T(8,128)}, f32[2,32,384]{2,1,0:T(8,128)S(1)}, u32[]{:S(2)}) copy-start(f32[2,32,384]{2,1,0:T(8,128)S(1)} %collective-permute-done.5.c_high) | copy-start | bytes 294916

commit v2 on v1

--- a/solution.py
+++ b/solution.py
@@ -34,7 +34,8 @@
 backward_z = (6, 12, 13, 16, 17)
 POPS = 19
 KEPT = POPS + 5
-VMEM_BYTES = 56 * 1024 * 1024
+VMEM_SMALL = 10 * 1024 * 1024
+VMEM_LARGE = 20 * 1024 * 1024
 
 
 def collide(pops, wanted=range(POPS)):
@@ -470,7 +471,7 @@
     stay = lambda j: j
     sibling = lambda j: j + 1 if j % 2 == 0 else j - 1
     beyond = lambda j: j - 1 if j % 2 == 0 else j + 1
-    params = pltpu.CompilerParams(vmem_limit_bytes=VMEM_BYTES)
+    params = pltpu.CompilerParams(vmem_limit_bytes=VMEM_SMALL)
 
     star_pre, star_main, x_hi, x_lo, z_same, z_cross, x_small = pl.pallas_call(
         first_kernel,
@@ -522,7 +523,7 @@
             pltpu.VMEM((5, 16, lanes), jnp.float32),
             pltpu.VMEM((5, 16, lanes), jnp.float32),
         ],
-        compiler_params=params,
+        compiler_params=pltpu.CompilerParams(vmem_limit_bytes=VMEM_LARGE),
         name="two_steps",
     )(
         tile_map,

time: 41.3 us -> 34.5 us (0.84)
  Pallas kernels: 11.9 us -> 5.18 us
  blocking collectives: 12.2 us -> 11.1 us
  waiting for transfers between devices: 1.7 us -> 2.43 us
    pallas_call x1, Pallas kernels: 3.97 us -> 0.83 us  [local(): pl.pallas_call(first_kernel, out_shape=(f32(*pre_pops.shape), f32(*main_p...]
    pallas_call x1, Pallas kernels: 6.09 us -> 4.28 us  [local(): pl.pallas_call(second_kernel, out_shape=(f32(*pre_pops.shape), f32(*main_...]
    pallas_call x1, Pallas kernels: 1.79 us -> 0.07 us  [local(): pl.pallas_call(corner_kernel, out_shape=(f32(2, 32, lanes), f32(2, 32, la...]
    all_gather x1, blocking collectives: 12.2 us -> 11.1 us  [local(): tiles = lax.all_gather(plane, 'span', axis=0, tiled=False)]
    slice x1, local copies, waits for them, and re-layouts: 0.93 us -> 0.01 us  [local(): plane = jnp.concatenate([x_hi[:, :, :coarse], beside], axis=0)]
    unnamed x12 -> x10, local copies, waits for them, and re-layouts: 1.57 us -> 2.38 us
    ppermute x7, waiting for transfers between devices: 1.7 us -> 2.43 us  [send(): return lax.ppermute(value, ('stream', 'span'), moves)]
  transfers between devices with their start and end apart: 7 -> 7, of which waited for: 2 -> 2; matrix products, arithmetic and copies ran while one was open for 2% -> 0% of each run, Pallas kernels for 4% -> 0%
where the time goes in v2:
time: 34.5 us; the launch traced here: 34.3 us
  starting transfers between devices  12.4 us (36%)
  blocking collectives  11.1 us (32%)
  Pallas kernels  5.18 us (15%)
  waiting for transfers between devices  2.43 us (7%)
  local copies, waits for them, and re-layouts  2.39 us (7%)
  between operations  0.74 us (2%)
    ppermute x7, starting transfers between devices, send(): return lax.ppermute(value, ('stream', 'span'), moves)  12.4 us
    all_gather x1, blocking collectives, local(): tiles = lax.all_gather(plane, 'span', axis=0, tiled=False)  11.1 us
    pallas_call x1, Pallas kernels, local(): pl.pallas_call(second_kernel, out_shape=(f32(*pre_pops.shape), f32(*main_...  4.28 us
    ppermute x7, waiting for transfers between devices, send(): return lax.ppermute(value, ('stream', 'span'), moves)  2.43 us
    unnamed x10, local copies, waits for them, and re-layouts  2.38 us
    pallas_call x1, Pallas kernels, local(): pl.pallas_call(first_kernel, out_shape=(f32(*pre_pops.shape), f32(*main_p...  0.83 us
  transfers between devices with their start and end apart: 7, of which 2 were waited for; matrix products, arithmetic and copies ran while one was open for 0% of the time, Pallas kernels for 0%

profile of v2, /device:TPU:0, one launch (start us, length us, event | category | flops | bytes accessed | tf_op | source)
XLA Modules:
  0.0 34.3 jit_solution(8213178663509048482)
XLA Ops:
  0.6 0.0 copy-start
  0.6 1.3 %copy-done = f32[19,8,8,256]{3,2,1,0:T(8,128)S(1)} copy-done((f32[19,8,8,256]{3,2,1,0:T(8,128)S(1)}, f32[19,8,8,256]{3,2,1,0:T(8,128)}, u32[]{:S(2)}) %copy-start) | copy-done | bytes 1245208
  1.9 0.0 copy-start.1
  1.9 1.1 %copy-done.1 = f32[19,8,8,128]{3,2,1,0:T(8,128)S(1)} copy-done((f32[19,8,8,128]{3,2,1,0:T(8,128)S(1)}, f32[19,8,8,128]{3,2,1,0:T(8,128)}, u32[]{:S(2)}) %copy-start.1) | copy-done | bytes 622616
  3.0 0.8 %collide_and_pack.1 = (f32[19,8,8,128]{3,2,1,0:T(8,128)S(1)}, f32[19,8,8,256]{3,2,1,0:T(8,128)S(1)}, f32[24,8,384]{2,1,0:T(8,128)S(1)}, f32[24,8,384]{2,1,0:T(8,...) custom-call(f32[19,8,8,128]{3,2,1,0:T(8,128)S(1)} %copy-done.1, ...), custom_call_target="tpu_custom_call" | custom-call | tf_op jit(solution)/shard_map/collide_and_pack/pallas_call | solution.py:476
  3.8 0.0 copy-start.2
  3.8 0.0 copy-start.3
  3.9 0.0 copy-start.4
  3.9 0.5 %collective-permute-start.2 = (f32[24,8,384]{2,1,0:T(8,128)S(1)}, f32[24,8,384]{2,1,0:T(8,128)S(1)}, u32[]{:S(2)}, u32[]{:S(2)}) collective-permute-start(f32[24,8,384]{2,1,0:T(8,128)S(1)} %get-tuple-element.15.edge_same), channel_id=1, source_target_pairs={{0,1},{1,0},{2,3},{3,2},{4,5},{5,4},{6,7},{7,6},{8,9},{9,8},{10,11... | collective-permute-start | bytes 884744 | tf_op jit(solution)/shard_map/ppermute | solution.py:469
  4.4 3.6 %collective-permute-start.3 = (f32[24,8,384]{2,1,0:T(8,128)S(1)}, f32[24,8,384]{2,1,0:T(8,128)S(1)}, u32[]{:S(2)}, u32[]{:S(2)}) collective-permute-start(f32[24,8,384]{2,1,0:T(8,128)S(1)} %get-tuple-element.16.edge_cross), channel_id=1, source_target_pairs={{0,7},{1,2},{2,1},{3,4},{4,3},{5,6},{6,5},{7,0},{8,15},{9,10},{10,... | collective-permute-start | bytes 884744 | tf_op jit(solution)/shard_map/ppermute | solution.py:469
  7.9 1.3 %collective-permute-start.6 = (f32[5,8,128]{2,1,0:T(8,128)S(1)}, f32[5,8,128]{2,1,0:T(8,128)S(1)}, u32[]{:S(2)}, u32[]{:S(2)}) collective-permute-start(f32[5,8,128]{2,1,0:T(8,128)S(1)} %get-tuple-element.19), channel_id=1, source_target_pairs={{8,0},{9,1},{10,2},{11,3},{12,4},{13,5},{14,6},{15,7}} | collective-permute-start | bytes 61448 | tf_op jit(solution)/shard_map/ppermute | solution.py:469
  9.2 3.0 %collective-permute-start.1 = (f32[24,8,384]{2,1,0:T(8,128)S(1)}, f32[24,8,384]{2,1,0:T(8,128)S(1)}, u32[]{:S(2)}, u32[]{:S(2)}) collective-permute-start(f32[24,8,384]{2,1,0:T(8,128)S(1)} %get-tuple-element.14), channel_id=1, source_target_pairs={{0,24},{1,25},{2,26},{3,27},{4,28},{5,29},{6,30},{7,31},{8,0},{9,1... | collective-permute-start | bytes 884744 | tf_op jit(solution)/shard_map/ppermute | solution.py:469
  12.3 0.0 collective-permute-start
  12.3 1.6 %collective-permute-done.6 = f32[5,8,128]{2,1,0:T(8,128)S(1)} collective-permute-done((f32[5,8,128]{2,1,0:T(8,128)S(1)}, f32[5,8,128]{2,1,0:T(8,128)S(1)}, u32[]{:S(2)}, u32[]{:S(2)}) %collective-permute-start.6) | collective-permute-done | bytes 20512 | tf_op jit(solution)/shard_map/ppermute | solution.py:469
  13.9 0.0 collective-permute-done.2.same
  13.9 0.8 %collective-permute-done.3.cross = f32[24,8,384]{2,1,0:T(8,128)S(1)} collective-permute-done((f32[24,8,384]{2,1,0:T(8,128)S(1)}, f32[24,8,384]{2,1,0:T(8,128)S(1)}, u32[]{:S(2)}, u32[]{:S(2)}) %collective-permute-start.3) | collective-permute-done | bytes 294944 | tf_op jit(solution)/shard_map/ppermute | solution.py:469
  14.7 0.1 corners.1
  14.8 2.0 %collective-permute-start.4 = (f32[2,32,384]{2,1,0:T(8,128)S(1)}, f32[2,32,384]{2,1,0:T(8,128)S(1)}, u32[]{:S(2)}, u32[]{:S(2)}) collective-permute-start(f32[2,32,384]{2,1,0:T(8,128)S(1)} %get-tuple-element.17), channel_id=1, source_target_pairs={{0,8},{1,9},{2,10},{3,11},{4,12},{5,13},{6,14},{7,15},{8,16},{9,17... | collective-permute-start | bytes 294920 | tf_op jit(solution)/shard_map/ppermute | solution.py:469
  16.8 2.1 %collective-permute-start.5 = (f32[2,32,384]{2,1,0:T(8,128)S(1)}, f32[2,32,384]{2,1,0:T(8,128)S(1)}, u32[]{:S(2)}, u32[]{:S(2)}) collective-permute-start(f32[2,32,384]{2,1,0:T(8,128)S(1)} %get-tuple-element.18), channel_id=1, source_target_pairs={{0,24},{1,25},{2,26},{3,27},{4,28},{5,29},{6,30},{7,31},{8,0},{9,1... | collective-permute-start | bytes 294920 | tf_op jit(solution)/shard_map/ppermute | solution.py:469
  18.8 11.1 %all-gather = f32[232,8,128]{2,1,0:T(8,128)S(1)} all-gather(f32[29,8,128]{2,1,0:T(8,128)S(1)} %pad_maximum_fusion), channel_id=2, replica_groups=mesh['stream'=4,'span'=8] {'span'}, dimensions={0}, use_global_device_ids=true | all-gather | bytes 1069056 | tf_op jit(solution)/shard_map/all_gather | solution.py:505
  29.9 0.0 collective-permute-done.1.x_high
  29.9 0.0 collective-permute-done.x_low
  29.9 0.0 collective-permute-done.4.c_low
  29.9 0.0 collective-permute-done.5.c_high
  29.9 0.0 copy-done.2
  30.0 0.0 copy-done.3
  30.0 0.0 copy-done.4
  30.0 4.3 %two_steps.1 = (f32[19,8,8,128]{3,2,1,0:T(8,128)}, f32[19,8,8,256]{3,2,1,0:T(8,128)}) custom-call(s32[8]{0:T(128)S(1)} %copy-done.3, s32[8]{0:T(128)S(1)} %copy-done.4, s32[1,256]{1,0:T(1,128)S(1)} %bitcast.3, f32[19,8,8,128]{3,2,1,0:T(8,128)S(1)} %get-tuple-element.11.star_pre, f32[19,8,8,256]{3,2,1,0:T(8,128)S(1)} %get-tuple-element.12.star_main, ...), custom_call_target="tpu_custom_call" | custom-call | tf_op jit(solution)/shard_map/two_steps/pallas_call | solution.py:509
  (2 shorter events, 0.0 us)
Async XLA Ops:
  0.6 1.3 %copy-start = (f32[19,8,8,256]{3,2,1,0:T(8,128)S(1)}, f32[19,8,8,256]{3,2,1,0:T(8,128)}, u32[]{:S(2)}) copy-start(f32[19,8,8,256]{3,2,1,0:T(8,128)} %main.1) | copy-start | bytes 3735556
  1.9 1.1 %copy-start.1 = (f32[19,8,8,128]{3,2,1,0:T(8,128)S(1)}, f32[19,8,8,128]{3,2,1,0:T(8,128)}, u32[]{:S(2)}) copy-start(f32[19,8,8,128]{3,2,1,0:T(8,128)} %pre.1) | copy-start | bytes 1867780
  3.8 26.1 %copy-start.2 = (s32[256]{0:T(256)S(1)}, s32[256]{0:T(256)}, u32[]{:S(2)}) copy-start(s32[256]{0:T(256)} %param.9) | copy-start | bytes 3076
  3.8 26.1 %copy-start.3 = (s32[8]{0:T(128)S(1)}, s32[8]{0:T(128)}, u32[]{:S(2)}) copy-start(s32[8]{0:T(128)} %tile_map.1) | copy-start | bytes 100
  3.9 26.1 %copy-start.4 = (s32[8]{0:T(128)S(1)}, s32[8]{0:T(128)}, u32[]{:S(2)}) copy-start(s32[8]{0:T(128)} %layer_phase.1) | copy-start | bytes 100
  3.9 10.0 %collective-permute-start.2 = (f32[24,8,384]{2,1,0:T(8,128)S(1)}, f32[24,8,384]{2,1,0:T(8,128)S(1)}, u32[]{:S(2)}, u32[]{:S(2)}) collective-permute-start(f32[24,8,384]{2,1,0:T(8,128)S(1)} %get-tuple-element.15.edge_same), channel_id=1, source_target_pairs={{0,1},{1,0},{2,3},{3,2},{4,5},{5,4},{6,7},{7,6},{8,9},{9,8},{10,11... | collective-permute-start | bytes 884744 | tf_op jit(solution)/shard_map/ppermute | solution.py:469
  4.4 10.3 %collective-permute-start.3 = (f32[24,8,384]{2,1,0:T(8,128)S(1)}, f32[24,8,384]{2,1,0:T(8,128)S(1)}, u32[]{:S(2)}, u32[]{:S(2)}) collective-permute-start(f32[24,8,384]{2,1,0:T(8,128)S(1)} %get-tuple-element.16.edge_cross), channel_id=1, source_target_pairs={{0,7},{1,2},{2,1},{3,4},{4,3},{5,6},{6,5},{7,0},{8,15},{9,10},{10,... | collective-permute-start | bytes 884744 | tf_op jit(solution)/shard_map/ppermute | solution.py:469
  7.9 5.9 %collective-permute-start.6 = (f32[5,8,128]{2,1,0:T(8,128)S(1)}, f32[5,8,128]{2,1,0:T(8,128)S(1)}, u32[]{:S(2)}, u32[]{:S(2)}) collective-permute-start(f32[5,8,128]{2,1,0:T(8,128)S(1)} %get-tuple-element.19), channel_id=1, source_target_pairs={{8,0},{9,1},{10,2},{11,3},{12,4},{13,5},{14,6},{15,7}} | collective-permute-start | bytes 61448 | tf_op jit(solution)/shard_map/ppermute | solution.py:469
  9.2 20.7 %collective-permute-start.1 = (f32[24,8,384]{2,1,0:T(8,128)S(1)}, f32[24,8,384]{2,1,0:T(8,128)S(1)}, u32[]{:S(2)}, u32[]{:S(2)}) collective-permute-start(f32[24,8,384]{2,1,0:T(8,128)S(1)} %get-tuple-element.14), channel_id=1, source_target_pairs={{0,24},{1,25},{2,26},{3,27},{4,28},{5,29},{6,30},{7,31},{8,0},{9,1... | collective-permute-start | bytes 884744 | tf_op jit(solution)/shard_map/ppermute | solution.py:469
  12.3 17.7 %collective-permute-start = (f32[24,8,384]{2,1,0:T(8,128)S(1)}, f32[24,8,384]{2,1,0:T(8,128)S(1)}, u32[]{:S(2)}, u32[]{:S(2)}) collective-permute-start(f32[24,8,384]{2,1,0:T(8,128)S(1)} %get-tuple-element.13), channel_id=1, source_target_pairs={{0,8},{1,9},{2,10},{3,11},{4,12},{5,13},{6,14},{7,15},{8,16},{9,17... | collective-permute-start | bytes 884744 | tf_op jit(solution)/shard_map/ppermute | solution.py:469
  14.8 15.2 %collective-permute-start.4 = (f32[2,32,384]{2,1,0:T(8,128)S(1)}, f32[2,32,384]{2,1,0:T(8,128)S(1)}, u32[]{:S(2)}, u32[]{:S(2)}) collective-permute-start(f32[2,32,384]{2,1,0:T(8,128)S(1)} %get-tuple-element.17), channel_id=1, source_target_pairs={{0,8},{1,9},{2,10},{3,11},{4,12},{5,13},{6,14},{7,15},{8,16},{9,17... | collective-permute-start | bytes 294920 | tf_op jit(solution)/shard_map/ppermute | solution.py:469
  16.8 13.2 %collective-permute-start.5 = (f32[2,32,384]{2,1,0:T(8,128)S(1)}, f32[2,32,384]{2,1,0:T(8,128)S(1)}, u32[]{:S(2)}, u32[]{:S(2)}) collective-permute-start(f32[2,32,384]{2,1,0:T(8,128)S(1)} %get-tuple-element.18), channel_id=1, source_target_pairs={{0,24},{1,25},{2,26},{3,27},{4,28},{5,29},{6,30},{7,31},{8,0},{9,1... | collective-permute-start | bytes 294920 | tf_op jit(solution)/shard_map/ppermute | solution.py:469

commit v3 on v2

v3 whole, which is shorter than its diff:
```python
import jax
import jax.numpy as jnp
from jax import lax
from jax.experimental import pallas as pl
from jax.experimental.pallas import tpu as pltpu
from jax.sharding import PartitionSpec as P

velocities = (
    (0, 0, 0),
    (1, 0, 0),
    (-1, 0, 0),
    (0, 1, 0),
    (0, -1, 0),
    (0, 0, 1),
    (0, 0, -1),
    (1, 1, 0),
    (-1, -1, 0),
    (1, -1, 0),
    (-1, 1, 0),
    (1, 0, 1),
    (-1, 0, -1),
    (1, 0, -1),
    (-1, 0, 1),
    (0, 1, 1),
    (0, -1, -1),
    (0, 1, -1),
    (0, -1, 1),
)
opposite = (0, 2, 1, 4, 3, 6, 5, 8, 7, 10, 9, 12, 11, 14, 13, 16, 15, 18, 17)
pairs = tuple((k, k + 1) for k in range(1, 19, 2))
incoming = (1, 7, 9, 11, 13)
backward_x = (2, 8, 10, 12, 14)
forward_z = (5, 11, 14, 15, 18)
backward_z = (6, 12, 13, 16, 17)
POPS = 19
PLANE = 16
FACE = 13
SIDE = 16
stays_x = tuple(k for k in range(POPS) if velocities[k][0] == 0)
KEPT = POPS + 5
VMEM_SMALL = 10 * 1024 * 1024
VMEM_LARGE = 20 * 1024 * 1024


def moments_of(pops):
    density = None
    moment = [None, None, None]

    def add(total, value):
        return value if total is None else total + value

    for group, weight in ((range(1, 7), 1.0 / 18.0), (range(7, POPS), 1.0 / 36.0)):
        part = None
        parts = [None, None, None]
        for a, b in ((k, k + 1) for k in group[::2]):
            if pops[a] is None and pops[b] is None:
                continue
            if pops[b] is None:
                both, diff = pops[a], pops[a]
            elif pops[a] is None:
                both, diff = pops[b], -pops[b]
            else:
                both, diff = pops[a] + pops[b], pops[a] - pops[b]
            part = add(part, both)
            for axis_num, step in enumerate(velocities[a]):
                if step != 0:
                    parts[axis_num] = add(parts[axis_num], diff if step == 1 else -diff)
        if part is not None:
            density = add(density, part * weight)
        for axis_num in range(3):
            if parts[axis_num] is not None:
                moment[axis_num] = add(moment[axis_num], parts[axis_num] * weight)
    if pops[0] is not None:
        density = add(density, pops[0] * (1.0 / 3.0))
    return density, moment


def relax(pops, density, moment, wanted):
    inverse = 1.0 / density
    speed = [component * inverse for component in moment]
    kinetic = moment[0] * speed[0] + moment[1] * speed[1] + moment[2] * speed[2]
    base = 1.25 * density - 1.875 * kinetic
    result = [None] * POPS
    if 0 in wanted:
        result[0] = base - 0.25 * pops[0]
    for a, b in pairs:
        if a not in wanted and b not in wanted:
            continue
        flux = None
        along = None
        for axis_num, step in enumerate(velocities[a]):
            if step == 0:
                continue
            if flux is None:
                flux, along = moment[axis_num], speed[axis_num]
            elif step == 1:
                flux, along = flux + moment[axis_num], along + speed[axis_num]
            else:
                flux, along = flux - moment[axis_num], along - speed[axis_num]
        even = base + 5.625 * (flux * along)
        odd = 3.75 * flux
        if a in wanted:
            result[a] = even + odd - 0.25 * pops[a]
        if b in wanted:
            result[b] = even - odd - 0.25 * pops[b]
    return result


def collide(pops, wanted=range(POPS)):
    density, moment = moments_of(pops)
    return relax(pops, density, moment, wanted)


def shift_layers(value, step_y):
    if step_y == 0:
        return value
    size = value.shape[-1]
    return pltpu.roll(value, step_y % size, value.ndim - 1)


def moved_row(base, left, right, masks, x_at, wanted=range(POPS)):
    result = []
    sub = None
    for which_pop in range(POPS):
        if which_pop not in wanted:
            result.append(None)
            continue
        step_x, step_y, step_z = velocities[which_pop]
        source = base(which_pop, x_at - step_x)
        if step_z != 0 and sub is None:
            sub = lax.broadcasted_iota(jnp.int32, source.shape, 0)
        width = source.shape[0]
        if step_z == 1:
            source = jnp.where(
                sub == 0, left(which_pop, x_at - step_x), pltpu.roll(source, 1, 0)
            )
        elif step_z == -1:
            source = jnp.where(
                sub == width - 1,
                right(which_pop, x_at - step_x),
                pltpu.roll(source, width - 1, 0),
            )
        source = shift_layers(source, step_y)
        result.append(
            jnp.where(masks[step_y] != 0, base(opposite[which_pop], x_at), source)
        )
    return result


def fill_masks(walls, masks):
    fine = walls.shape[1]
    coarse = masks.shape[2] - fine

    def fill(solid, lanes):
        layers = solid.shape[1]
        lane = lax.broadcasted_iota(jnp.int32, solid.shape, 1)
        masks[0, :, lanes] = solid
        masks[1, :, lanes] = jnp.where(lane == 0, 1.0, pltpu.roll(solid, 1, 1))
        masks[2, :, lanes] = jnp.where(lane == layers - 1, 1.0, pltpu.roll(solid, layers - 1, 1))

    solid = jnp.broadcast_to(jnp.where(walls[...] > 0, 1.0, 0.0), (8, fine))
    fine_at = lax.broadcasted_iota(jnp.int32, (fine, coarse), 0)
    coarse_at = lax.broadcasted_iota(jnp.int32, (fine, coarse), 1)
    halves = jnp.where(lax.shift_right_logical(fine_at, 1) == coarse_at, 1.0, 0.0)
    hits = jnp.dot(solid, halves, preferred_element_type=jnp.float32)
    fill(jnp.where(hits > 0.5, 1.0, 0.0), slice(0, coarse))
    fill(solid, slice(coarse, coarse + fine))


def first_kernel(
    pre,
    main,
    star_pre,
    star_main,
    z_same,
    z_cross,
):
    rows = pre.shape[1]
    coarse = pre.shape[3]
    parity = lax.rem(lax.axis_index("span"), 2)
    domains = ((pre, star_pre, slice(0, coarse)), (main, star_main, slice(coarse, None)))
    for x_at in range(rows):
        for pops, star, lanes in domains:
            out = collide([pops[which_pop, x_at] for which_pop in range(POPS)])
            for which_pop in range(POPS):
                star[which_pop, x_at] = out[which_pop]

    def edges(hi, lo):
        for _, star, lanes in domains:
            width = star.shape[2]
            for which_pop in range(POPS):
                hi[which_pop, :, lanes] = star[which_pop, :, width - 1, :]
                lo[which_pop, :, lanes] = star[which_pop, :, 0, :]
            for k in range(5):
                hi[POPS + k, :, lanes] = star[forward_z[k], :, width - 2, :]
                lo[POPS + k, :, lanes] = star[backward_z[k], :, 1, :]

    @pl.when(parity == 0)
    def _():
        edges(z_same, z_cross)

    @pl.when(parity == 1)
    def _():
        edges(z_cross, z_same)


def fill_face(star, lanes, blocked, at_top, face):
    last = star.shape[1] - 1
    moving = incoming if at_top else backward_x
    rim = last if at_top else 0
    none = lambda pop, x_at: 0.0
    base = lambda pop, x_at: star[pop, x_at]
    new = moved_row(base, none, none, blocked, rim, moving + stays_x)
    for k, pop in enumerate(moving):
        face[k, :, lanes] = star[pop, rim]
        face[5 + k, :, lanes] = new[pop]
        new[pop] = None
    density, moment = moments_of(new)
    face[10, :, lanes] = density
    face[11, :, lanes] = moment[1]
    face[12, :, lanes] = moment[2]


def face_kernel(walls, star_pre, star_main, masks, x_hi, x_lo, plane):
    coarse = star_pre.shape[3]
    fill_masks(walls, masks)
    for star, lanes in zip((star_pre, star_main), lanes_of(coarse, star_main.shape[3])):
        blocked = masks_of(masks, lanes)
        fill_face(star, lanes, blocked, True, x_hi)
        fill_face(star, lanes, blocked, False, x_lo)
    fill_plane(star_pre, masks_of(masks, slice(0, coarse)), plane)


def fill_plane(star, blocked, plane):
    width, coarse = plane.shape[1:]
    last = star.shape[1] - 1
    zero = jnp.zeros((width, coarse), jnp.float32)
    stream_pos = lax.axis_index("stream")

    @pl.when(stream_pos != 1)
    def _():
        base = lambda pop, x_at: zero if x_at > last else star[pop, x_at]
        none = lambda pop, x_at: 0.0
        new = moved_row(base, none, none, blocked, last)
        density, moment = moments_of(new)
        for k, pop in enumerate(incoming):
            plane[k] = star[pop, last]
            plane[5 + k] = new[pop]
        plane[10] = density
        for axis_num in range(3):
            plane[11 + axis_num] = moment[axis_num]
        plane[14] = zero
        plane[15] = zero
        for k in range(5):
            hi, lo = forward_z[k], backward_z[k]
            plane[14, k : k + 1, :] = base(hi, last - velocities[hi][0])[width - 1 : width]
            plane[15, k : k + 1, :] = base(lo, last - velocities[lo][0])[0:1]

    @pl.when(stream_pos == 1)
    def _():
        none = lambda pop, x_at: 0.0
        back = moved_row(
            lambda pop, x_at: star[pop, x_at] if pop in backward_x else zero,
            none,
            none,
            blocked,
            -1,
            backward_x,
        )
        density, moment = moments_of(back)
        for k, value in enumerate([density] + moment):
            plane[k] = value
        for k in range(4, PLANE):
            plane[k] = zero
        plane[14, 1:2, :] = star[14, 0, width - 1 : width, :]
        plane[15, 1:2, :] = star[12, 0, 0:1, :]


def column_values(is_left, first, second, inner, shift, blocked):
    inward, outward = (forward_z, backward_z) if is_left else (backward_z, forward_z)
    result = []
    for pop in range(POPS):
        step_x, step_y, _ = velocities[pop]
        if pop in inward:
            source = shift(second, inward.index(pop), step_x)
        elif pop in outward:
            source = shift(inner, outward.index(pop), step_x)
        else:
            source = shift(first, pop, step_x)
        result.append(
            jnp.where(blocked[step_y] != 0, first(opposite[pop]), shift_layers(source, step_y))
        )
    return result


def turned(read, at, step_x):
    value = read(at)
    return value if step_x == 0 else pltpu.roll(value, step_x % value.shape[0], 0)


def only(pops, values):
    return [values[pop] if pop in pops else None for pop in range(POPS)]


def corner_lines(is_left, side, halo, edge, masks, lanes, c_hi, c_lo):
    inward, outward = (forward_z, backward_z) if is_left else (backward_z, forward_z)
    last = halo.shape[1] - 1
    new = column_values(
        is_left,
        lambda pop: halo[pop, :, lanes],
        lambda k: halo[POPS + k, :, lanes],
        lambda k: edge[outward[k], :, lanes],
        turned,
        masks_of(masks, lanes),
    )
    for target, moving, rim, inner in ((c_hi, incoming, last, last - 1), (c_lo, backward_x, 0, 1)):
        turning = [pop for pop in moving if pop in inward][0]
        density, moment = moments_of(only(moving + stays_x, new))
        lines = [halo[pop, rim : rim + 1, lanes] for pop in moving]
        lines += [halo[pop, rim : rim + 1, lanes] for pop in inward if pop in stays_x]
        lines += [halo[turning, inner : inner + 1, lanes]]
        lines += [halo[POPS + inward.index(turning), rim : rim + 1, lanes]]
        lines += [value[rim : rim + 1] for value in [density] + moment + [new[turning]]]
        for k, line in enumerate(lines):
            target[side + k : side + k + 1, lanes] = line


def corner_kernel(
    tile_map, masks, same, cross, edge_same, edge_cross, tiles_hbm, c_hi, c_lo, tiles, arrived
):
    lanes_all = masks.shape[2]
    coarse = tiles.shape[3]
    parity = lax.rem(lax.axis_index("span"), 2)
    on_relay = lax.axis_index("stream") == 1
    copy = pltpu.make_async_copy(tiles_hbm, tiles, arrived)

    @pl.when(on_relay)
    def _():
        copy.start()

    for lanes in lanes_of(coarse, lanes_all - coarse):

        @pl.when(parity == 0)
        def _():
            corner_lines(True, SIDE, cross, edge_cross, masks, lanes, c_hi, c_lo)
            corner_lines(False, 0, same, edge_same, masks, lanes, c_hi, c_lo)

        @pl.when(parity == 1)
        def _():
            corner_lines(True, 0, same, edge_same, masks, lanes, c_hi, c_lo)
            corner_lines(False, SIDE, cross, edge_cross, masks, lanes, c_hi, c_lo)

    @pl.when(on_relay)
    def _():
        copy.wait()
        span_pos = lax.axis_index("span")
        span_count = lax.axis_size("span")
        width = tiles.shape[2]
        sub = lax.broadcasted_iota(jnp.int32, (width, coarse), 0)
        open_layers = masks[0, :, :coarse] == 0
        for at, offset in enumerate((span_count - 1, 0, 1)):
            tile = tile_map[lax.rem(span_pos + offset, span_count)]
            edges = [None] * POPS
            for pop, side, row, slot in ((14, span_count - 1, 0, 14), (12, 1, width - 1, 15)):
                line = tiles[lax.rem(tile + side, span_count), slot, 1:2, :]
                line = jnp.broadcast_to(line, (width, coarse))
                edges[pop] = jnp.where((sub == row) & open_layers, line, 0.0)
            density, moment = moments_of(edges)
            lanes = slice(at * coarse, (at + 1) * coarse)
            base = 2 * SIDE
            c_lo[base : base + 8, lanes] = tiles[tile, 0] + density
            c_lo[base + 8 : base + 16, lanes] = tiles[tile, 2]
            c_lo[base + 16 : base + 24, lanes] = tiles[tile, 3] + moment[2]


def build_columns(is_left, col, corner, halo, edge, side, x_low, x_high, c_low, c_high):
    inward, outward = (forward_z, backward_z) if is_left else (backward_z, forward_z)
    rim = 0 if is_left else x_low.shape[1] - 1
    for k in range(KEPT):
        col[k, 8:16, :] = halo[k]
    for k in range(5):
        col[KEPT + k, 8:16, :] = edge[outward[k]]
    corner[...] = jnp.zeros(corner.shape, jnp.float32)
    for moving, face, lines, near, beyond, row in (
        (incoming, x_low, c_low, 7, 6, 0),
        (backward_x, x_high, c_high, 16, 17, 9),
    ):
        line = lambda k: lines[side + k : side + k + 1, :]
        for k in range(5):
            col[moving[k], near : near + 1, :] = line(k)
        for k, pop in enumerate([pop for pop in inward if pop in stays_x]):
            col[pop, near : near + 1, :] = line(5 + k)
        turning = [pop for pop in moving if pop in inward][0]
        leaving = [pop for pop in moving if pop in outward][0]
        col[turning, beyond : beyond + 1, :] = line(8)
        at = POPS + inward.index(turning)
        col[at, near : near + 1, :] = line(9)
        at = KEPT + outward.index(leaving)
        col[at, near : near + 1, :] = face[moving.index(leaving), rim : rim + 1, :]
        for k in range(4):
            corner[k, row : row + 1, :] = line(10 + k)
        at = 4 if moving is incoming else 5
        corner[at, row : row + 1, :] = line(14)


def refine(coarse, phases, fine_len):
    coarse_len = coarse.shape[1]
    count = coarse.shape[0] // 3
    rows = lax.broadcasted_iota(jnp.int32, (coarse_len, fine_len), 0)
    fine = lax.broadcasted_iota(jnp.int32, (coarse_len, fine_len), 1)
    outs = []
    for phase in (0, 1):
        position = fine + phase
        lower = lax.shift_right_arithmetic(position - 1, 1)
        upper_wt = jnp.where(position % 2 == 0, 0.75, 0.25)
        low_idx = jnp.clip(lower, 0, coarse_len - 1)
        high_idx = jnp.clip(lower + 1, 0, coarse_len - 1)
        matrix = jnp.where(rows == low_idx, 1.0 - upper_wt, 0.0) + jnp.where(
            rows == high_idx, upper_wt, 0.0
        )
        outs.append(
            jnp.dot(
                coarse,
                matrix,
                precision=lax.Precision.HIGHEST,
                preferred_element_type=jnp.float32,
            )
        )
    return [
        jnp.where(
            phases[tile] > 0,
            outs[1][tile * count : (tile + 1) * count],
            outs[0][tile * count : (tile + 1) * count],
        )
        for tile in range(3)
    ]


def lanes_of(coarse, fine):
    return slice(0, coarse), slice(coarse, coarse + fine)


def masks_of(masks, lanes, height=8):
    values = {step: masks[step % 3, :, lanes] for step in (0, 1, -1)}
    if height == 8:
        return values
    return {
        step: jnp.broadcast_to(value[:1], (height, value.shape[1]))
        for step, value in values.items()
    }


def middle_kernel(
    tile_map,
    layer_phase,
    masks,
    star_pre,
    star_main,
    same,
    cross,
    edge_same,
    edge_cross,
    tiles_hbm,
    mid_pre,
    mid_main,
    inflow,
    awaited,
    out_pre_hbm,
    out_main_hbm,
    ghost_left,
    ghost_right,
    rim_left,
    rim_right,
    out_pre,
    out_main,
    tiles,
    arrived,
    sent,
):
    rows, width, coarse = star_pre.shape[1:]
    fine = star_main.shape[3]
    span_pos = lax.axis_index("span")
    span_count = lax.axis_size("span")
    parity = lax.rem(span_pos, 2)

    on_inlet = lax.axis_index("stream") == 0
    copy = pltpu.make_async_copy(tiles_hbm, tiles, arrived)

    @pl.when(on_inlet)
    def _():
        copy.start()

    def ghosts(is_left, ghost, halo, edge, rim):
        inward, outward = (forward_z, backward_z) if is_left else (backward_z, forward_z)
        for k in range(5):
            ghost[k] = halo[inward[k]]
        for lanes in lanes_of(coarse, fine):
            new = column_values(
                is_left,
                lambda pop: halo[pop, :, lanes],
                lambda k: halo[POPS + k, :, lanes],
                lambda k: edge[outward[k], :, lanes],
                turned,
                masks_of(masks, lanes),
            )
            out = collide(new, inward)
            for k in range(5):
                rim[k, :, lanes] = out[inward[k]]

    @pl.when(parity == 0)
    def _():
        ghosts(True, ghost_left, cross, edge_cross, rim_left)
        ghosts(False, ghost_right, same, edge_same, rim_right)

    @pl.when(parity == 1)
    def _():
        ghosts(True, ghost_left, same, edge_same, rim_left)
        ghosts(False, ghost_right, cross, edge_cross, rim_right)

    stars = (star_pre, star_main)
    for x_at in range(1, rows - 1):
        for domain, lanes in enumerate(lanes_of(coarse, fine)):
            new = moved_row(
                lambda pop, at: stars[domain][pop, at],
                lambda pop, at: ghost_left[forward_z.index(pop), at : at + 1, lanes],
                lambda pop, at: ghost_right[backward_z.index(pop), at : at + 1, lanes],
                masks_of(masks, lanes),
                x_at,
            )
            out = collide(new)
            for pop in range(POPS):
                (mid_pre, mid_main)[domain][pop, x_at - 1] = out[pop]

    copies = []
    for x_at in range(2, rows - 2):
        for domain, lanes in enumerate(lanes_of(coarse, fine)):
            new = moved_row(
                lambda pop, at: (mid_pre, mid_main)[domain][pop, at - 1],
                lambda pop, at: rim_left[forward_z.index(pop), at : at + 1, lanes],
                lambda pop, at: rim_right[backward_z.index(pop), at : at + 1, lanes],
                masks_of(masks, lanes),
                x_at,
            )
            kept = (out_pre, out_main)[domain]
            for pop in range(POPS):
                kept[pop, x_at - 2] = new[pop]
            copies.append(
                pltpu.make_async_copy(
                    kept.at[:, x_at - 2],
                    (out_pre_hbm, out_main_hbm)[domain].at[:, x_at],
                    sent.at[domain, x_at - 2],
                )
            )
            copies[-1].start()

    @pl.when(on_inlet)
    def _():
        copy.wait()
        chosen, phases = [], []
        for offset in (span_count - 1, 0, 1):
            at = lax.rem(span_pos + offset, span_count)
            chosen.append(tile_map[at])
            phases.append(layer_phase[at])

        planes = [[tiles[tile, k] for k in range(5)] for tile in chosen]
        blocked = masks_of(masks, slice(0, coarse))
        sub = lax.broadcasted_iota(jnp.int32, (width, coarse), 0)
        for place, tile in enumerate(chosen):
            edges = [None] * POPS
            for k in range(5):
                for pop, at, row, slot in (
                    (forward_z[k], span_count - 1, 0, 14),
                    (backward_z[k], 1, width - 1, 15),
                ):
                    line = tiles[lax.rem(tile + at, span_count), slot, k : k + 1, :]
                    line = shift_layers(jnp.broadcast_to(line, (width, coarse)), velocities[pop][1])
                    keep = (sub == row) & (blocked[velocities[pop][1]] == 0)
                    edges[pop] = jnp.where(keep, line, 0.0)
            density, moment = moments_of(edges)
            density = density + tiles[tile, 10]
            moment = [moment[axis_num] + tiles[tile, 11 + axis_num] for axis_num in range(3)]
            for k, value in enumerate([density] + moment):
                awaited[place, k] = value
            for k, pop in enumerate(incoming):
                new = tiles[tile, 5 + k]
                if edges[pop] is not None:
                    new = new + edges[pop]
                awaited[place, 4 + k] = new
        stacked = jnp.concatenate([plane for group in planes for plane in group], axis=0)
        for place, value in enumerate(refine(stacked, phases, fine)):
            inflow[place] = value.reshape(5, width, fine)

    for copy_out in copies:
        copy_out.wait()


def last_kernel(
    layer_phase,
    masks,
    star_pre,
    star_main,
    mid_pre,
    mid_main,
    inflow,
    awaited,
    x_low,
    x_high,
    same,
    cross,
    edge_same,
    edge_cross,
    c_low,
    c_high,
    part_pre,
    part_main,
    out_pre_hbm,
    out_main_hbm,
    col_left,
    col_right,
    corner_left,
    corner_right,
    in_low,
    in_high,
    next_pre,
    next_main,
    rim_left,
    rim_right,
    out_pre,
    out_main,
    sent,
):
    rows, width, coarse = star_pre.shape[1:]
    fine = star_main.shape[3]
    pre_lanes, main_lanes = lanes_of(coarse, fine)
    is_first = lax.axis_index("stream") == 0
    is_last = lax.axis_index("stream") == lax.axis_size("stream") - 1
    parity = lax.rem(lax.axis_index("span"), 2)
    ends = (x_low, x_high, c_low, c_high)

    @pl.when(parity == 0)
    def _():
        build_columns(True, col_left, corner_left, cross, edge_cross, SIDE, *ends)
        build_columns(False, col_right, corner_right, same, edge_same, 0, *ends)

    @pl.when(parity == 1)
    def _():
        build_columns(True, col_left, corner_left, same, edge_same, 0, *ends)
        build_columns(False, col_right, corner_right, cross, edge_cross, SIDE, *ends)

    for k in range(5):
        in_low[k] = x_low[k, :, main_lanes]
        in_high[k] = x_high[k, :, main_lanes]

    @pl.when(is_last)
    def _():
        for k in range(5):
            in_high[k] = star_main[backward_x[k], rows - 1]
        for col in (col_left, col_right):
            for k in range(KEPT + 5):
                col[k, 16:17, main_lanes] = col[k, 15:16, main_lanes]

    @pl.when(is_first)
    def _():
        before, own, after = (inflow.at[tile] for tile in range(3))
        for k in range(5):
            in_low[k] = own[k]
            col_left[incoming[k], 7:8, main_lanes] = before[k, width - 1 : width]
            col_right[incoming[k], 7:8, main_lanes] = after[k, 0:1]
        col_left[POPS + 1, 7:8, main_lanes] = before[3, width - 2 : width - 1]
        col_left[KEPT + 2, 7:8, main_lanes] = own[4, 0:1]
        col_right[POPS + 2, 7:8, main_lanes] = after[4, 1:2]
        col_right[KEPT + 1, 7:8, main_lanes] = own[3, width - 1 : width]

    for is_left, col, corner, rim in (
        (True, col_left, corner_left, rim_left),
        (False, col_right, corner_right, rim_right),
    ):
        moving = forward_z if is_left else backward_z
        for lanes in (pre_lanes, main_lanes):
            new = column_values(
                is_left,
                lambda pop, step_x=0: col[pop, 7 - step_x : 23 - step_x, lanes],
                lambda k, step_x: col[POPS + k, 7 - step_x : 23 - step_x, lanes],
                lambda k, step_x: col[KEPT + k, 7 - step_x : 23 - step_x, lanes],
                lambda read, at, step_x: read(at, step_x),
                masks_of(masks, lanes, 16),
            )
            row = lax.broadcasted_iota(jnp.int32, new[0].shape, 0)
            for pop in range(POPS):
                if pop not in backward_x:
                    new[pop] = jnp.where(row == 0, 0.0, new[pop])
                if pop not in incoming:
                    new[pop] = jnp.where(row == rows + 1, 0.0, new[pop])
            density, moment = moments_of(new)
            density = density + corner[0, :, lanes]
            moment = [moment[axis_num] + corner[1 + axis_num, :, lanes] for axis_num in range(3)]
            for at, ends_of in ((4, incoming), (5, backward_x)):
                pop = [pop for pop in moving if pop in ends_of][0]
                new[pop] = new[pop] + corner[at, :, lanes]
            out = relax(new, density, moment, moving)
            for k in range(5):
                rim[k, :, lanes] = out[moving[k]]

    stars = (star_pre, star_main)
    outer = {-1: 0, 0: 1, rows - 1: 2, rows: 3}

    def base_of(domain, lanes):
        def base(pop, x_at):
            if 0 <= x_at < rows:
                return stars[domain][pop, x_at]
            if x_at == -1:
                k = incoming.index(pop)
                return in_low[k] if domain == 1 else x_low[k, :, lanes]
            k = backward_x.index(pop)
            return in_high[k] if domain == 1 else x_high[k, :, lanes]

        return base

    def beside_tile(domain, lanes, x_at):
        star = stars[domain]
        face, moving, back = (
            (x_low, incoming, backward_x) if x_at < 0 else (x_high, backward_x, incoming)
        )
        blocked = masks_of(masks, lanes)
        left = lambda pop, at: col_left[pop, 8 + at : 9 + at, lanes]
        right = lambda pop, at: col_right[pop, 8 + at : 9 + at, lanes]

        def base(pop, at):
            return face[moving.index(pop), :, lanes] if at == x_at else star[pop, at]

        new = moved_row(base, left, right, blocked, x_at, back)
        sub = lax.broadcasted_iota(jnp.int32, new[back[0]].shape, 0)
        for pop in range(POPS):
            if pop in back:
                continue
            step_x, step_y, step_z = velocities[pop]
            if step_z != 0:
                line = (left if step_z == 1 else right)(pop, x_at - step_x)
                line = shift_layers(jnp.broadcast_to(line, sub.shape), step_y)
                keep = (sub == (0 if step_z == 1 else width - 1)) & (blocked[step_y] == 0)
                new[pop] = jnp.where(keep, line, 0.0)
            if pop in moving:
                part = face[5 + moving.index(pop), :, lanes]
                new[pop] = part if new[pop] is None else part + new[pop]
        density, moment = moments_of(new)
        density = density + face[10, :, lanes]
        moment = [moment[0], moment[1] + face[11, :, lanes], moment[2] + face[12, :, lanes]]
        return relax(new, density, moment, moving), moving

    for x_at in outer:
        for domain, lanes in enumerate((pre_lanes, main_lanes)):
            if 0 <= x_at < rows:
                new = moved_row(
                    base_of(domain, lanes),
                    lambda pop, at: col_left[pop, 8 + at : 9 + at, lanes],
                    lambda pop, at: col_right[pop, 8 + at : 9 + at, lanes],
                    masks_of(masks, lanes),
                    x_at,
                )
                out, wanted = collide(new), range(POPS)
            else:
                out, wanted = beside_tile(domain, lanes, x_at)
            for pop in wanted:
                (next_pre, next_main)[domain][pop, outer[x_at]] = out[pop]

    @pl.when(is_first)
    def _():
        span_pos, span_count = lax.axis_index("span"), lax.axis_size("span")
        phases, planes = [], []
        for place, offset in enumerate((span_count - 1, 0, 1)):
            phases.append(layer_phase[lax.rem(span_pos + offset, span_count)])
            lanes = slice(place * coarse, (place + 1) * coarse)
            base = 2 * SIDE
            back = c_high[base : base + 8, lanes]
            density = awaited[place, 0] + back
            moment = [
                awaited[place, 1] - back,
                awaited[place, 2] + c_high[base + 8 : base + 16, lanes],
                awaited[place, 3] + c_high[base + 16 : base + 24, lanes],
            ]
            new = [None] * POPS
            for k, pop in enumerate(incoming):
                new[pop] = awaited[place, 4 + k]
            out = relax(new, density, moment, incoming)
            planes += [out[pop] for pop in incoming]
        before, own, after = (
            value.reshape(5, width, fine)
            for value in refine(jnp.concatenate(planes, axis=0), phases, fine)
        )
        for k in range(5):
            next_main[incoming[k], 0] = own[k]
        rim_left[1, 0:1, main_lanes] = before[3, width - 1 : width]
        rim_right[2, 0:1, main_lanes] = after[4, 0:1]

    @pl.when(is_last)
    def _():
        for k in range(5):
            next_main[backward_x[k], 3] = next_main[backward_x[k], 2]
            for rim in (rim_left, rim_right):
                rim[k, rows + 1 : rows + 2, main_lanes] = rim[k, rows : rows + 1, main_lanes]

    def next_of(domain):
        def base(pop, x_at):
            if x_at in outer:
                return (next_pre, next_main)[domain][pop, outer[x_at]]
            return (mid_pre, mid_main)[domain][pop, x_at - 1]

        return base

    copies = []
    for at_end, x_at in enumerate((0, 1, rows - 2, rows - 1)):
        for domain, lanes in enumerate((pre_lanes, main_lanes)):
            new = moved_row(
                next_of(domain),
                lambda pop, at: rim_left[forward_z.index(pop), at + 1 : at + 2, lanes],
                lambda pop, at: rim_right[backward_z.index(pop), at + 1 : at + 2, lanes],
                masks_of(masks, lanes),
                x_at,
            )
            kept = (out_pre, out_main)[domain]
            for pop in range(POPS):
                kept[pop, at_end] = new[pop]
            copy = pltpu.make_async_copy(
                kept.at[:, at_end],
                (out_pre_hbm, out_main_hbm)[domain].at[:, x_at],
                sent.at[domain, at_end],
            )
            copy.start()
            copies.append(copy)
    for copy in copies:
        copy.wait()


def f32(*shape):
    return jax.ShapeDtypeStruct(shape, jnp.float32)


def local(pre_pops, main_pops, tile_map, layer_phase, wall_flags):
    span_count = lax.axis_size("span")
    stream_count = lax.axis_size("stream")
    _, rows, width, coarse = pre_pops.shape
    fine = main_pops.shape[3]
    lanes = coarse + fine

    def send(value, step_x, place, only=range(stream_count)):
        moves = []
        for s in range(stream_count):
            if s not in only:
                continue
            for j in range(span_count):
                target = (s + step_x) % stream_count * span_count + place(j) % span_count
                moves.append((s * span_count + j, target))
        return lax.ppermute(value, ("stream", "span"), moves)

    stay = lambda j: j
    sibling = lambda j: j + 1 if j % 2 == 0 else j - 1
    beyond = lambda j: j - 1 if j % 2 == 0 else j + 1
    params = pltpu.CompilerParams(vmem_limit_bytes=VMEM_SMALL)

    whole = pl.BlockSpec(memory_space=pltpu.VMEM)
    outside = pl.BlockSpec(memory_space=pltpu.HBM)
    scalars = pl.BlockSpec(memory_space=pltpu.SMEM)

    star_pre, star_main, z_same, z_cross = pl.pallas_call(
        first_kernel,
        out_shape=(
            f32(*pre_pops.shape),
            f32(*main_pops.shape),
            f32(KEPT, rows, lanes),
            f32(KEPT, rows, lanes),
        ),
        compiler_params=params,
        name="collide_and_pack",
    )(pre_pops, main_pops)
    masks, x_hi, x_lo, plane = pl.pallas_call(
        face_kernel,
        out_shape=(
            f32(3, 8, lanes),
            f32(FACE, width, lanes),
            f32(FACE, width, lanes),
            f32(PLANE, width, coarse),
        ),
        compiler_params=params,
        name="faces",
    )(wall_flags.reshape(1, fine), star_pre, star_main)

    same = send(z_same, 0, sibling)
    cross = send(z_cross, 0, beyond)
    x_low = send(x_hi, 1, stay)
    x_high = send(x_lo, -1, stay)
    tiles = lax.all_gather(plane, "span", axis=0, tiled=False)
    anywhere = pl.BlockSpec(memory_space=pl.ANY)
    all_tiles = [
        pltpu.VMEM((span_count, PLANE, width, coarse), jnp.float32),
        pltpu.SemaphoreType.DMA,
    ]
    c_hi, c_lo = pl.pallas_call(
        corner_kernel,
        out_shape=(f32(2 * SIDE, lanes), f32(2 * SIDE + 24, lanes)),
        in_specs=[scalars] + [whole] * 5 + [anywhere],
        scratch_shapes=all_tiles,
        compiler_params=params,
        name="corners",
    )(tile_map, masks, same, cross, z_same, z_cross, tiles)
    c_low = send(c_hi, 1, stay)
    c_high = send(c_lo, -1, stay)
    half_pre = pltpu.VMEM((POPS, 4, width, coarse), jnp.float32)
    half_main = pltpu.VMEM((POPS, 4, width, fine), jnp.float32)
    mid_pre, mid_main, inflow, awaited, part_pre, part_main = pl.pallas_call(
        middle_kernel,
        out_shape=(
            f32(POPS, rows - 2, width, coarse),
            f32(POPS, rows - 2, width, fine),
            f32(3, 5, width, fine),
            f32(3, 9, width, coarse),
            f32(*pre_pops.shape),
            f32(*main_pops.shape),
        ),
        in_specs=[scalars, scalars] + [whole] * 7 + [anywhere],
        out_specs=[whole] * 4 + [outside] * 2,
        scratch_shapes=[
            pltpu.VMEM((5, rows, lanes), jnp.float32),
            pltpu.VMEM((5, rows, lanes), jnp.float32),
            pltpu.VMEM((5, rows, lanes), jnp.float32),
            pltpu.VMEM((5, rows, lanes), jnp.float32),
            pltpu.VMEM((POPS, rows - 4, width, coarse), jnp.float32),
            pltpu.VMEM((POPS, rows - 4, width, fine), jnp.float32),
        ]
        + all_tiles
        + [pltpu.SemaphoreType.DMA((2, rows - 4))],
        compiler_params=params,
        name="middle_rows",
    )(tile_map, layer_phase, masks, star_pre, star_main, same, cross, z_same, z_cross, tiles)
    return pl.pallas_call(
        last_kernel,
        out_shape=(f32(*pre_pops.shape), f32(*main_pops.shape)),
        in_specs=[scalars] + [whole] * 15 + [outside] * 2,
        out_specs=(outside, outside),
        input_output_aliases={16: 0, 17: 1},
        scratch_shapes=[
            pltpu.VMEM((KEPT + 5, 24, lanes), jnp.float32),
            pltpu.VMEM((KEPT + 5, 24, lanes), jnp.float32),
            pltpu.VMEM((6, 16, lanes), jnp.float32),
            pltpu.VMEM((6, 16, lanes), jnp.float32),
            pltpu.VMEM((5, width, fine), jnp.float32),
            pltpu.VMEM((5, width, fine), jnp.float32),
            half_pre,
            half_main,
            pltpu.VMEM((5, 16, lanes), jnp.float32),
            pltpu.VMEM((5, 16, lanes), jnp.float32),
            half_pre,
            half_main,
            pltpu.SemaphoreType.DMA((2, 4)),
        ],
        compiler_params=pltpu.CompilerParams(vmem_limit_bytes=VMEM_LARGE),
        name="last_rows",
    )(
        layer_phase,
        masks,
        star_pre,
        star_main,
        mid_pre,
        mid_main,
        inflow,
        awaited,
        x_low,
        x_high,
        same,
        cross,
        z_same,
        z_cross,
        c_low,
        c_high,
        part_pre,
        part_main,
    )


def solution(mesh):
    return jax.shard_map(
        local,
        mesh=mesh,
        in_specs=(P(None, "stream", "span", None), P(None, "stream", "span", None), P(), P(), P()),
        out_specs=(P(None, "stream", "span", None), P(None, "stream", "span", None)),
        check_vma=False,
    )
```

time: 34.5 us -> 33.6 us (0.974)
  blocking collectives: 11.1 us -> 8.89 us
  Pallas kernels: 5.18 us -> 7.33 us
  starting transfers between devices: 12.4 us -> 10.7 us
  waiting for transfers between devices: 2.43 us -> 3.43 us
    all_gather x1, blocking collectives: 11.1 us -> 8.89 us  [local(): tiles = lax.all_gather(plane, 'span', axis=0, tiled=False)]
    pallas_call x2 -> x4, Pallas kernels: 4.35 us -> 6.49 us  [the longest x1 2.94 us: local(): pl.pallas_call(last_kernel, out_shape=(f32(*pre_pops.shape), f32(*main_po...]
    ppermute x7 -> x6, starting transfers between devices: 12.4 us -> 10.7 us  [send(): return lax.ppermute(value, ('stream', 'span'), moves)]
    ppermute x7 -> x6, waiting for transfers between devices: 2.43 us -> 3.43 us  [send(): return lax.ppermute(value, ('stream', 'span'), moves)]
  transfers between devices with their start and end apart: 7 -> 6, of which waited for: 2 -> 1; matrix products, arithmetic and copies ran while one was open for 0% -> 0% of each run, Pallas kernels for 0% -> 11%
where the time goes in v3:
time: 33.6 us; the launch traced here: 33.4 us
  starting transfers between devices  10.7 us (32%)
  blocking collectives  8.89 us (26%)
  Pallas kernels  7.33 us (22%)
  waiting for transfers between devices  3.43 us (10%)
  local copies, waits for them, and re-layouts  2.38 us (7%)
  between operations  0.71 us (2%)
    ppermute x6, starting transfers between devices, send(): return lax.ppermute(value, ('stream', 'span'), moves)  10.7 us
    all_gather x1, blocking collectives, local(): tiles = lax.all_gather(plane, 'span', axis=0, tiled=False)  8.89 us
    ppermute x6, waiting for transfers between devices, send(): return lax.ppermute(value, ('stream', 'span'), moves)  3.43 us
    pallas_call x1, Pallas kernels, local(): pl.pallas_call(last_kernel, out_shape=(f32(*pre_pops.shape), f32(*main_po...  2.94 us
    pallas_call x1, Pallas kernels, local(): pl.pallas_call(middle_kernel, out_shape=(f32(POPS, rows - 2, width, coars...  2.44 us
    unnamed x10, local copies, waits for them, and re-layouts  2.38 us
    pallas_call x1, Pallas kernels, local(): pl.pallas_call(first_kernel, out_shape=(f32(*pre_pops.shape), f32(*main_p...  0.85 us
    pallas_call x1, Pallas kernels, local(): pl.pallas_call(corner_kernel, out_shape=(f32(2 * SIDE, lanes), f32(2 * SI...  0.81 us
  transfers between devices with their start and end apart: 6, of which 1 were waited for; matrix products, arithmetic and copies ran while one was open for 0% of the time, Pallas kernels for 11%

profile of v3, /device:TPU:0, one launch (start us, length us, event | category | flops | bytes accessed | tf_op | source)
XLA Modules:
  0.0 33.4 jit_solution(6409056301523246181)
XLA Ops:
  0.6 0.0 copy-start
  0.6 1.3 %copy-done = f32[19,8,8,256]{3,2,1,0:T(8,128)S(1)} copy-done((f32[19,8,8,256]{3,2,1,0:T(8,128)S(1)}, f32[19,8,8,256]{3,2,1,0:T(8,128)}, u32[]{:S(2)}) %copy-start) | copy-done | bytes 1245208
  1.9 0.0 copy-start.1
  1.9 1.1 %copy-done.1 = f32[19,8,8,128]{3,2,1,0:T(8,128)S(1)} copy-done((f32[19,8,8,128]{3,2,1,0:T(8,128)S(1)}, f32[19,8,8,128]{3,2,1,0:T(8,128)}, u32[]{:S(2)}) %copy-start.1) | copy-done | bytes 622616
  3.0 0.0 copy-start.4
  3.0 0.8 %collide_and_pack.1 = (f32[19,8,8,128]{3,2,1,0:T(8,128)S(1)}, f32[19,8,8,256]{3,2,1,0:T(8,128)S(1)}, f32[24,8,384]{2,1,0:T(8,128)S(1)}, f32[24,8,384]{2,1,0:T(8,128)S(1)}) custom-call(f32[19,8,8,128]{3,2,1,0:T(8,128)S(1)} %copy-done.1, f32[19,8,8,256]{3,2,1,0:T(8,128)S(1)} %copy-done), custom_call_target="tpu_custom_call" | custom-call | tf_op jit(solution)/shard_map/collide_and_pack/pallas_call | solution.py:864
  3.9 0.0 copy-start.2
  3.9 0.5 %collective-permute-start = (f32[24,8,384]{2,1,0:T(8,128)S(1)}, f32[24,8,384]{2,1,0:T(8,128)S(1)}, u32[]{:S(2)}, u32[]{:S(2)}) collective-permute-start(f32[24,8,384]{2,1,0:T(8,128)S(1)} %get-tuple-element.21.edge_same), channel_id=1, source_target_pairs={{0,1},{1,0},{2,3},{3,2},{4,5},{5,4},{6,7},{7,6},{8,9},{9,8},{10,11... | collective-permute-start | bytes 884744 | tf_op jit(solution)/shard_map/ppermute | solution.py:853
  4.4 3.6 %collective-permute-start.1 = (f32[24,8,384]{2,1,0:T(8,128)S(1)}, f32[24,8,384]{2,1,0:T(8,128)S(1)}, u32[]{:S(2)}, u32[]{:S(2)}) collective-permute-start(f32[24,8,384]{2,1,0:T(8,128)S(1)} %get-tuple-element.22.edge_cross), channel_id=1, source_target_pairs={{0,7},{1,2},{2,1},{3,4},{4,3},{5,6},{6,5},{7,0},{8,15},{9,10},{10,... | collective-permute-start | bytes 884744 | tf_op jit(solution)/shard_map/ppermute | solution.py:853
  7.9 0.0 copy-done.4
  7.9 0.3 faces.1
  8.3 0.0 copy-start.3
  8.3 1.6 %collective-permute-start.2 = (f32[13,8,384]{2,1,0:T(8,128)S(1)}, f32[13,8,384]{2,1,0:T(8,128)S(1)}, u32[]{:S(2)}, u32[]{:S(2)}) collective-permute-start(f32[13,8,384]{2,1,0:T(8,128)S(1)} %get-tuple-element.28), channel_id=1, source_target_pairs={{0,8},{1,9},{2,10},{3,11},{4,12},{5,13},{6,14},{7,15},{8,16},{9,17... | collective-permute-start | bytes 479240 | tf_op jit(solution)/shard_map/ppermute | solution.py:853
  9.8 2.3 %collective-permute-start.3 = (f32[13,8,384]{2,1,0:T(8,128)S(1)}, f32[13,8,384]{2,1,0:T(8,128)S(1)}, u32[]{:S(2)}, u32[]{:S(2)}) collective-permute-start(f32[13,8,384]{2,1,0:T(8,128)S(1)} %get-tuple-element.29), channel_id=1, source_target_pairs={{0,24},{1,25},{2,26},{3,27},{4,28},{5,29},{6,30},{7,31},{8,0},{9,1... | collective-permute-start | bytes 479240 | tf_op jit(solution)/shard_map/ppermute | solution.py:853
  12.1 8.9 %all-gather = f32[128,8,128]{2,1,0:T(8,128)S(1)} all-gather(f32[16,8,128]{2,1,0:T(8,128)S(1)} %get-tuple-element.23), channel_id=2, replica_groups=mesh['stream'=4,'span'=8] {'span'}, dimensions={0}, use_global_device_ids=true | all-gather | bytes 589824 | tf_op jit(solution)/shard_map/all_gather | solution.py:891
  21.0 0.0 collective-permute-done.same
  21.0 0.0 collective-permute-done.1.cross
  21.0 0.0 copy-done.2
  21.0 0.8 %corners.1 = (f32[32,384]{1,0:T(8,128)S(1)}, f32[56,384]{1,0:T(8,128)S(1)}) custom-call(s32[8]{0:T(128)S(1)} %copy-done.2, f32[3,8,384]{2,1,0:T(8,128)S(1)} %get-tuple-element.20.masks, f32[24,8,384]{2,1,0:T(8,128)S(1)} %collective-permute-done.same, f32[24,8,384]{2,1,0:T(8,128)S(1)} %collective-permute-done.1.cross, ...), custom_call_target="tpu_custom_call" | custom-call | tf_op jit(solution)/shard_map/corners/pallas_call | solution.py:897
  21.9 2.7 %collective-permute-start.5 = (f32[56,384]{1,0:T(8,128)S(1)}, f32[56,384]{1,0:T(8,128)S(1)}, u32[]{:S(2)}, u32[]{:S(2)}) collective-permute-start(f32[56,384]{1,0:T(8,128)S(1)} %get-tuple-element.31), channel_id=1, source_target_pairs={{0,24},{1,25},{2,26},{3,27},{4,28},{5,29},{6,30},{7,31},{8,0},{9,1... | collective-permute-start | bytes 258056 | tf_op jit(solution)/shard_map/ppermute | solution.py:853
  24.6 0.0 collective-permute-start.4
  24.6 0.0 copy-done.3
  24.6 2.4 %middle_rows.1 = (f32[19,6,8,128]{3,2,1,0:T(8,128)S(1)}, f32[19,6,8,256]{3,2,1,0:T(8,128)S(1)}, f32[3,5,8,256]{3,2,1,0:T(8,128)S(1)}, f32[3,9,8,128]{3,2,1,0:T(8...) custom-call(s32[8]{0:T(128)S(1)} %copy-done.2, s32[8]{0:T(128)S(1)} %copy-done.3, ...), custom_call_target="tpu_custom_call" | custom-call | tf_op jit(solution)/shard_map/middle_rows/pallas_call | solution.py:909
  27.0 0.0 collective-permute-done.2.x_low
  27.0 0.0 collective-permute-done.3.x_high
  27.0 3.4 %collective-permute-done.4.c_low = f32[32,384]{1,0:T(8,128)S(1)} collective-permute-done((f32[32,384]{1,0:T(8,128)S(1)}, f32[32,384]{1,0:T(8,128)S(1)}, u32[]{:S(2)}, u32[]{:S(2)}) %collective-permute-start.4) | collective-permute-done | bytes 49184 | tf_op jit(solution)/shard_map/ppermute | solution.py:853
  30.5 0.0 collective-permute-done.5.c_high
  30.5 2.9 %last_rows.1 = (f32[19,8,8,128]{3,2,1,0:T(8,128)}, f32[19,8,8,256]{3,2,1,0:T(8,128)}) custom-call(s32[8]{0:T(128)S(1)} %copy-done.3, f32[3,8,384]{2,1,0:T(8,128)S(1)} %get-tuple-element.20.masks, f32[19,8,8,128]{3,2,1,0:T(8,128)S(1)} %get-tuple-element.18.star_pre, ...), custom_call_target="tpu_custom_call", output_to_operand_aliasing={{0}: (16, {}), {1}: (17, {})} | custom-call | tf_op jit(solution)/shard_map/last_rows/pallas_call | solution.py:934
Async XLA Ops:
  0.6 1.3 %copy-start = (f32[19,8,8,256]{3,2,1,0:T(8,128)S(1)}, f32[19,8,8,256]{3,2,1,0:T(8,128)}, u32[]{:S(2)}) copy-start(f32[19,8,8,256]{3,2,1,0:T(8,128)} %main.1) | copy-start | bytes 3735556
  1.9 1.1 %copy-start.1 = (f32[19,8,8,128]{3,2,1,0:T(8,128)S(1)}, f32[19,8,8,128]{3,2,1,0:T(8,128)}, u32[]{:S(2)}) copy-start(f32[19,8,8,128]{3,2,1,0:T(8,128)} %pre.1) | copy-start | bytes 1867780
  3.0 4.9 %copy-start.4 = (s32[256]{0:T(256)S(1)}, s32[256]{0:T(256)}, u32[]{:S(2)}) copy-start(s32[256]{0:T(256)} %param.9) | copy-start | bytes 3076
  3.9 17.2 %copy-start.2 = (s32[8]{0:T(128)S(1)}, s32[8]{0:T(128)}, u32[]{:S(2)}) copy-start(s32[8]{0:T(128)} %tile_map.3) | copy-start | bytes 100
  3.9 17.2 %collective-permute-start = (f32[24,8,384]{2,1,0:T(8,128)S(1)}, f32[24,8,384]{2,1,0:T(8,128)S(1)}, u32[]{:S(2)}, u32[]{:S(2)}) collective-permute-start(f32[24,8,384]{2,1,0:T(8,128)S(1)} %get-tuple-element.21.edge_same), channel_id=1, source_target_pairs={{0,1},{1,0},{2,3},{3,2},{4,5},{5,4},{6,7},{7,6},{8,9},{9,8},{10,11... | collective-permute-start | bytes 884744 | tf_op jit(solution)/shard_map/ppermute | solution.py:853
  4.4 16.6 %collective-permute-start.1 = (f32[24,8,384]{2,1,0:T(8,128)S(1)}, f32[24,8,384]{2,1,0:T(8,128)S(1)}, u32[]{:S(2)}, u32[]{:S(2)}) collective-permute-start(f32[24,8,384]{2,1,0:T(8,128)S(1)} %get-tuple-element.22.edge_cross), channel_id=1, source_target_pairs={{0,7},{1,2},{2,1},{3,4},{4,3},{5,6},{6,5},{7,0},{8,15},{9,10},{10,... | collective-permute-start | bytes 884744 | tf_op jit(solution)/shard_map/ppermute | solution.py:853
  8.3 16.3 %copy-start.3 = (s32[8]{0:T(128)S(1)}, s32[8]{0:T(128)}, u32[]{:S(2)}) copy-start(s32[8]{0:T(128)} %layer_phase.3) | copy-start | bytes 100
  8.3 18.8 %collective-permute-start.2 = (f32[13,8,384]{2,1,0:T(8,128)S(1)}, f32[13,8,384]{2,1,0:T(8,128)S(1)}, u32[]{:S(2)}, u32[]{:S(2)}) collective-permute-start(f32[13,8,384]{2,1,0:T(8,128)S(1)} %get-tuple-element.28), channel_id=1, source_target_pairs={{0,8},{1,9},{2,10},{3,11},{4,12},{5,13},{6,14},{7,15},{8,16},{9,17... | collective-permute-start | bytes 479240 | tf_op jit(solution)/shard_map/ppermute | solution.py:853
  9.8 17.2 %collective-permute-start.3 = (f32[13,8,384]{2,1,0:T(8,128)S(1)}, f32[13,8,384]{2,1,0:T(8,128)S(1)}, u32[]{:S(2)}, u32[]{:S(2)}) collective-permute-start(f32[13,8,384]{2,1,0:T(8,128)S(1)} %get-tuple-element.29), channel_id=1, source_target_pairs={{0,24},{1,25},{2,26},{3,27},{4,28},{5,29},{6,30},{7,31},{8,0},{9,1... | collective-permute-start | bytes 479240 | tf_op jit(solution)/shard_map/ppermute | solution.py:853
  21.9 8.6 %collective-permute-start.5 = (f32[56,384]{1,0:T(8,128)S(1)}, f32[56,384]{1,0:T(8,128)S(1)}, u32[]{:S(2)}, u32[]{:S(2)}) collective-permute-start(f32[56,384]{1,0:T(8,128)S(1)} %get-tuple-element.31), channel_id=1, source_target_pairs={{0,24},{1,25},{2,26},{3,27},{4,28},{5,29},{6,30},{7,31},{8,0},{9,1... | collective-permute-start | bytes 258056 | tf_op jit(solution)/shard_map/ppermute | solution.py:853
  24.6 5.9 %collective-permute-start.4 = (f32[32,384]{1,0:T(8,128)S(1)}, f32[32,384]{1,0:T(8,128)S(1)}, u32[]{:S(2)}, u32[]{:S(2)}) collective-permute-start(f32[32,384]{1,0:T(8,128)S(1)} %get-tuple-element.30), channel_id=1, source_target_pairs={{0,8},{1,9},{2,10},{3,11},{4,12},{5,13},{6,14},{7,15},{8,16},{9,17... | collective-permute-start | bytes 147464 | tf_op jit(solution)/shard_map/ppermute | solution.py:853

commit v4 on v3

--- a/solution.py
+++ b/solution.py
@@ -34,7 +34,7 @@
 backward_z = (6, 12, 13, 16, 17)
 POPS = 19
 PLANE = 16
-FACE = 13
+FACE = 14
 SIDE = 16
 stays_x = tuple(k for k in range(POPS) if velocities[k][0] == 0)
 KEPT = POPS + 5
@@ -168,18 +168,33 @@
 
 
 def first_kernel(
-    pre,
-    main,
+    pre_hbm,
+    main_hbm,
     star_pre,
     star_main,
     z_same,
     z_cross,
+    pre,
+    main,
+    arrived,
 ):
     rows = pre.shape[1]
     coarse = pre.shape[3]
     parity = lax.rem(lax.axis_index("span"), 2)
     domains = ((pre, star_pre, slice(0, coarse)), (main, star_main, slice(coarse, None)))
+    copies = [
+        [
+            pltpu.make_async_copy(source.at[:, x_at], target.at[:, x_at], arrived.at[at, x_at])
+            for at, (source, target) in enumerate(((pre_hbm, pre), (main_hbm, main)))
+        ]
+        for x_at in range(rows)
+    ]
+    for row in copies:
+        for copy in row:
+            copy.start()
     for x_at in range(rows):
+        for copy in copies[x_at]:
+            copy.wait()
         for pops, star, lanes in domains:
             out = collide([pops[which_pop, x_at] for which_pop in range(POPS)])
             for which_pop in range(POPS):
@@ -202,6 +217,12 @@
     @pl.when(parity == 1)
     def _():
         edges(z_cross, z_same)
+
+
+def edge_lines(pops, moving, rim, inner):
+    return [(pop, rim) for pop in pops if pop in stays_x] + [
+        (pop, inner) for pop in pops if pop in moving
+    ]
 
 
 def fill_face(star, lanes, blocked, at_top, face):
@@ -219,6 +240,11 @@
     face[10, :, lanes] = density
     face[11, :, lanes] = moment[1]
     face[12, :, lanes] = moment[2]
+    inner = rim - 1 if at_top else rim + 1
+    for first, pops, z_at in ((0, backward_z, 0), (4, forward_z, star.shape[2] - 1)):
+        for k, (pop, x_at) in enumerate(edge_lines(pops, moving, rim, inner)):
+            row = first + k
+            face[13, row : row + 1, lanes] = star[pop, x_at, z_at : z_at + 1, :]
 
 
 def face_kernel(walls, star_pre, star_main, masks, x_hi, x_lo, plane):
@@ -302,60 +328,52 @@
     return [values[pop] if pop in pops else None for pop in range(POPS)]
 
 
-def corner_lines(is_left, side, halo, edge, masks, lanes, c_hi, c_lo):
-    inward, outward = (forward_z, backward_z) if is_left else (backward_z, forward_z)
-    last = halo.shape[1] - 1
-    new = column_values(
-        is_left,
-        lambda pop: halo[pop, :, lanes],
-        lambda k: halo[POPS + k, :, lanes],
-        lambda k: edge[outward[k], :, lanes],
-        turned,
-        masks_of(masks, lanes),
-    )
-    for target, moving, rim, inner in ((c_hi, incoming, last, last - 1), (c_lo, backward_x, 0, 1)):
-        turning = [pop for pop in moving if pop in inward][0]
-        density, moment = moments_of(only(moving + stays_x, new))
-        lines = [halo[pop, rim : rim + 1, lanes] for pop in moving]
-        lines += [halo[pop, rim : rim + 1, lanes] for pop in inward if pop in stays_x]
-        lines += [halo[turning, inner : inner + 1, lanes]]
-        lines += [halo[POPS + inward.index(turning), rim : rim + 1, lanes]]
-        lines += [value[rim : rim + 1] for value in [density] + moment + [new[turning]]]
-        for k, line in enumerate(lines):
-            target[side + k : side + k + 1, lanes] = line
-
-
-def corner_kernel(
-    tile_map, masks, same, cross, edge_same, edge_cross, tiles_hbm, c_hi, c_lo, tiles, arrived
-):
-    lanes_all = masks.shape[2]
-    coarse = tiles.shape[3]
+def corner_kernel(x_low, x_high, tiles, e_same, e_cross):
+    def lines(is_left, target):
+        inward = forward_z if is_left else backward_z
+        edge, second, first = (7, 6, 4) if is_left else (0, 1, 0)
+        for start, moving, face in ((0, incoming, x_low), (SIDE, backward_x, x_high)):
+            turning = moving.index([pop for pop in moving if pop in inward][0])
+            new = [None] * POPS
+            for k, pop in enumerate(moving):
+                new[pop] = face[5 + k]
+            density, moment = moments_of(new)
+            sums = [
+                density + face[10],
+                moment[0],
+                moment[1] + face[11],
+                moment[2] + face[12],
+                face[5 + turning],
+            ]
+            found = [face[k, edge : edge + 1, :] for k in range(5)]
+            found += [face[13, first + k : first + k + 1, :] for k in range(4)]
+            found += [face[turning, second : second + 1, :]]
+            found += [value[edge : edge + 1] for value in sums]
+            for k, line in enumerate(found):
+                target[start + k : start + k + 1, :] = line
+
     parity = lax.rem(lax.axis_index("span"), 2)
-    on_relay = lax.axis_index("stream") == 1
-    copy = pltpu.make_async_copy(tiles_hbm, tiles, arrived)
-
-    @pl.when(on_relay)
-    def _():
+
+    @pl.when(parity == 0)
+    def _():
+        lines(True, e_same)
+        lines(False, e_cross)
+
+    @pl.when(parity == 1)
+    def _():
+        lines(False, e_same)
+        lines(True, e_cross)
+
+
+def back_kernel(tile_map, masks, tiles_hbm, back, tiles, arrived):
+    @pl.when(lax.axis_index("stream") == 1)
+    def _():
+        copy = pltpu.make_async_copy(tiles_hbm, tiles, arrived)
         copy.start()
-
-    for lanes in lanes_of(coarse, lanes_all - coarse):
-
-        @pl.when(parity == 0)
-        def _():
-            corner_lines(True, SIDE, cross, edge_cross, masks, lanes, c_hi, c_lo)
-            corner_lines(False, 0, same, edge_same, masks, lanes, c_hi, c_lo)
-
-        @pl.when(parity == 1)
-        def _():
-            corner_lines(True, 0, same, edge_same, masks, lanes, c_hi, c_lo)
-            corner_lines(False, SIDE, cross, edge_cross, masks, lanes, c_hi, c_lo)
-
-    @pl.when(on_relay)
-    def _():
         copy.wait()
         span_pos = lax.axis_index("span")
         span_count = lax.axis_size("span")
-        width = tiles.shape[2]
+        width, coarse = tiles.shape[2:]
         sub = lax.broadcasted_iota(jnp.int32, (width, coarse), 0)
         open_layers = masks[0, :, :coarse] == 0
         for at, offset in enumerate((span_count - 1, 0, 1)):
@@ -366,26 +384,24 @@
                 line = jnp.broadcast_to(line, (width, coarse))
                 edges[pop] = jnp.where((sub == row) & open_layers, line, 0.0)
             density, moment = moments_of(edges)
-            lanes = slice(at * coarse, (at + 1) * coarse)
-            base = 2 * SIDE
-            c_lo[base : base + 8, lanes] = tiles[tile, 0] + density
-            c_lo[base + 8 : base + 16, lanes] = tiles[tile, 2]
-            c_lo[base + 16 : base + 24, lanes] = tiles[tile, 3] + moment[2]
-
-
-def build_columns(is_left, col, corner, halo, edge, side, x_low, x_high, c_low, c_high):
+            back[at, 0] = tiles[tile, 0] + density
+            back[at, 1] = tiles[tile, 2]
+            back[at, 2] = tiles[tile, 3] + moment[2]
+
+
+def build_columns(is_left, col, corner, halo, edge, lines, x_low, x_high, masks):
     inward, outward = (forward_z, backward_z) if is_left else (backward_z, forward_z)
-    rim = 0 if is_left else x_low.shape[1] - 1
+    rim, first = (0, 0) if is_left else (7, 4)
     for k in range(KEPT):
         col[k, 8:16, :] = halo[k]
     for k in range(5):
         col[KEPT + k, 8:16, :] = edge[outward[k]]
     corner[...] = jnp.zeros(corner.shape, jnp.float32)
-    for moving, face, lines, near, beyond, row in (
-        (incoming, x_low, c_low, 7, 6, 0),
-        (backward_x, x_high, c_high, 16, 17, 9),
+    for moving, face, start, near, beyond, row in (
+        (incoming, x_low, 0, 7, 6, 0),
+        (backward_x, x_high, SIDE, 16, 17, 9),
     ):
-        line = lambda k: lines[side + k : side + k + 1, :]
+        line = lambda k: lines[start + k : start + k + 1, :]
         for k in range(5):
             col[moving[k], near : near + 1, :] = line(k)
         for k, pop in enumerate([pop for pop in inward if pop in stays_x]):
@@ -401,6 +417,16 @@
             corner[k, row : row + 1, :] = line(10 + k)
         at = 4 if moving is incoming else 5
         corner[at, row : row + 1, :] = line(14)
+        for lanes, blocked in masks:
+            missing = [None] * POPS
+            for k, (pop, _) in enumerate(edge_lines(outward, moving, 0, 0)):
+                step_y = velocities[pop][1]
+                value = face[13, first + k : first + k + 1, lanes]
+                value = shift_layers(jnp.broadcast_to(value, blocked[0].shape), step_y)
+                missing[pop] = jnp.where(blocked[step_y] != 0, 0.0, value)
+            density, moment = moments_of(missing)
+            for k, value in enumerate([density] + moment):
+                corner[k, row : row + 1, lanes] += value[:1]
 
 
 def refine(coarse, phases, fine_len):
@@ -595,26 +621,25 @@
 
 
 def last_kernel(
-    layer_phase,
     masks,
     star_pre,
     star_main,
     mid_pre,
     mid_main,
     inflow,
-    awaited,
     x_low,
     x_high,
     same,
     cross,
     edge_same,
     edge_cross,
-    c_low,
-    c_high,
+    e_same,
+    e_cross,
     part_pre,
     part_main,
     out_pre_hbm,
     out_main_hbm,
+    kept_rows,
     col_left,
     col_right,
     corner_left,
@@ -635,17 +660,17 @@
     is_first = lax.axis_index("stream") == 0
     is_last = lax.axis_index("stream") == lax.axis_size("stream") - 1
     parity = lax.rem(lax.axis_index("span"), 2)
-    ends = (x_low, x_high, c_low, c_high)
+    ends = (x_low, x_high, [(lanes, masks_of(masks, lanes)) for lanes in (pre_lanes, main_lanes)])
 
     @pl.when(parity == 0)
     def _():
-        build_columns(True, col_left, corner_left, cross, edge_cross, SIDE, *ends)
-        build_columns(False, col_right, corner_right, same, edge_same, 0, *ends)
+        build_columns(True, col_left, corner_left, cross, edge_cross, e_cross, *ends)
+        build_columns(False, col_right, corner_right, same, edge_same, e_same, *ends)
 
     @pl.when(parity == 1)
     def _():
-        build_columns(True, col_left, corner_left, same, edge_same, 0, *ends)
-        build_columns(False, col_right, corner_right, cross, edge_cross, SIDE, *ends)
+        build_columns(True, col_left, corner_left, same, edge_same, e_same, *ends)
+        build_columns(False, col_right, corner_right, cross, edge_cross, e_cross, *ends)
 
     for k in range(5):
         in_low[k] = x_low[k, :, main_lanes]
@@ -763,34 +788,8 @@
             for pop in wanted:
                 (next_pre, next_main)[domain][pop, outer[x_at]] = out[pop]
 
-    @pl.when(is_first)
-    def _():
-        span_pos, span_count = lax.axis_index("span"), lax.axis_size("span")
-        phases, planes = [], []
-        for place, offset in enumerate((span_count - 1, 0, 1)):
-            phases.append(layer_phase[lax.rem(span_pos + offset, span_count)])
-            lanes = slice(place * coarse, (place + 1) * coarse)
-            base = 2 * SIDE
-            back = c_high[base : base + 8, lanes]
-            density = awaited[place, 0] + back
-            moment = [
-                awaited[place, 1] - back,
-                awaited[place, 2] + c_high[base + 8 : base + 16, lanes],
-                awaited[place, 3] + c_high[base + 16 : base + 24, lanes],
-            ]
-            new = [None] * POPS
-            for k, pop in enumerate(incoming):
-                new[pop] = awaited[place, 4 + k]
-            out = relax(new, density, moment, incoming)
-            planes += [out[pop] for pop in incoming]
-        before, own, after = (
-            value.reshape(5, width, fine)
-            for value in refine(jnp.concatenate(planes, axis=0), phases, fine)
-        )
-        for k in range(5):
-            next_main[incoming[k], 0] = own[k]
-        rim_left[1, 0:1, main_lanes] = before[3, width - 1 : width]
-        rim_right[2, 0:1, main_lanes] = after[4, 0:1]
+    for k in range(5):
+        kept_rows[k] = next_main[backward_x[k], 1]
 
     @pl.when(is_last)
     def _():
@@ -831,6 +830,51 @@
         copy.wait()
 
 
+def inlet_kernel(layer_phase, masks, awaited, back, kept_rows, main_hbm, out_hbm, ready, sent):
+    @pl.when(lax.axis_index("stream") == 0)
+    def _():
+        width, coarse = awaited.shape[2:]
+        fine = masks.shape[2] - coarse
+        span_pos, span_count = lax.axis_index("span"), lax.axis_size("span")
+        phases, planes = [], []
+        for place, offset in enumerate((span_count - 1, 0, 1)):
+            phases.append(layer_phase[lax.rem(span_pos + offset, span_count)])
+            density = awaited[place, 0] + back[place, 0]
+            moment = [
+                awaited[place, 1] - back[place, 0],
+                awaited[place, 2] + back[place, 1],
+                awaited[place, 3] + back[place, 2],
+            ]
+            new = [None] * POPS
+            for k, pop in enumerate(incoming):
+                new[pop] = awaited[place, 4 + k]
+            out = relax(new, density, moment, incoming)
+            planes += [out[pop] for pop in incoming]
+        before, own, after = (
+            value.reshape(5, width, fine)
+            for value in refine(jnp.concatenate(planes, axis=0), phases, fine)
+        )
+
+        def base(pop, x_at):
+            return own[incoming.index(pop)] if x_at < 0 else kept_rows[backward_x.index(pop)]
+
+        new = moved_row(
+            base,
+            lambda pop, x_at: before[incoming.index(pop), width - 1 : width],
+            lambda pop, x_at: after[incoming.index(pop), 0:1],
+            masks_of(masks, slice(coarse, coarse + fine)),
+            0,
+            incoming,
+        )
+        copies = []
+        for k, pop in enumerate(incoming):
+            ready[k] = new[pop]
+            copies.append(pltpu.make_async_copy(ready.at[k], out_hbm.at[pop, 0], sent.at[k]))
+            copies[-1].start()
+        for copy in copies:
+            copy.wait()
+
+
 def f32(*shape):
     return jax.ShapeDtypeStruct(shape, jnp.float32)
 
@@ -861,6 +905,7 @@
     outside = pl.BlockSpec(memory_space=pltpu.HBM)
     scalars = pl.BlockSpec(memory_space=pltpu.SMEM)
 
+    in_hbm = lambda value: pltpu.with_memory_space_constraint(value, pltpu.HBM)
     star_pre, star_main, z_same, z_cross = pl.pallas_call(
         first_kernel,
         out_shape=(
@@ -869,9 +914,15 @@
             f32(KEPT, rows, lanes),
             f32(KEPT, rows, lanes),
         ),
-        compiler_params=params,
+        in_specs=[outside, outside],
+        scratch_shapes=[
+            pltpu.VMEM(pre_pops.shape, jnp.float32),
+            pltpu.VMEM(main_pops.shape, jnp.float32),
+            pltpu.SemaphoreType.DMA((2, rows)),
+        ],
+        compiler_params=pltpu.CompilerParams(vmem_limit_bytes=VMEM_SMALL),
         name="collide_and_pack",
-    )(pre_pops, main_pops)
+    )(in_hbm(pre_pops), in_hbm(main_pops))
     masks, x_hi, x_lo, plane = pl.pallas_call(
         face_kernel,
         out_shape=(
@@ -894,16 +945,24 @@
         pltpu.VMEM((span_count, PLANE, width, coarse), jnp.float32),
         pltpu.SemaphoreType.DMA,
     ]
-    c_hi, c_lo = pl.pallas_call(
+    e_to_same, e_to_cross = pl.pallas_call(
         corner_kernel,
-        out_shape=(f32(2 * SIDE, lanes), f32(2 * SIDE + 24, lanes)),
-        in_specs=[scalars] + [whole] * 5 + [anywhere],
+        out_shape=(f32(2 * SIDE, lanes), f32(2 * SIDE, lanes)),
+        in_specs=[whole] * 2 + [anywhere],
+        compiler_params=params,
+        name="corners",
+    )(x_low, x_high, tiles)
+    e_same = send(e_to_same, 0, sibling)
+    e_cross = send(e_to_cross, 0, beyond)
+    back = pl.pallas_call(
+        back_kernel,
+        out_shape=f32(3, 3, width, coarse),
+        in_specs=[scalars, whole, anywhere],
         scratch_shapes=all_tiles,
         compiler_params=params,
-        name="corners",
-    )(tile_map, masks, same, cross, z_same, z_cross, tiles)
-    c_low = send(c_hi, 1, stay)
-    c_high = send(c_lo, -1, stay)
+        name="behind_plane",
+    )(tile_map, masks, tiles)
+    back = send(back, -1, stay, (1 % stream_count,))
     half_pre = pltpu.VMEM((POPS, 4, width, coarse), jnp.float32)
     half_main = pltpu.VMEM((POPS, 4, width, fine), jnp.float32)
     mid_pre, mid_main, inflow, awaited, part_pre, part_main = pl.pallas_call(
@@ -931,12 +990,12 @@
         compiler_params=params,
         name="middle_rows",
     )(tile_map, layer_phase, masks, star_pre, star_main, same, cross, z_same, z_cross, tiles)
-    return pl.pallas_call(
+    out_pre, out_main, kept_rows = pl.pallas_call(
         last_kernel,
-        out_shape=(f32(*pre_pops.shape), f32(*main_pops.shape)),
-        in_specs=[scalars] + [whole] * 15 + [outside] * 2,
-        out_specs=(outside, outside),
-        input_output_aliases={16: 0, 17: 1},
+        out_shape=(f32(*pre_pops.shape), f32(*main_pops.shape), f32(5, width, fine)),
+        in_specs=[whole] * 14 + [outside] * 2,
+        out_specs=(outside, outside, whole),
+        input_output_aliases={14: 0, 15: 1},
         scratch_shapes=[
             pltpu.VMEM((KEPT + 5, 24, lanes), jnp.float32),
             pltpu.VMEM((KEPT + 5, 24, lanes), jnp.float32),
@@ -955,25 +1014,37 @@
         compiler_params=pltpu.CompilerParams(vmem_limit_bytes=VMEM_LARGE),
         name="last_rows",
     )(
-        layer_phase,
         masks,
         star_pre,
         star_main,
         mid_pre,
         mid_main,
         inflow,
-        awaited,
         x_low,
         x_high,
         same,
         cross,
         z_same,
         z_cross,
-        c_low,
-        c_high,
+        e_same,
+        e_cross,
         part_pre,
         part_main,
     )
+    out_main = pl.pallas_call(
+        inlet_kernel,
+        out_shape=f32(*main_pops.shape),
+        in_specs=[scalars] + [whole] * 4 + [outside],
+        out_specs=outside,
+        input_output_aliases={5: 0},
+        scratch_shapes=[
+            pltpu.VMEM((5, width, fine), jnp.float32),
+            pltpu.SemaphoreType.DMA((5,)),
+        ],
+        compiler_params=params,
+        name="inlet_row",
+    )(layer_phase, masks, awaited, back, kept_rows, out_main)
+    return out_pre, out_main
 
 
 def solution(mesh):

time: 33.6 us -> 29.9 us (0.89)
  waiting for transfers between devices: 3.43 us -> 0.05 us
  local copies, waits for them, and re-layouts: 2.38 us -> 0.01 us
  Pallas kernels: 7.33 us -> 9.17 us
    ppermute x6 -> x7, waiting for transfers between devices: 3.43 us -> 0.05 us  [send(): return lax.ppermute(value, ('stream', 'span'), moves)]
    unnamed x10 -> x6, local copies, waits for them, and re-layouts: 2.38 us -> 0.01 us
    pallas_call x0 -> x2, Pallas kernels: none -> 2.28 us  [the longest x1 1.71 us: local(): pl.pallas_call(inlet_kernel, out_shape=f32(*main_pops.shape), in_specs=[s...]
    pallas_call x1, Pallas kernels: 0.85 us -> 2.06 us  [local(): pl.pallas_call(first_kernel, out_shape=(f32(*pre_pops.shape), f32(*main_p...]
    pallas_call x1, Pallas kernels: 2.94 us -> 2 us  [local(): pl.pallas_call(last_kernel, out_shape=(f32(*pre_pops.shape), f32(*main_po...]
    pallas_call x1, Pallas kernels: 0.81 us -> 0.05 us  [local(): pl.pallas_call(corner_kernel, out_shape=(f32(2 * SIDE, lanes), f32(2 * SI...]
    ppermute x6 -> x7, starting transfers between devices: 10.7 us -> 10.9 us  [send(): return lax.ppermute(value, ('stream', 'span'), moves)]
  transfers between devices with their start and end apart: 6 -> 7, of which waited for: 1 -> 0; matrix products, arithmetic and copies ran while one was open for 0% -> 0% of each run, Pallas kernels for 11% -> 18%
where the time goes in v4:
time: 29.9 us; the launch traced here: 29.7 us
  starting transfers between devices  10.9 us (36%)
  Pallas kernels  9.17 us (31%)
  blocking collectives  8.88 us (30%)
  between operations  0.75 us (3%)
    ppermute x7, starting transfers between devices, send(): return lax.ppermute(value, ('stream', 'span'), moves)  10.9 us
    all_gather x1, blocking collectives, local(): tiles = lax.all_gather(plane, 'span', axis=0, tiled=False)  8.88 us
    pallas_call x1, Pallas kernels, local(): pl.pallas_call(middle_kernel, out_shape=(f32(POPS, rows - 2, width, coars...  2.48 us
    pallas_call x1, Pallas kernels, local(): pl.pallas_call(first_kernel, out_shape=(f32(*pre_pops.shape), f32(*main_p...  2.06 us
    pallas_call x1, Pallas kernels, local(): pl.pallas_call(last_kernel, out_shape=(f32(*pre_pops.shape), f32(*main_po...  2 us
    pallas_call x1, Pallas kernels, local(): pl.pallas_call(inlet_kernel, out_shape=f32(*main_pops.shape), in_specs=[s...  1.71 us
  transfers between devices with their start and end apart: 7, of which 0 were waited for; matrix products, arithmetic and copies ran while one was open for 0% of the time, Pallas kernels for 18%

profile of v4, /device:TPU:0, one launch (start us, length us, event | category | flops | bytes accessed | tf_op | source)
XLA Modules:
  0.0 29.7 jit_solution(5254506891774292528)
XLA Ops:
  0.6 0.0 copy-start.2
  0.6 2.1 %collide_and_pack.1 = (f32[19,8,8,128]{3,2,1,0:T(8,128)S(1)}, f32[19,8,8,256]{3,2,1,0:T(8,128)S(1)}, f32[24,8,384]{2,1,0:T(8,128)S(1)}, f32[24,8,384]{2,1,0:T(8,128)S(1)}) custom-call(f32[19,8,8,128]{3,2,1,0:T(8,128)} %pre_hbm.1, f32[19,8,8,256]{3,2,1,0:T(8,128)} %main_hbm.1), custom_call_target="tpu_custom_call" | custom-call | tf_op jit(solution)/shard_map/collide_and_pack/pallas_call | solution.py:909
  2.7 0.5 %collective-permute-start = (f32[24,8,384]{2,1,0:T(8,128)S(1)}, f32[24,8,384]{2,1,0:T(8,128)S(1)}, u32[]{:S(2)}, u32[]{:S(2)}) collective-permute-start(f32[24,8,384]{2,1,0:T(8,128)S(1)} %get-tuple-element.24.edge_same), channel_id=1, source_target_pairs={{0,1},{1,0},{2,3},{3,2},{4,5},{5,4},{6,7},{7,6},{8,9},{9,8},{10,11... | collective-permute-start | bytes 884744 | tf_op jit(solution)/shard_map/ppermute | solution.py:897
  3.2 3.5 %collective-permute-start.1 = (f32[24,8,384]{2,1,0:T(8,128)S(1)}, f32[24,8,384]{2,1,0:T(8,128)S(1)}, u32[]{:S(2)}, u32[]{:S(2)}) collective-permute-start(f32[24,8,384]{2,1,0:T(8,128)S(1)} %get-tuple-element.25.edge_cross), channel_id=1, source_target_pairs={{0,7},{1,2},{2,1},{3,4},{4,3},{5,6},{6,5},{7,0},{8,15},{9,10},{10,... | collective-permute-start | bytes 884744 | tf_op jit(solution)/shard_map/ppermute | solution.py:897
  6.8 0.0 copy-done.2
  6.8 0.0 copy-start.1
  6.8 0.3 %faces.1 = (f32[3,8,384]{2,1,0:T(8,128)S(1)}, f32[14,8,384]{2,1,0:T(8,128)S(1)}, f32[14,8,384]{2,1,0:T(8,128)S(1)}, f32[16,8,128]{2,1,0:T(8,128)S(1)}) custom-call(s32[1,256]{1,0:T(1,128)S(1)} %bitcast.5, f32[19,8,8,128]{3,2,1,0:T(8,128)S(1)} %get-tuple-element.21.star_pre, f32[19,8,8,256]{3,2,1,0:T(8,128)S(1)} %get-tuple-element.22.star_main), custom_call_target="tpu_custom_call" | custom-call | tf_op jit(solution)/shard_map/faces/pallas_call | solution.py:926
  7.1 0.0 copy-start
  7.1 1.6 %collective-permute-start.2 = (f32[14,8,384]{2,1,0:T(8,128)S(1)}, f32[14,8,384]{2,1,0:T(8,128)S(1)}, u32[]{:S(2)}, u32[]{:S(2)}) collective-permute-start(f32[14,8,384]{2,1,0:T(8,128)S(1)} %get-tuple-element.30), channel_id=1, source_target_pairs={{0,8},{1,9},{2,10},{3,11},{4,12},{5,13},{6,14},{7,15},{8,16},{9,17... | collective-permute-start | bytes 516104 | tf_op jit(solution)/shard_map/ppermute | solution.py:897
  8.7 2.3 %collective-permute-start.3 = (f32[14,8,384]{2,1,0:T(8,128)S(1)}, f32[14,8,384]{2,1,0:T(8,128)S(1)}, u32[]{:S(2)}, u32[]{:S(2)}) collective-permute-start(f32[14,8,384]{2,1,0:T(8,128)S(1)} %get-tuple-element.31), channel_id=1, source_target_pairs={{0,24},{1,25},{2,26},{3,27},{4,28},{5,29},{6,30},{7,31},{8,0},{9,1... | collective-permute-start | bytes 516104 | tf_op jit(solution)/shard_map/ppermute | solution.py:897
  11.0 8.9 %all-gather = f32[128,8,128]{2,1,0:T(8,128)S(1)} all-gather(f32[16,8,128]{2,1,0:T(8,128)S(1)} %get-tuple-element.26), channel_id=2, replica_groups=mesh['stream'=4,'span'=8] {'span'}, dimensions={0}, use_global_device_ids=true | all-gather | bytes 589824 | tf_op jit(solution)/shard_map/all_gather | solution.py:942
  19.9 0.0 collective-permute-done.2.x_low
  19.9 0.0 collective-permute-done.3.x_high
  19.9 0.4 %collective-permute-start.4 = (f32[32,384]{1,0:T(8,128)S(1)}, f32[32,384]{1,0:T(8,128)S(1)}, u32[]{:S(2)}, u32[]{:S(2)}) collective-permute-start(f32[32,384]{1,0:T(8,128)S(1)} %get-tuple-element.32), channel_id=1, source_target_pairs={{0,1},{1,0},{2,3},{3,2},{4,5},{5,4},{6,7},{7,6},{8,9},{9,8},{10,11... | collective-permute-start | bytes 147464 | tf_op jit(solution)/shard_map/ppermute | solution.py:897
  20.4 1.2 %collective-permute-start.5 = (f32[32,384]{1,0:T(8,128)S(1)}, f32[32,384]{1,0:T(8,128)S(1)}, u32[]{:S(2)}, u32[]{:S(2)}) collective-permute-start(f32[32,384]{1,0:T(8,128)S(1)} %get-tuple-element.33), channel_id=1, source_target_pairs={{0,7},{1,2},{2,1},{3,4},{4,3},{5,6},{6,5},{7,0},{8,15},{9,10},{10,... | collective-permute-start | bytes 147464 | tf_op jit(solution)/shard_map/ppermute | solution.py:897
  21.6 0.0 copy-done.1
  21.6 0.6 %behind_plane.1 = f32[3,3,8,128]{3,2,1,0:T(8,128)S(1)} custom-call(s32[8]{0:T(128)S(1)} %copy-done.1, f32[3,8,384]{2,1,0:T(8,128)S(1)} %get-tuple-element.23.masks, f32[8,16,8,128]{3,2,1,0:T(8,128)S(1)} %bitcast.3), custom_call_target="tpu_custom_call" | custom-call | tf_op jit(solution)/shard_map/behind_plane/pallas_call | solution.py:957
  22.2 1.3 %collective-permute-start.6 = (f32[3,3,8,128]{3,2,1,0:T(8,128)S(1)}, f32[3,3,8,128]{3,2,1,0:T(8,128)S(1)}, u32[]{:S(2)}, u32[]{:S(2)}) collective-permute-start(f32[3,3,8,128]{3,2,1,0:T(8,128)S(1)} %behind_plane.1), channel_id=1, source_target_pairs={{8,0},{9,1},{10,2},{11,3},{12,4},{13,5},{14,6},{15,7}} | collective-permute-start | bytes 110600 | tf_op jit(solution)/shard_map/ppermute | solution.py:897
  23.5 0.0 collective-permute-done.same
  23.5 0.0 collective-permute-done.1.cross
  23.5 0.0 copy-done
  23.5 2.5 %middle_rows.1 = (f32[19,6,8,128]{3,2,1,0:T(8,128)S(1)}, f32[19,6,8,256]{3,2,1,0:T(8,128)S(1)}, f32[3,5,8,256]{3,2,1,0:T(8,128)S(1)}, f32[3,9,8,128]{3,2,1,0:T(8...) custom-call(s32[8]{0:T(128)S(1)} %copy-done.1, s32[8]{0:T(128)S(1)} %copy-done, ...), custom_call_target="tpu_custom_call" | custom-call | tf_op jit(solution)/shard_map/middle_rows/pallas_call | solution.py:968
  26.0 0.0 collective-permute-done.4.e_same
  26.0 0.0 collective-permute-done.5.e_cross
  26.0 2.0 %last_rows.1 = (f32[19,8,8,128]{3,2,1,0:T(8,128)}, f32[19,8,8,256]{3,2,1,0:T(8,128)}, f32[5,8,256]{2,1,0:T(8,128)S(1)}) custom-call(f32[3,8,384]{2,1,0:T(8,128)S(1)} %get-tuple-element.23.masks, f32[19,8,8,128]{3,2,1,0:T(8,128)S(1)} %get-tuple-element.21.star_pre, ...), custom_call_target="tpu_custom_call", output_to_operand_aliasing={{0}: (14, {}), {1}: (15, {})} | custom-call | tf_op jit(solution)/shard_map/last_rows/pallas_call | solution.py:993
  28.0 0.0 collective-permute-done.6.back
  28.0 1.7 %inlet_row.1 = f32[19,8,8,256]{3,2,1,0:T(8,128)} custom-call(s32[8]{0:T(128)S(1)} %copy-done, f32[3,8,384]{2,1,0:T(8,128)S(1)} %get-tuple-element.23.masks, f32[3,9,8,128]{3,2,1,0:T(8,128)S(1)} %get-tuple-element.37.awaited, f32[3,3,8,128]{3,2,1,0:T(8,128)S(1)} %collective-permute-done.6.back, ...), custom_call_target="tpu_custom_call", output_to_operand_aliasing={{}: (5, {})} | custom-call | tf_op jit(solution)/shard_map/inlet_row/pallas_call | solution.py:1034
  (1 shorter events, 0.0 us)
Async XLA Ops:
  0.6 6.2 %copy-start.2 = (s32[256]{0:T(256)S(1)}, s32[256]{0:T(256)}, u32[]{:S(2)}) copy-start(s32[256]{0:T(256)} %param.9) | copy-start | bytes 3076
  2.7 20.7 %collective-permute-start = (f32[24,8,384]{2,1,0:T(8,128)S(1)}, f32[24,8,384]{2,1,0:T(8,128)S(1)}, u32[]{:S(2)}, u32[]{:S(2)}) collective-permute-start(f32[24,8,384]{2,1,0:T(8,128)S(1)} %get-tuple-element.24.edge_same), channel_id=1, source_target_pairs={{0,1},{1,0},{2,3},{3,2},{4,5},{5,4},{6,7},{7,6},{8,9},{9,8},{10,11... | collective-permute-start | bytes 884744 | tf_op jit(solution)/shard_map/ppermute | solution.py:897
  3.2 20.2 %collective-permute-start.1 = (f32[24,8,384]{2,1,0:T(8,128)S(1)}, f32[24,8,384]{2,1,0:T(8,128)S(1)}, u32[]{:S(2)}, u32[]{:S(2)}) collective-permute-start(f32[24,8,384]{2,1,0:T(8,128)S(1)} %get-tuple-element.25.edge_cross), channel_id=1, source_target_pairs={{0,7},{1,2},{2,1},{3,4},{4,3},{5,6},{6,5},{7,0},{8,15},{9,10},{10,... | collective-permute-start | bytes 884744 | tf_op jit(solution)/shard_map/ppermute | solution.py:897
  6.8 14.8 %copy-start.1 = (s32[8]{0:T(128)S(1)}, s32[8]{0:T(128)}, u32[]{:S(2)}) copy-start(s32[8]{0:T(128)} %tile_map.3) | copy-start | bytes 100
  7.1 16.4 %copy-start = (s32[8]{0:T(128)S(1)}, s32[8]{0:T(128)}, u32[]{:S(2)}) copy-start(s32[8]{0:T(128)} %layer_phase.3) | copy-start | bytes 100
  7.1 12.8 %collective-permute-start.2 = (f32[14,8,384]{2,1,0:T(8,128)S(1)}, f32[14,8,384]{2,1,0:T(8,128)S(1)}, u32[]{:S(2)}, u32[]{:S(2)}) collective-permute-start(f32[14,8,384]{2,1,0:T(8,128)S(1)} %get-tuple-element.30), channel_id=1, source_target_pairs={{0,8},{1,9},{2,10},{3,11},{4,12},{5,13},{6,14},{7,15},{8,16},{9,17... | collective-permute-start | bytes 516104 | tf_op jit(solution)/shard_map/ppermute | solution.py:897
  8.7 11.2 %collective-permute-start.3 = (f32[14,8,384]{2,1,0:T(8,128)S(1)}, f32[14,8,384]{2,1,0:T(8,128)S(1)}, u32[]{:S(2)}, u32[]{:S(2)}) collective-permute-start(f32[14,8,384]{2,1,0:T(8,128)S(1)} %get-tuple-element.31), channel_id=1, source_target_pairs={{0,24},{1,25},{2,26},{3,27},{4,28},{5,29},{6,30},{7,31},{8,0},{9,1... | collective-permute-start | bytes 516104 | tf_op jit(solution)/shard_map/ppermute | solution.py:897
  19.9 6.0 %collective-permute-start.4 = (f32[32,384]{1,0:T(8,128)S(1)}, f32[32,384]{1,0:T(8,128)S(1)}, u32[]{:S(2)}, u32[]{:S(2)}) collective-permute-start(f32[32,384]{1,0:T(8,128)S(1)} %get-tuple-element.32), channel_id=1, source_target_pairs={{0,1},{1,0},{2,3},{3,2},{4,5},{5,4},{6,7},{7,6},{8,9},{9,8},{10,11... | collective-permute-start | bytes 147464 | tf_op jit(solution)/shard_map/ppermute | solution.py:897
  20.4 5.6 %collective-permute-start.5 = (f32[32,384]{1,0:T(8,128)S(1)}, f32[32,384]{1,0:T(8,128)S(1)}, u32[]{:S(2)}, u32[]{:S(2)}) collective-permute-start(f32[32,384]{1,0:T(8,128)S(1)} %get-tuple-element.33), channel_id=1, source_target_pairs={{0,7},{1,2},{2,1},{3,4},{4,3},{5,6},{6,5},{7,0},{8,15},{9,10},{10,... | collective-permute-start | bytes 147464 | tf_op jit(solution)/shard_map/ppermute | solution.py:897
  22.2 5.9 %collective-permute-start.6 = (f32[3,3,8,128]{3,2,1,0:T(8,128)S(1)}, f32[3,3,8,128]{3,2,1,0:T(8,128)S(1)}, u32[]{:S(2)}, u32[]{:S(2)}) collective-permute-start(f32[3,3,8,128]{3,2,1,0:T(8,128)S(1)} %behind_plane.1), channel_id=1, source_target_pairs={{8,0},{9,1},{10,2},{11,3},{12,4},{13,5},{14,6},{15,7}} | collective-permute-start | bytes 110600 | tf_op jit(solution)/shard_map/ppermute | solution.py:897

commit v5 on v4

--- a/solution.py
+++ b/solution.py
@@ -371,22 +371,20 @@
         copy = pltpu.make_async_copy(tiles_hbm, tiles, arrived)
         copy.start()
         copy.wait()
-        span_pos = lax.axis_index("span")
-        span_count = lax.axis_size("span")
         width, coarse = tiles.shape[2:]
         sub = lax.broadcasted_iota(jnp.int32, (width, coarse), 0)
         open_layers = masks[0, :, :coarse] == 0
-        for at, offset in enumerate((span_count - 1, 0, 1)):
-            tile = tile_map[lax.rem(span_pos + offset, span_count)]
+        for at, number in enumerate(neighbours(tile_map)):
             edges = [None] * POPS
-            for pop, side, row, slot in ((14, span_count - 1, 0, 14), (12, 1, width - 1, 15)):
-                line = tiles[lax.rem(tile + side, span_count), slot, 1:2, :]
+            for pop, offset, row, slot in ((14, -1, 0, 14), (12, 1, width - 1, 15)):
+                line = tile_at(tiles, number, (slot,), offset)[0][1:2]
                 line = jnp.broadcast_to(line, (width, coarse))
                 edges[pop] = jnp.where((sub == row) & open_layers, line, 0.0)
             density, moment = moments_of(edges)
-            back[at, 0] = tiles[tile, 0] + density
-            back[at, 1] = tiles[tile, 2]
-            back[at, 2] = tiles[tile, 3] + moment[2]
+            sums = tile_at(tiles, number, (0, 2, 3))
+            back[at, 0] = sums[0] + density
+            back[at, 1] = sums[1]
+            back[at, 2] = sums[2] + moment[2]
 
 
 def build_columns(is_left, col, corner, halo, edge, lines, x_low, x_high, masks):
@@ -429,12 +427,35 @@
                 corner[k, row : row + 1, lanes] += value[:1]
 
 
+def entry_at(row, at):
+    lane = lax.broadcasted_iota(jnp.int32, row.shape, 1)
+    return jnp.sum(jnp.where(lane == at, row[...].astype(jnp.float32), 0.0), axis=1, keepdims=True)
+
+
+def neighbours(row):
+    count = row.shape[1]
+    position = lax.axis_index("span")
+    return [entry_at(row, lax.rem(position + step, count)) for step in (count - 1, 0, 1)]
+
+
+def tile_at(tiles, number, slots, offset=0):
+    count = tiles.shape[0]
+    found = [tiles[offset % count, slot] for slot in slots]
+    for tile in range(1, count):
+        here = jnp.broadcast_to(number, found[0].shape) == float(tile)
+        found = [
+            jnp.where(here, tiles[(tile + offset) % count, slot], value)
+            for slot, value in zip(slots, found)
+        ]
+    return found
+
+
 def refine(coarse, phases, fine_len):
     coarse_len = coarse.shape[1]
     count = coarse.shape[0] // 3
     rows = lax.broadcasted_iota(jnp.int32, (coarse_len, fine_len), 0)
     fine = lax.broadcasted_iota(jnp.int32, (coarse_len, fine_len), 1)
-    outs = []
+    matrices = []
     for phase in (0, 1):
         position = fine + phase
         lower = lax.shift_right_arithmetic(position - 1, 1)
@@ -444,17 +465,22 @@
         matrix = jnp.where(rows == low_idx, 1.0 - upper_wt, 0.0) + jnp.where(
             rows == high_idx, upper_wt, 0.0
         )
-        outs.append(
-            jnp.dot(
-                coarse,
-                matrix,
-                precision=lax.Precision.HIGHEST,
-                preferred_element_type=jnp.float32,
-            )
-        )
+        matrices.append(matrix.astype(jnp.bfloat16))
+    parts = []
+    rest = coarse
+    for _ in range(3):
+        parts.append(rest.astype(jnp.bfloat16))
+        rest = rest - parts[-1].astype(jnp.float32)
+    outs = []
+    for matrix in matrices:
+        total = None
+        for part in reversed(parts):
+            product = jnp.dot(part, matrix, preferred_element_type=jnp.float32)
+            total = product if total is None else total + product
+        outs.append(total)
     return [
         jnp.where(
-            phases[tile] > 0,
+            jnp.broadcast_to(phases[tile], (count, fine_len)) > 0.5,
             outs[1][tile * count : (tile + 1) * count],
             outs[0][tile * count : (tile + 1) * count],
         )
@@ -505,9 +531,7 @@
 ):
     rows, width, coarse = star_pre.shape[1:]
     fine = star_main.shape[3]
-    span_pos = lax.axis_index("span")
-    span_count = lax.axis_size("span")
-    parity = lax.rem(span_pos, 2)
+    parity = lax.rem(lax.axis_index("span"), 2)
 
     on_inlet = lax.axis_index("stream") == 0
     copy = pltpu.make_async_copy(tiles_hbm, tiles, arrived)
@@ -582,38 +606,31 @@
     @pl.when(on_inlet)
     def _():
         copy.wait()
-        chosen, phases = [], []
-        for offset in (span_count - 1, 0, 1):
-            at = lax.rem(span_pos + offset, span_count)
-            chosen.append(tile_map[at])
-            phases.append(layer_phase[at])
-
-        planes = [[tiles[tile, k] for k in range(5)] for tile in chosen]
+        planes = []
         blocked = masks_of(masks, slice(0, coarse))
         sub = lax.broadcasted_iota(jnp.int32, (width, coarse), 0)
-        for place, tile in enumerate(chosen):
+        for place, number in enumerate(neighbours(tile_map)):
+            found = tile_at(tiles, number, range(14))
+            planes += found[:5]
             edges = [None] * POPS
-            for k in range(5):
-                for pop, at, row, slot in (
-                    (forward_z[k], span_count - 1, 0, 14),
-                    (backward_z[k], 1, width - 1, 15),
-                ):
-                    line = tiles[lax.rem(tile + at, span_count), slot, k : k + 1, :]
-                    line = shift_layers(jnp.broadcast_to(line, (width, coarse)), velocities[pop][1])
+            for pops, offset, row, slot in (
+                (forward_z, -1, 0, 14),
+                (backward_z, 1, width - 1, 15),
+            ):
+                lines = tile_at(tiles, number, (slot,), offset)[0]
+                for k, pop in enumerate(pops):
+                    line = jnp.broadcast_to(lines[k : k + 1], (width, coarse))
+                    line = shift_layers(line, velocities[pop][1])
                     keep = (sub == row) & (blocked[velocities[pop][1]] == 0)
                     edges[pop] = jnp.where(keep, line, 0.0)
             density, moment = moments_of(edges)
-            density = density + tiles[tile, 10]
-            moment = [moment[axis_num] + tiles[tile, 11 + axis_num] for axis_num in range(3)]
             for k, value in enumerate([density] + moment):
-                awaited[place, k] = value
+                awaited[place, k] = found[10 + k] + value
             for k, pop in enumerate(incoming):
-                new = tiles[tile, 5 + k]
-                if edges[pop] is not None:
-                    new = new + edges[pop]
-                awaited[place, 4 + k] = new
-        stacked = jnp.concatenate([plane for group in planes for plane in group], axis=0)
-        for place, value in enumerate(refine(stacked, phases, fine)):
+                new = found[5 + k]
+                awaited[place, 4 + k] = new if edges[pop] is None else new + edges[pop]
+        refined = refine(jnp.concatenate(planes, axis=0), neighbours(layer_phase), fine)
+        for place, value in enumerate(refined):
             inflow[place] = value.reshape(5, width, fine)
 
     for copy_out in copies:
@@ -835,10 +852,8 @@
     def _():
         width, coarse = awaited.shape[2:]
         fine = masks.shape[2] - coarse
-        span_pos, span_count = lax.axis_index("span"), lax.axis_size("span")
-        phases, planes = [], []
-        for place, offset in enumerate((span_count - 1, 0, 1)):
-            phases.append(layer_phase[lax.rem(span_pos + offset, span_count)])
+        planes = []
+        for place in range(3):
             density = awaited[place, 0] + back[place, 0]
             moment = [
                 awaited[place, 1] - back[place, 0],
@@ -852,7 +867,7 @@
             planes += [out[pop] for pop in incoming]
         before, own, after = (
             value.reshape(5, width, fine)
-            for value in refine(jnp.concatenate(planes, axis=0), phases, fine)
+            for value in refine(jnp.concatenate(planes, axis=0), neighbours(layer_phase), fine)
         )
 
         def base(pop, x_at):
@@ -903,7 +918,7 @@
 
     whole = pl.BlockSpec(memory_space=pltpu.VMEM)
     outside = pl.BlockSpec(memory_space=pltpu.HBM)
-    scalars = pl.BlockSpec(memory_space=pltpu.SMEM)
+    tile_row, phase_row = (row.reshape(1, span_count) for row in (tile_map, layer_phase))
 
     in_hbm = lambda value: pltpu.with_memory_space_constraint(value, pltpu.HBM)
     star_pre, star_main, z_same, z_cross = pl.pallas_call(
@@ -957,11 +972,11 @@
     back = pl.pallas_call(
         back_kernel,
         out_shape=f32(3, 3, width, coarse),
-        in_specs=[scalars, whole, anywhere],
+        in_specs=[whole, whole, anywhere],
         scratch_shapes=all_tiles,
         compiler_params=params,
         name="behind_plane",
-    )(tile_map, masks, tiles)
+    )(tile_row, masks, tiles)
     back = send(back, -1, stay, (1 % stream_count,))
     half_pre = pltpu.VMEM((POPS, 4, width, coarse), jnp.float32)
     half_main = pltpu.VMEM((POPS, 4, width, fine), jnp.float32)
@@ -975,7 +990,7 @@
             f32(*pre_pops.shape),
             f32(*main_pops.shape),
         ),
-        in_specs=[scalars, scalars] + [whole] * 7 + [anywhere],
+        in_specs=[whole] * 9 + [anywhere],
         out_specs=[whole] * 4 + [outside] * 2,
         scratch_shapes=[
             pltpu.VMEM((5, rows, lanes), jnp.float32),
@@ -989,7 +1004,7 @@
         + [pltpu.SemaphoreType.DMA((2, rows - 4))],
         compiler_params=params,
         name="middle_rows",
-    )(tile_map, layer_phase, masks, star_pre, star_main, same, cross, z_same, z_cross, tiles)
+    )(tile_row, phase_row, masks, star_pre, star_main, same, cross, z_same, z_cross, tiles)
     out_pre, out_main, kept_rows = pl.pallas_call(
         last_kernel,
         out_shape=(f32(*pre_pops.shape), f32(*main_pops.shape), f32(5, width, fine)),
@@ -1034,7 +1049,7 @@
     out_main = pl.pallas_call(
         inlet_kernel,
         out_shape=f32(*main_pops.shape),
-        in_specs=[scalars] + [whole] * 4 + [outside],
+        in_specs=[whole] * 5 + [outside],
         out_specs=outside,
         input_output_aliases={5: 0},
         scratch_shapes=[
@@ -1043,7 +1058,7 @@
         ],
         compiler_params=params,
         name="inlet_row",
-    )(layer_phase, masks, awaited, back, kept_rows, out_main)
+    )(phase_row, masks, awaited, back, kept_rows, out_main)
     return out_pre, out_main
 
 

time: 29.9 us -> 28.7 us (0.960)
  Pallas kernels: 9.17 us -> 7.36 us
  waiting for transfers between devices: 0.05 us -> 0.62 us
    pallas_call x1, Pallas kernels: 1.71 us -> 1.02 us  [local(): pl.pallas_call(inlet_kernel, out_shape=f32(*main_pops.shape), in_specs=[w...]
    ppermute x7, waiting for transfers between devices: 0.05 us -> 0.62 us  [send(): return lax.ppermute(value, ('stream', 'span'), moves)]
    pallas_call x1, Pallas kernels: 0.56 us -> 0.01 us  [local(): pl.pallas_call(back_kernel, out_shape=f32(3, 3, width, coarse), in_specs=...]
    pallas_call x1, Pallas kernels: 2.48 us -> 1.93 us  [local(): pl.pallas_call(middle_kernel, out_shape=(f32(POPS, rows - 2, width, coars...]
  transfers between devices with their start and end apart: 7 -> 7, of which waited for: 0 -> 2; matrix products, arithmetic and copies ran while one was open for 0% -> 0% of each run, Pallas kernels for 18% -> 15%
where the time goes in v5:
time: 28.7 us; the launch traced here: 28.5 us
  starting transfers between devices  10.9 us (38%)
  blocking collectives  8.88 us (31%)
  Pallas kernels  7.36 us (26%)
  between operations  0.74 us (3%)
  waiting for transfers between devices  0.62 us (2%)
    ppermute x7, starting transfers between devices, send(): return lax.ppermute(value, ('stream', 'span'), moves)  10.9 us
    all_gather x1, blocking collectives, local(): tiles = lax.all_gather(plane, 'span', axis=0, tiled=False)  8.88 us
    pallas_call x1, Pallas kernels, local(): pl.pallas_call(first_kernel, out_shape=(f32(*pre_pops.shape), f32(*main_p...  2.06 us
    pallas_call x1, Pallas kernels, local(): pl.pallas_call(last_kernel, out_shape=(f32(*pre_pops.shape), f32(*main_po...  1.98 us
    pallas_call x1, Pallas kernels, local(): pl.pallas_call(middle_kernel, out_shape=(f32(POPS, rows - 2, width, coars...  1.93 us
    pallas_call x1, Pallas kernels, local(): pl.pallas_call(inlet_kernel, out_shape=f32(*main_pops.shape), in_specs=[w...  1.02 us
    ppermute x7, waiting for transfers between devices, send(): return lax.ppermute(value, ('stream', 'span'), moves)  0.62 us
  transfers between devices with their start and end apart: 7, of which 2 were waited for; matrix products, arithmetic and copies ran while one was open for 0% of the time, Pallas kernels for 15%

profile of v5, /device:TPU:0, one launch (start us, length us, event | category | flops | bytes accessed | tf_op | source)
XLA Modules:
  0.0 28.5 jit_solution(10362169735613192609)
XLA Ops:
  0.6 0.0 copy-start.2
  0.6 2.1 %collide_and_pack.1 = (f32[19,8,8,128]{3,2,1,0:T(8,128)S(1)}, f32[19,8,8,256]{3,2,1,0:T(8,128)S(1)}, f32[24,8,384]{2,1,0:T(8,128)S(1)}, f32[24,8,384]{2,1,0:T(8,128)S(1)}) custom-call(f32[19,8,8,128]{3,2,1,0:T(8,128)} %pre_hbm.1, f32[19,8,8,256]{3,2,1,0:T(8,128)} %main_hbm.1), custom_call_target="tpu_custom_call" | custom-call | tf_op jit(solution)/shard_map/collide_and_pack/pallas_call | solution.py:924
  2.7 0.5 %collective-permute-start = (f32[24,8,384]{2,1,0:T(8,128)S(1)}, f32[24,8,384]{2,1,0:T(8,128)S(1)}, u32[]{:S(2)}, u32[]{:S(2)}) collective-permute-start(f32[24,8,384]{2,1,0:T(8,128)S(1)} %get-tuple-element.24.edge_same), channel_id=1, source_target_pairs={{0,1},{1,0},{2,3},{3,2},{4,5},{5,4},{6,7},{7,6},{8,9},{9,8},{10,11... | collective-permute-start | bytes 884744 | tf_op jit(solution)/shard_map/ppermute | solution.py:912
  3.2 3.5 %collective-permute-start.1 = (f32[24,8,384]{2,1,0:T(8,128)S(1)}, f32[24,8,384]{2,1,0:T(8,128)S(1)}, u32[]{:S(2)}, u32[]{:S(2)}) collective-permute-start(f32[24,8,384]{2,1,0:T(8,128)S(1)} %get-tuple-element.25.edge_cross), channel_id=1, source_target_pairs={{0,7},{1,2},{2,1},{3,4},{4,3},{5,6},{6,5},{7,0},{8,15},{9,10},{10,... | collective-permute-start | bytes 884744 | tf_op jit(solution)/shard_map/ppermute | solution.py:912
  6.8 0.0 copy-done.2
  6.8 0.0 copy-start.1
  6.8 0.3 %faces.1 = (f32[3,8,384]{2,1,0:T(8,128)S(1)}, f32[14,8,384]{2,1,0:T(8,128)S(1)}, f32[14,8,384]{2,1,0:T(8,128)S(1)}, f32[16,8,128]{2,1,0:T(8,128)S(1)}) custom-call(s32[1,256]{1,0:T(1,128)S(1)} %bitcast.11, f32[19,8,8,128]{3,2,1,0:T(8,128)S(1)} %get-tuple-element.21.star_pre, f32[19,8,8,256]{3,2,1,0:T(8,128)S(1)} %get-tuple-element.22.star_main), custom_call_target="tpu_custom_call" | custom-call | tf_op jit(solution)/shard_map/faces/pallas_call | solution.py:941
  7.1 0.0 copy-start
  7.1 1.6 %collective-permute-start.2 = (f32[14,8,384]{2,1,0:T(8,128)S(1)}, f32[14,8,384]{2,1,0:T(8,128)S(1)}, u32[]{:S(2)}, u32[]{:S(2)}) collective-permute-start(f32[14,8,384]{2,1,0:T(8,128)S(1)} %get-tuple-element.30), channel_id=1, source_target_pairs={{0,8},{1,9},{2,10},{3,11},{4,12},{5,13},{6,14},{7,15},{8,16},{9,17... | collective-permute-start | bytes 516104 | tf_op jit(solution)/shard_map/ppermute | solution.py:912
  8.7 2.3 %collective-permute-start.3 = (f32[14,8,384]{2,1,0:T(8,128)S(1)}, f32[14,8,384]{2,1,0:T(8,128)S(1)}, u32[]{:S(2)}, u32[]{:S(2)}) collective-permute-start(f32[14,8,384]{2,1,0:T(8,128)S(1)} %get-tuple-element.31), channel_id=1, source_target_pairs={{0,24},{1,25},{2,26},{3,27},{4,28},{5,29},{6,30},{7,31},{8,0},{9,1... | collective-permute-start | bytes 516104 | tf_op jit(solution)/shard_map/ppermute | solution.py:912
  11.0 8.9 %all-gather = f32[128,8,128]{2,1,0:T(8,128)S(1)} all-gather(f32[16,8,128]{2,1,0:T(8,128)S(1)} %get-tuple-element.26), channel_id=2, replica_groups=mesh['stream'=4,'span'=8] {'span'}, dimensions={0}, use_global_device_ids=true | all-gather | bytes 589824 | tf_op jit(solution)/shard_map/all_gather | solution.py:957
  19.9 0.0 collective-permute-done.2.x_low
  19.9 0.0 collective-permute-done.3.x_high
  19.9 0.4 %collective-permute-start.4 = (f32[32,384]{1,0:T(8,128)S(1)}, f32[32,384]{1,0:T(8,128)S(1)}, u32[]{:S(2)}, u32[]{:S(2)}) collective-permute-start(f32[32,384]{1,0:T(8,128)S(1)} %get-tuple-element.32), channel_id=1, source_target_pairs={{0,1},{1,0},{2,3},{3,2},{4,5},{5,4},{6,7},{7,6},{8,9},{9,8},{10,11... | collective-permute-start | bytes 147464 | tf_op jit(solution)/shard_map/ppermute | solution.py:912
  20.4 1.2 %collective-permute-start.5 = (f32[32,384]{1,0:T(8,128)S(1)}, f32[32,384]{1,0:T(8,128)S(1)}, u32[]{:S(2)}, u32[]{:S(2)}) collective-permute-start(f32[32,384]{1,0:T(8,128)S(1)} %get-tuple-element.33), channel_id=1, source_target_pairs={{0,7},{1,2},{2,1},{3,4},{4,3},{5,6},{6,5},{7,0},{8,15},{9,10},{10,... | collective-permute-start | bytes 147464 | tf_op jit(solution)/shard_map/ppermute | solution.py:912
  21.6 0.0 copy-done.1
  21.6 1.3 %collective-permute-start.6 = (f32[3,3,8,128]{3,2,1,0:T(8,128)S(1)}, f32[3,3,8,128]{3,2,1,0:T(8,128)S(1)}, u32[]{:S(2)}, u32[]{:S(2)}) collective-permute-start(f32[3,3,8,128]{3,2,1,0:T(8,128)S(1)} %behind_plane.1), channel_id=1, source_target_pairs={{8,0},{9,1},{10,2},{11,3},{12,4},{13,5},{14,6},{15,7}} | collective-permute-start | bytes 110600 | tf_op jit(solution)/shard_map/ppermute | solution.py:912
  22.9 0.0 collective-permute-done.same
  22.9 0.0 collective-permute-done.1.cross
  22.9 0.0 copy-done
  22.9 1.9 %middle_rows.1 = (f32[19,6,8,128]{3,2,1,0:T(8,128)S(1)}, f32[19,6,8,256]{3,2,1,0:T(8,128)S(1)}, f32[3,5,8,256]{3,2,1,0:T(8,128)S(1)}, f32[3,9,8,128]{3,2,1,0:T(8...) custom-call(s32[1,8]{1,0:T(1,128)S(1)} %bitcast.10, s32[1,8]{1,0:T(1,128)S(1)} %bitcast.7, ...), custom_call_target="tpu_custom_call" | custom-call | tf_op jit(solution)/shard_map/middle_rows/pallas_call | solution.py:983
  24.9 0.0 collective-permute-done.4.e_same
  24.9 0.1 collective-permute-done.5.e_cross
  25.0 2.0 %last_rows.1 = (f32[19,8,8,128]{3,2,1,0:T(8,128)}, f32[19,8,8,256]{3,2,1,0:T(8,128)}, f32[5,8,256]{2,1,0:T(8,128)S(1)}) custom-call(f32[3,8,384]{2,1,0:T(8,128)S(1)} %get-tuple-element.23.masks, f32[19,8,8,128]{3,2,1,0:T(8,128)S(1)} %get-tuple-element.21.star_pre, ...), custom_call_target="tpu_custom_call", output_to_operand_aliasing={{0}: (14, {}), {1}: (15, {})} | custom-call | tf_op jit(solution)/shard_map/last_rows/pallas_call | solution.py:1008
  27.0 0.5 %collective-permute-done.6.back = f32[3,3,8,128]{3,2,1,0:T(8,128)S(1)} collective-permute-done((f32[3,3,8,128]{3,2,1,0:T(8,128)S(1)}, f32[3,3,8,128]{3,2,1,0:T(8,128)S(1)}, u32[]{:S(2)}, u32[]{:S(2)}) %collective-permute-start.6) | collective-permute-done | bytes 36896 | tf_op jit(solution)/shard_map/ppermute | solution.py:912
  27.5 1.0 %inlet_row.1 = f32[19,8,8,256]{3,2,1,0:T(8,128)} custom-call(s32[1,8]{1,0:T(1,128)S(1)} %bitcast.8, f32[3,8,384]{2,1,0:T(8,128)S(1)} %get-tuple-element.23.masks, f32[3,9,8,128]{3,2,1,0:T(8,128)S(1)} %get-tuple-element.37.awaited, f32[3,3,8,128]{3,2,1,0:T(8,128)S(1)} %collective-permute-done.6.back, ...), custom_call_target="tpu_custom_call", output_to_operand_aliasing={{}: (5, {})} | custom-call | tf_op jit(solution)/shard_map/inlet_row/pallas_call | solution.py:1049
  (2 shorter events, 0.1 us)
Async XLA Ops:
  0.6 6.2 %copy-start.2 = (s32[256]{0:T(256)S(1)}, s32[256]{0:T(256)}, u32[]{:S(2)}) copy-start(s32[256]{0:T(256)} %param.9) | copy-start | bytes 3076
  2.7 20.2 %collective-permute-start = (f32[24,8,384]{2,1,0:T(8,128)S(1)}, f32[24,8,384]{2,1,0:T(8,128)S(1)}, u32[]{:S(2)}, u32[]{:S(2)}) collective-permute-start(f32[24,8,384]{2,1,0:T(8,128)S(1)} %get-tuple-element.24.edge_same), channel_id=1, source_target_pairs={{0,1},{1,0},{2,3},{3,2},{4,5},{5,4},{6,7},{7,6},{8,9},{9,8},{10,11... | collective-permute-start | bytes 884744 | tf_op jit(solution)/shard_map/ppermute | solution.py:912
  3.2 19.7 %collective-permute-start.1 = (f32[24,8,384]{2,1,0:T(8,128)S(1)}, f32[24,8,384]{2,1,0:T(8,128)S(1)}, u32[]{:S(2)}, u32[]{:S(2)}) collective-permute-start(f32[24,8,384]{2,1,0:T(8,128)S(1)} %get-tuple-element.25.edge_cross), channel_id=1, source_target_pairs={{0,7},{1,2},{2,1},{3,4},{4,3},{5,6},{6,5},{7,0},{8,15},{9,10},{10,... | collective-permute-start | bytes 884744 | tf_op jit(solution)/shard_map/ppermute | solution.py:912
  6.8 14.8 %copy-start.1 = (s32[8]{0:T(128)S(1)}, s32[8]{0:T(128)}, u32[]{:S(2)}) copy-start(s32[8]{0:T(128)} %param.7) | copy-start | bytes 100
  7.1 15.8 %copy-start = (s32[8]{0:T(128)S(1)}, s32[8]{0:T(128)}, u32[]{:S(2)}) copy-start(s32[8]{0:T(128)} %param.8) | copy-start | bytes 100
  7.1 12.8 %collective-permute-start.2 = (f32[14,8,384]{2,1,0:T(8,128)S(1)}, f32[14,8,384]{2,1,0:T(8,128)S(1)}, u32[]{:S(2)}, u32[]{:S(2)}) collective-permute-start(f32[14,8,384]{2,1,0:T(8,128)S(1)} %get-tuple-element.30), channel_id=1, source_target_pairs={{0,8},{1,9},{2,10},{3,11},{4,12},{5,13},{6,14},{7,15},{8,16},{9,17... | collective-permute-start | bytes 516104 | tf_op jit(solution)/shard_map/ppermute | solution.py:912
  8.7 11.2 %collective-permute-start.3 = (f32[14,8,384]{2,1,0:T(8,128)S(1)}, f32[14,8,384]{2,1,0:T(8,128)S(1)}, u32[]{:S(2)}, u32[]{:S(2)}) collective-permute-start(f32[14,8,384]{2,1,0:T(8,128)S(1)} %get-tuple-element.31), channel_id=1, source_target_pairs={{0,24},{1,25},{2,26},{3,27},{4,28},{5,29},{6,30},{7,31},{8,0},{9,1... | collective-permute-start | bytes 516104 | tf_op jit(solution)/shard_map/ppermute | solution.py:912
  19.9 4.9 %collective-permute-start.4 = (f32[32,384]{1,0:T(8,128)S(1)}, f32[32,384]{1,0:T(8,128)S(1)}, u32[]{:S(2)}, u32[]{:S(2)}) collective-permute-start(f32[32,384]{1,0:T(8,128)S(1)} %get-tuple-element.32), channel_id=1, source_target_pairs={{0,1},{1,0},{2,3},{3,2},{4,5},{5,4},{6,7},{7,6},{8,9},{9,8},{10,11... | collective-permute-start | bytes 147464 | tf_op jit(solution)/shard_map/ppermute | solution.py:912
  20.4 4.6 %collective-permute-start.5 = (f32[32,384]{1,0:T(8,128)S(1)}, f32[32,384]{1,0:T(8,128)S(1)}, u32[]{:S(2)}, u32[]{:S(2)}) collective-permute-start(f32[32,384]{1,0:T(8,128)S(1)} %get-tuple-element.33), channel_id=1, source_target_pairs={{0,7},{1,2},{2,1},{3,4},{4,3},{5,6},{6,5},{7,0},{8,15},{9,10},{10,... | collective-permute-start | bytes 147464 | tf_op jit(solution)/shard_map/ppermute | solution.py:912
  21.6 5.9 %collective-permute-start.6 = (f32[3,3,8,128]{3,2,1,0:T(8,128)S(1)}, f32[3,3,8,128]{3,2,1,0:T(8,128)S(1)}, u32[]{:S(2)}, u32[]{:S(2)}) collective-permute-start(f32[3,3,8,128]{3,2,1,0:T(8,128)S(1)} %behind_plane.1), channel_id=1, source_target_pairs={{8,0},{9,1},{10,2},{11,3},{12,4},{13,5},{14,6},{15,7}} | collective-permute-start | bytes 110600 | tf_op jit(solution)/shard_map/ppermute | solution.py:912

commit v6 on v5

--- a/solution.py
+++ b/solution.py
@@ -328,7 +328,7 @@
     return [values[pop] if pop in pops else None for pop in range(POPS)]
 
 
-def corner_kernel(x_low, x_high, tiles, e_same, e_cross):
+def corner_kernel(x_high, x_low, tiles, e_same, e_cross):
     def lines(is_left, target):
         inward = forward_z if is_left else backward_z
         edge, second, first = (7, 6, 4) if is_left else (0, 1, 0)
@@ -450,42 +450,40 @@
     return found
 
 
-def refine(coarse, phases, fine_len):
-    coarse_len = coarse.shape[1]
-    count = coarse.shape[0] // 3
-    rows = lax.broadcasted_iota(jnp.int32, (coarse_len, fine_len), 0)
-    fine = lax.broadcasted_iota(jnp.int32, (coarse_len, fine_len), 1)
-    matrices = []
+def fill_matrices(layer_phase, matrices):
+    shape = matrices.shape[1:]
+    rows = lax.broadcasted_iota(jnp.int32, shape, 0)
+    fine = lax.broadcasted_iota(jnp.int32, shape, 1)
+    choices = []
     for phase in (0, 1):
         position = fine + phase
         lower = lax.shift_right_arithmetic(position - 1, 1)
         upper_wt = jnp.where(position % 2 == 0, 0.75, 0.25)
-        low_idx = jnp.clip(lower, 0, coarse_len - 1)
-        high_idx = jnp.clip(lower + 1, 0, coarse_len - 1)
-        matrix = jnp.where(rows == low_idx, 1.0 - upper_wt, 0.0) + jnp.where(
-            rows == high_idx, upper_wt, 0.0
+        low_idx = jnp.clip(lower, 0, shape[0] - 1)
+        high_idx = jnp.clip(lower + 1, 0, shape[0] - 1)
+        choices.append(
+            jnp.where(rows == low_idx, 1.0 - upper_wt, 0.0)
+            + jnp.where(rows == high_idx, upper_wt, 0.0)
         )
-        matrices.append(matrix.astype(jnp.bfloat16))
-    parts = []
-    rest = coarse
-    for _ in range(3):
-        parts.append(rest.astype(jnp.bfloat16))
-        rest = rest - parts[-1].astype(jnp.float32)
-    outs = []
-    for matrix in matrices:
+    for tile, phase in enumerate(neighbours(layer_phase)):
+        chosen = jnp.where(jnp.broadcast_to(phase, shape) > 0.5, choices[1], choices[0])
+        matrices[tile] = chosen.astype(jnp.bfloat16)
+
+
+def refine(planes, matrices):
+    refined = []
+    for tile, group in enumerate(planes):
+        parts = []
+        rest = jnp.concatenate(group, axis=0)
+        for _ in range(3):
+            parts.append(rest.astype(jnp.bfloat16))
+            rest = rest - parts[-1].astype(jnp.float32)
         total = None
         for part in reversed(parts):
-            product = jnp.dot(part, matrix, preferred_element_type=jnp.float32)
+            product = jnp.dot(part, matrices[tile], preferred_element_type=jnp.float32)
             total = product if total is None else total + product
-        outs.append(total)
-    return [
-        jnp.where(
-            jnp.broadcast_to(phases[tile], (count, fine_len)) > 0.5,
-            outs[1][tile * count : (tile + 1) * count],
-            outs[0][tile * count : (tile + 1) * count],
-        )
-        for tile in range(3)
-    ]
+        refined.append(total.reshape(len(group), group[0].shape[0], total.shape[1]))
+    return refined
 
 
 def lanes_of(coarse, fine):
@@ -508,8 +506,8 @@
     masks,
     star_pre,
     star_main,
+    cross,
     same,
-    cross,
     edge_same,
     edge_cross,
     tiles_hbm,
@@ -517,6 +515,7 @@
     mid_main,
     inflow,
     awaited,
+    matrices,
     out_pre_hbm,
     out_main_hbm,
     ghost_left,
@@ -568,7 +567,8 @@
         ghosts(False, ghost_right, cross, edge_cross, rim_right)
 
     stars = (star_pre, star_main)
-    for x_at in range(1, rows - 1):
+
+    def first_step(x_at):
         for domain, lanes in enumerate(lanes_of(coarse, fine)):
             new = moved_row(
                 lambda pop, at: stars[domain][pop, at],
@@ -582,7 +582,8 @@
                 (mid_pre, mid_main)[domain][pop, x_at - 1] = out[pop]
 
     copies = []
-    for x_at in range(2, rows - 2):
+
+    def second_step(x_at):
         for domain, lanes in enumerate(lanes_of(coarse, fine)):
             new = moved_row(
                 lambda pop, at: (mid_pre, mid_main)[domain][pop, at - 1],
@@ -603,6 +604,11 @@
             )
             copies[-1].start()
 
+    for x_at in range(1, rows - 1):
+        first_step(x_at)
+        if x_at >= 3:
+            second_step(x_at - 1)
+
     @pl.when(on_inlet)
     def _():
         copy.wait()
@@ -611,7 +617,7 @@
         sub = lax.broadcasted_iota(jnp.int32, (width, coarse), 0)
         for place, number in enumerate(neighbours(tile_map)):
             found = tile_at(tiles, number, range(14))
-            planes += found[:5]
+            planes.append(found[:5])
             edges = [None] * POPS
             for pops, offset, row, slot in (
                 (forward_z, -1, 0, 14),
@@ -629,9 +635,9 @@
             for k, pop in enumerate(incoming):
                 new = found[5 + k]
                 awaited[place, 4 + k] = new if edges[pop] is None else new + edges[pop]
-        refined = refine(jnp.concatenate(planes, axis=0), neighbours(layer_phase), fine)
-        for place, value in enumerate(refined):
-            inflow[place] = value.reshape(5, width, fine)
+        fill_matrices(layer_phase, matrices)
+        for place, value in enumerate(refine(planes, matrices)):
+            inflow[place] = value
 
     for copy_out in copies:
         copy_out.wait()
@@ -644,14 +650,14 @@
     mid_pre,
     mid_main,
     inflow,
+    x_high,
     x_low,
-    x_high,
+    cross,
     same,
-    cross,
     edge_same,
     edge_cross,
+    e_cross,
     e_same,
-    e_cross,
     part_pre,
     part_main,
     out_pre_hbm,
@@ -789,7 +795,15 @@
         moment = [moment[0], moment[1] + face[11, :, lanes], moment[2] + face[12, :, lanes]]
         return relax(new, density, moment, moving), moving
 
-    for x_at in outer:
+    def next_of(domain):
+        def base(pop, x_at):
+            if x_at in outer:
+                return (next_pre, next_main)[domain][pop, outer[x_at]]
+            return (mid_pre, mid_main)[domain][pop, x_at - 1]
+
+        return base
+
+    def end_row(x_at):
         for domain, lanes in enumerate((pre_lanes, main_lanes)):
             if 0 <= x_at < rows:
                 new = moved_row(
@@ -805,26 +819,9 @@
             for pop in wanted:
                 (next_pre, next_main)[domain][pop, outer[x_at]] = out[pop]
 
-    for k in range(5):
-        kept_rows[k] = next_main[backward_x[k], 1]
-
-    @pl.when(is_last)
-    def _():
-        for k in range(5):
-            next_main[backward_x[k], 3] = next_main[backward_x[k], 2]
-            for rim in (rim_left, rim_right):
-                rim[k, rows + 1 : rows + 2, main_lanes] = rim[k, rows : rows + 1, main_lanes]
-
-    def next_of(domain):
-        def base(pop, x_at):
-            if x_at in outer:
-                return (next_pre, next_main)[domain][pop, outer[x_at]]
-            return (mid_pre, mid_main)[domain][pop, x_at - 1]
-
-        return base
-
     copies = []
-    for at_end, x_at in enumerate((0, 1, rows - 2, rows - 1)):
+
+    def second_step(at_end, x_at):
         for domain, lanes in enumerate((pre_lanes, main_lanes)):
             new = moved_row(
                 next_of(domain),
@@ -836,18 +833,38 @@
             kept = (out_pre, out_main)[domain]
             for pop in range(POPS):
                 kept[pop, at_end] = new[pop]
-            copy = pltpu.make_async_copy(
-                kept.at[:, at_end],
-                (out_pre_hbm, out_main_hbm)[domain].at[:, x_at],
-                sent.at[domain, at_end],
+            copies.append(
+                pltpu.make_async_copy(
+                    kept.at[:, at_end],
+                    (out_pre_hbm, out_main_hbm)[domain].at[:, x_at],
+                    sent.at[domain, at_end],
+                )
             )
-            copy.start()
-            copies.append(copy)
+            copies[-1].start()
+
+    end_row(0)
+    for k in range(5):
+        kept_rows[k] = next_main[backward_x[k], 1]
+    second_step(0, 1)
+    end_row(-1)
+    second_step(1, 0)
+    end_row(rows - 1)
+    second_step(2, rows - 2)
+    end_row(rows)
+
+    @pl.when(is_last)
+    def _():
+        for k in range(5):
+            next_main[backward_x[k], 3] = next_main[backward_x[k], 2]
+            for rim in (rim_left, rim_right):
+                rim[k, rows + 1 : rows + 2, main_lanes] = rim[k, rows : rows + 1, main_lanes]
+
+    second_step(3, rows - 1)
     for copy in copies:
         copy.wait()
 
 
-def inlet_kernel(layer_phase, masks, awaited, back, kept_rows, main_hbm, out_hbm, ready, sent):
+def inlet_kernel(matrices, masks, awaited, back, kept_rows, main_hbm, out_hbm, ready, sent):
     @pl.when(lax.axis_index("stream") == 0)
     def _():
         width, coarse = awaited.shape[2:]
@@ -864,11 +881,8 @@
             for k, pop in enumerate(incoming):
                 new[pop] = awaited[place, 4 + k]
             out = relax(new, density, moment, incoming)
-            planes += [out[pop] for pop in incoming]
-        before, own, after = (
-            value.reshape(5, width, fine)
-            for value in refine(jnp.concatenate(planes, axis=0), neighbours(layer_phase), fine)
-        )
+            planes.append([out[pop] for pop in incoming])
+        before, own, after = refine(planes, matrices)
 
         def base(pop, x_at):
             return own[incoming.index(pop)] if x_at < 0 else kept_rows[backward_x.index(pop)]
@@ -909,6 +923,13 @@
             for j in range(span_count):
                 target = (s + step_x) % stream_count * span_count + place(j) % span_count
                 moves.append((s * span_count + j, target))
+        return lax.ppermute(value, ("stream", "span"), moves)
+
+    def swap_in_pairs(value):
+        moves = []
+        for s in range(stream_count):
+            other = min(s ^ 1, stream_count - 1)
+            moves += [(s * span_count + j, other * span_count + j) for j in range(span_count)]
         return lax.ppermute(value, ("stream", "span"), moves)
 
     stay = lambda j: j
@@ -966,7 +987,7 @@
         in_specs=[whole] * 2 + [anywhere],
         compiler_params=params,
         name="corners",
-    )(x_low, x_high, tiles)
+    )(x_high, x_low, tiles)
     e_same = send(e_to_same, 0, sibling)
     e_cross = send(e_to_cross, 0, beyond)
     back = pl.pallas_call(
@@ -977,21 +998,22 @@
         compiler_params=params,
         name="behind_plane",
     )(tile_row, masks, tiles)
-    back = send(back, -1, stay, (1 % stream_count,))
+    back = swap_in_pairs(back)
     half_pre = pltpu.VMEM((POPS, 4, width, coarse), jnp.float32)
     half_main = pltpu.VMEM((POPS, 4, width, fine), jnp.float32)
-    mid_pre, mid_main, inflow, awaited, part_pre, part_main = pl.pallas_call(
+    mid_pre, mid_main, inflow, awaited, matrices, part_pre, part_main = pl.pallas_call(
         middle_kernel,
         out_shape=(
             f32(POPS, rows - 2, width, coarse),
             f32(POPS, rows - 2, width, fine),
             f32(3, 5, width, fine),
             f32(3, 9, width, coarse),
+            jax.ShapeDtypeStruct((3, coarse, fine), jnp.bfloat16),
             f32(*pre_pops.shape),
             f32(*main_pops.shape),
         ),
         in_specs=[whole] * 9 + [anywhere],
-        out_specs=[whole] * 4 + [outside] * 2,
+        out_specs=[whole] * 5 + [outside] * 2,
         scratch_shapes=[
             pltpu.VMEM((5, rows, lanes), jnp.float32),
             pltpu.VMEM((5, rows, lanes), jnp.float32),
@@ -1004,7 +1026,7 @@
         + [pltpu.SemaphoreType.DMA((2, rows - 4))],
         compiler_params=params,
         name="middle_rows",
-    )(tile_row, phase_row, masks, star_pre, star_main, same, cross, z_same, z_cross, tiles)
+    )(tile_row, phase_row, masks, star_pre, star_main, cross, same, z_same, z_cross, tiles)
     out_pre, out_main, kept_rows = pl.pallas_call(
         last_kernel,
         out_shape=(f32(*pre_pops.shape), f32(*main_pops.shape), f32(5, width, fine)),
@@ -1035,14 +1057,14 @@
         mid_pre,
         mid_main,
         inflow,
+        x_high,
         x_low,
-        x_high,
+        cross,
         same,
-        cross,
         z_same,
         z_cross,
+        e_cross,
         e_same,
-        e_cross,
         part_pre,
         part_main,
     )
@@ -1058,7 +1080,7 @@
         ],
         compiler_params=params,
         name="inlet_row",
-    )(phase_row, masks, awaited, back, kept_rows, out_main)
+    )(matrices, masks, awaited, back, kept_rows, out_main)
     return out_pre, out_main
 
 

time: 28.7 us -> 27.8 us (0.969)
  starting transfers between devices: 10.9 us -> 9.77 us
  blocking collectives: 8.88 us -> 9.56 us
  waiting for transfers between devices: 0.62 us -> 0.2 us
    ppermute x7 -> x6, starting transfers between devices: 10.9 us -> 8.57 us  [send(): return lax.ppermute(value, ('stream', 'span'), moves)]
    ppermute x0 -> x1, starting transfers between devices: none -> 1.2 us  [swap_in_pairs(): return lax.ppermute(value, ('stream', 'span'), moves)]
    all_gather x1, blocking collectives: 8.88 us -> 9.56 us  [local(): tiles = lax.all_gather(plane, 'span', axis=0, tiled=False)]
    ppermute x7 -> x6, waiting for transfers between devices: 0.62 us -> 0.2 us  [send(): return lax.ppermute(value, ('stream', 'span'), moves)]
  transfers between devices with their start and end apart: 7 -> 7, of which waited for: 2 -> 1; matrix products, arithmetic and copies ran while one was open for 0% -> 0% of each run, Pallas kernels for 15% -> 16%
where the time goes in v6:
time: 27.8 us; the launch traced here: 27.6 us
  starting transfers between devices  9.77 us (35%)
  blocking collectives  9.56 us (34%)
  Pallas kernels  7.33 us (26%)
  between operations  0.71 us (3%)
    all_gather x1, blocking collectives, local(): tiles = lax.all_gather(plane, 'span', axis=0, tiled=False)  9.56 us
    ppermute x6, starting transfers between devices, send(): return lax.ppermute(value, ('stream', 'span'), moves)  8.57 us
    pallas_call x1, Pallas kernels, local(): pl.pallas_call(first_kernel, out_shape=(f32(*pre_pops.shape), f32(*main_p...  2.06 us
    pallas_call x1, Pallas kernels, local(): pl.pallas_call(last_kernel, out_shape=(f32(*pre_pops.shape), f32(*main_po...  2 us
    pallas_call x1, Pallas kernels, local(): pl.pallas_call(middle_kernel, out_shape=(f32(POPS, rows - 2, width, coars...  1.96 us
    ppermute x1, starting transfers between devices, swap_in_pairs(): return lax.ppermute(value, ('stream', 'span'), moves)  1.2 us
    pallas_call x1, Pallas kernels, local(): pl.pallas_call(inlet_kernel, out_shape=f32(*main_pops.shape), in_specs=[w...  0.95 us
  transfers between devices with their start and end apart: 7, of which 1 were waited for; matrix products, arithmetic and copies ran while one was open for 0% of the time, Pallas kernels for 16%

profile of v6, /device:TPU:0, one launch (start us, length us, event | category | flops | bytes accessed | tf_op | source)
XLA Modules:
  0.0 27.6 jit_solution(8610826376476406496)
XLA Ops:
  0.6 0.0 copy-start.1
  0.6 2.1 %collide_and_pack.1 = (f32[19,8,8,128]{3,2,1,0:T(8,128)S(1)}, f32[19,8,8,256]{3,2,1,0:T(8,128)S(1)}, f32[24,8,384]{2,1,0:T(8,128)S(1)}, f32[24,8,384]{2,1,0:T(8,128)S(1)}) custom-call(f32[19,8,8,128]{3,2,1,0:T(8,128)} %pre_hbm.1, f32[19,8,8,256]{3,2,1,0:T(8,128)} %main_hbm.1), custom_call_target="tpu_custom_call" | custom-call | tf_op jit(solution)/shard_map/collide_and_pack/pallas_call | solution.py:945
  2.7 3.4 %collective-permute-start = (f32[24,8,384]{2,1,0:T(8,128)S(1)}, f32[24,8,384]{2,1,0:T(8,128)S(1)}, u32[]{:S(2)}, u32[]{:S(2)}) collective-permute-start(f32[24,8,384]{2,1,0:T(8,128)S(1)} %get-tuple-element.25.edge_cross), channel_id=1, source_target_pairs={{0,7},{1,2},{2,1},{3,4},{4,3},{5,6},{6,5},{7,0},{8,15},{9,10},{10,... | collective-permute-start | bytes 884744 | tf_op jit(solution)/shard_map/ppermute | solution.py:926
  6.1 0.0 collective-permute-start.1
  6.1 0.0 copy-done.1
  6.1 0.0 copy-start
  6.1 0.3 %faces.1 = (f32[3,8,384]{2,1,0:T(8,128)S(1)}, f32[14,8,384]{2,1,0:T(8,128)S(1)}, f32[14,8,384]{2,1,0:T(8,128)S(1)}, f32[16,8,128]{2,1,0:T(8,128)S(1)}) custom-call(s32[1,256]{1,0:T(1,128)S(1)} %bitcast.9, f32[19,8,8,128]{3,2,1,0:T(8,128)S(1)} %get-tuple-element.22.star_pre, f32[19,8,8,256]{3,2,1,0:T(8,128)S(1)} %get-tuple-element.23.star_main), custom_call_target="tpu_custom_call" | custom-call | tf_op jit(solution)/shard_map/faces/pallas_call | solution.py:962
  6.4 0.0 copy-start.2
  6.5 3.7 %collective-permute-start.2 = (f32[14,8,384]{2,1,0:T(8,128)S(1)}, f32[14,8,384]{2,1,0:T(8,128)S(1)}, u32[]{:S(2)}, u32[]{:S(2)}) collective-permute-start(f32[14,8,384]{2,1,0:T(8,128)S(1)} %get-tuple-element.31), channel_id=1, source_target_pairs={{0,24},{1,25},{2,26},{3,27},{4,28},{5,29},{6,30},{7,31},{8,0},{9,1... | collective-permute-start | bytes 516104 | tf_op jit(solution)/shard_map/ppermute | solution.py:926
  10.1 0.0 collective-permute-start.3
  10.1 9.6 %all-gather = f32[128,8,128]{2,1,0:T(8,128)S(1)} all-gather(f32[16,8,128]{2,1,0:T(8,128)S(1)} %get-tuple-element.27), channel_id=2, replica_groups=mesh['stream'=4,'span'=8] {'span'}, dimensions={0}, use_global_device_ids=true | all-gather | bytes 589824 | tf_op jit(solution)/shard_map/all_gather | solution.py:978
  19.7 0.0 collective-permute-done.2.x_high
  19.7 0.0 collective-permute-done.3.x_low
  19.7 1.5 %collective-permute-start.4 = (f32[32,384]{1,0:T(8,128)S(1)}, f32[32,384]{1,0:T(8,128)S(1)}, u32[]{:S(2)}, u32[]{:S(2)}) collective-permute-start(f32[32,384]{1,0:T(8,128)S(1)} %get-tuple-element.33), channel_id=1, source_target_pairs={{0,7},{1,2},{2,1},{3,4},{4,3},{5,6},{6,5},{7,0},{8,15},{9,10},{10,... | collective-permute-start | bytes 147464 | tf_op jit(solution)/shard_map/ppermute | solution.py:926
  21.2 0.0 collective-permute-start.5
  21.2 0.0 copy-done
  21.3 1.2 %collective-permute-start.6 = (f32[3,3,8,128]{3,2,1,0:T(8,128)S(1)}, f32[3,3,8,128]{3,2,1,0:T(8,128)S(1)}, u32[]{:S(2)}, u32[]{:S(2)}) collective-permute-start(f32[3,3,8,128]{3,2,1,0:T(8,128)S(1)} %behind_plane.1), channel_id=1, source_target_pairs={{0,8},{1,9},{2,10},{3,11},{4,12},{5,13},{6,14},{7,15},{8,0},{9,1},... | collective-permute-start | bytes 110600 | tf_op jit(solution)/shard_map/ppermute | solution.py:933
  22.5 0.0 collective-permute-done.cross
  22.5 0.0 collective-permute-done.1.same
  22.5 0.0 copy-done.2
  22.5 2.0 %middle_rows.1 = (f32[19,6,8,128]{3,2,1,0:T(8,128)S(1)}, f32[19,6,8,256]{3,2,1,0:T(8,128)S(1)}, f32[3,5,8,256]{3,2,1,0:T(8,128)S(1)}, f32[3,9,8,128]{3,2,1,0:T(8...) custom-call(s32[1,8]{1,0:T(1,128)S(1)} %bitcast.8, ...), custom_call_target="tpu_custom_call" | custom-call | tf_op jit(solution)/shard_map/middle_rows/pallas_call | solution.py:1004
  24.4 0.2 collective-permute-done.4.e_cross
  24.6 0.0 collective-permute-done.5.e_same
  24.6 2.0 %last_rows.1 = (f32[19,8,8,128]{3,2,1,0:T(8,128)}, f32[19,8,8,256]{3,2,1,0:T(8,128)}, f32[5,8,256]{2,1,0:T(8,128)S(1)}) custom-call(f32[3,8,384]{2,1,0:T(8,128)S(1)} %get-tuple-element.24.masks, f32[19,8,8,128]{3,2,1,0:T(8,128)S(1)} %get-tuple-element.22.star_pre, ...), custom_call_target="tpu_custom_call", output_to_operand_aliasing={{0}: (14, {}), {1}: (15, {})} | custom-call | tf_op jit(solution)/shard_map/last_rows/pallas_call | solution.py:1030
  26.6 0.0 collective-permute-done.6.back
  26.6 0.9 %inlet_row.1 = f32[19,8,8,256]{3,2,1,0:T(8,128)} custom-call(bf16[3,128,256]{2,1,0:T(8,128)(2,1)S(1)} %get-tuple-element.38.matrices, f32[3,8,384]{2,1,0:T(8,128)S(1)} %get-tuple-element.24.masks, f32[3,9,8,128]{3,2,1,0:T(8,128)S(1)} %get-tuple-element.39.awaited, f32[3,3,8,128]{3,2,1,0:T(8,128)S(1)} %collective-permute-done.6.back, ...), custom_call_target="tpu_custom_call", output_to_operand_aliasing={{}: (5, {})} | custom-call | tf_op jit(solution)/shard_map/inlet_row/pallas_call | solution.py:1071
  (2 shorter events, 0.1 us)
Async XLA Ops:
  0.6 5.5 %copy-start.1 = (s32[256]{0:T(256)S(1)}, s32[256]{0:T(256)}, u32[]{:S(2)}) copy-start(s32[256]{0:T(256)} %param.9) | copy-start | bytes 3076
  2.7 19.8 %collective-permute-start = (f32[24,8,384]{2,1,0:T(8,128)S(1)}, f32[24,8,384]{2,1,0:T(8,128)S(1)}, u32[]{:S(2)}, u32[]{:S(2)}) collective-permute-start(f32[24,8,384]{2,1,0:T(8,128)S(1)} %get-tuple-element.25.edge_cross), channel_id=1, source_target_pairs={{0,7},{1,2},{2,1},{3,4},{4,3},{5,6},{6,5},{7,0},{8,15},{9,10},{10,... | collective-permute-start | bytes 884744 | tf_op jit(solution)/shard_map/ppermute | solution.py:926
  6.1 16.3 %collective-permute-start.1 = (f32[24,8,384]{2,1,0:T(8,128)S(1)}, f32[24,8,384]{2,1,0:T(8,128)S(1)}, u32[]{:S(2)}, u32[]{:S(2)}) collective-permute-start(f32[24,8,384]{2,1,0:T(8,128)S(1)} %get-tuple-element.26.edge_same), channel_id=1, source_target_pairs={{0,1},{1,0},{2,3},{3,2},{4,5},{5,4},{6,7},{7,6},{8,9},{9,8},{10,11... | collective-permute-start | bytes 884744 | tf_op jit(solution)/shard_map/ppermute | solution.py:926
  6.1 15.1 %copy-start = (s32[8]{0:T(128)S(1)}, s32[8]{0:T(128)}, u32[]{:S(2)}) copy-start(s32[8]{0:T(128)} %param.7) | copy-start | bytes 100
  6.4 16.0 %copy-start.2 = (s32[8]{0:T(128)S(1)}, s32[8]{0:T(128)}, u32[]{:S(2)}) copy-start(s32[8]{0:T(128)} %param.8) | copy-start | bytes 100
  6.5 13.2 %collective-permute-start.2 = (f32[14,8,384]{2,1,0:T(8,128)S(1)}, f32[14,8,384]{2,1,0:T(8,128)S(1)}, u32[]{:S(2)}, u32[]{:S(2)}) collective-permute-start(f32[14,8,384]{2,1,0:T(8,128)S(1)} %get-tuple-element.31), channel_id=1, source_target_pairs={{0,24},{1,25},{2,26},{3,27},{4,28},{5,29},{6,30},{7,31},{8,0},{9,1... | collective-permute-start | bytes 516104 | tf_op jit(solution)/shard_map/ppermute | solution.py:926
  10.1 9.6 %collective-permute-start.3 = (f32[14,8,384]{2,1,0:T(8,128)S(1)}, f32[14,8,384]{2,1,0:T(8,128)S(1)}, u32[]{:S(2)}, u32[]{:S(2)}) collective-permute-start(f32[14,8,384]{2,1,0:T(8,128)S(1)} %get-tuple-element.32), channel_id=1, source_target_pairs={{0,8},{1,9},{2,10},{3,11},{4,12},{5,13},{6,14},{7,15},{8,16},{9,17... | collective-permute-start | bytes 516104 | tf_op jit(solution)/shard_map/ppermute | solution.py:926
  19.7 4.9 %collective-permute-start.4 = (f32[32,384]{1,0:T(8,128)S(1)}, f32[32,384]{1,0:T(8,128)S(1)}, u32[]{:S(2)}, u32[]{:S(2)}) collective-permute-start(f32[32,384]{1,0:T(8,128)S(1)} %get-tuple-element.33), channel_id=1, source_target_pairs={{0,7},{1,2},{2,1},{3,4},{4,3},{5,6},{6,5},{7,0},{8,15},{9,10},{10,... | collective-permute-start | bytes 147464 | tf_op jit(solution)/shard_map/ppermute | solution.py:926
  21.2 3.4 %collective-permute-start.5 = (f32[32,384]{1,0:T(8,128)S(1)}, f32[32,384]{1,0:T(8,128)S(1)}, u32[]{:S(2)}, u32[]{:S(2)}) collective-permute-start(f32[32,384]{1,0:T(8,128)S(1)} %get-tuple-element.34), channel_id=1, source_target_pairs={{0,1},{1,0},{2,3},{3,2},{4,5},{5,4},{6,7},{7,6},{8,9},{9,8},{10,11... | collective-permute-start | bytes 147464 | tf_op jit(solution)/shard_map/ppermute | solution.py:926
  21.3 5.4 %collective-permute-start.6 = (f32[3,3,8,128]{3,2,1,0:T(8,128)S(1)}, f32[3,3,8,128]{3,2,1,0:T(8,128)S(1)}, u32[]{:S(2)}, u32[]{:S(2)}) collective-permute-start(f32[3,3,8,128]{3,2,1,0:T(8,128)S(1)} %behind_plane.1), channel_id=1, source_target_pairs={{0,8},{1,9},{2,10},{3,11},{4,12},{5,13},{6,14},{7,15},{8,0},{9,1},... | collective-permute-start | bytes 110600 | tf_op jit(solution)/shard_map/ppermute | solution.py:933

commit v7 on v6

--- a/solution.py
+++ b/solution.py
@@ -382,9 +382,12 @@
                 edges[pop] = jnp.where((sub == row) & open_layers, line, 0.0)
             density, moment = moments_of(edges)
             sums = tile_at(tiles, number, (0, 2, 3))
-            back[at, 0] = sums[0] + density
-            back[at, 1] = sums[1]
-            back[at, 2] = sums[2] + moment[2]
+            for k, value in enumerate((sums[0] + density, sums[1], sums[2] + moment[2])):
+                if at == 1:
+                    back[k] = value
+                else:
+                    line, edge = (k, width - 1) if at == 0 else (3 + k, 0)
+                    back[3, line : line + 1, :] = value[edge : edge + 1]
 
 
 def build_columns(is_left, col, corner, halo, edge, lines, x_low, x_high, masks):
@@ -658,11 +661,13 @@
     edge_cross,
     e_cross,
     e_same,
+    awaited,
+    back,
+    matrices,
     part_pre,
     part_main,
     out_pre_hbm,
     out_main_hbm,
-    kept_rows,
     col_left,
     col_right,
     corner_left,
@@ -842,12 +847,6 @@
             )
             copies[-1].start()
 
-    end_row(0)
-    for k in range(5):
-        kept_rows[k] = next_main[backward_x[k], 1]
-    second_step(0, 1)
-    end_row(-1)
-    second_step(1, 0)
     end_row(rows - 1)
     second_step(2, rows - 2)
     end_row(rows)
@@ -860,22 +859,21 @@
                 rim[k, rows + 1 : rows + 2, main_lanes] = rim[k, rows : rows + 1, main_lanes]
 
     second_step(3, rows - 1)
-    for copy in copies:
-        copy.wait()
-
-
-def inlet_kernel(matrices, masks, awaited, back, kept_rows, main_hbm, out_hbm, ready, sent):
-    @pl.when(lax.axis_index("stream") == 0)
-    def _():
-        width, coarse = awaited.shape[2:]
-        fine = masks.shape[2] - coarse
+    end_row(0)
+    second_step(0, 1)
+    end_row(-1)
+
+    @pl.when(is_first)
+    def _():
         planes = []
         for place in range(3):
-            density = awaited[place, 0] + back[place, 0]
+            first = 0 if place == 0 else 3
+            rest = [back[k] if place == 1 else back[3, first + k : first + k + 1, :] for k in range(3)]
+            density = awaited[place, 0] + rest[0]
             moment = [
-                awaited[place, 1] - back[place, 0],
-                awaited[place, 2] + back[place, 1],
-                awaited[place, 3] + back[place, 2],
+                awaited[place, 1] - rest[0],
+                awaited[place, 2] + rest[1],
+                awaited[place, 3] + rest[2],
             ]
             new = [None] * POPS
             for k, pop in enumerate(incoming):
@@ -883,25 +881,14 @@
             out = relax(new, density, moment, incoming)
             planes.append([out[pop] for pop in incoming])
         before, own, after = refine(planes, matrices)
-
-        def base(pop, x_at):
-            return own[incoming.index(pop)] if x_at < 0 else kept_rows[backward_x.index(pop)]
-
-        new = moved_row(
-            base,
-            lambda pop, x_at: before[incoming.index(pop), width - 1 : width],
-            lambda pop, x_at: after[incoming.index(pop), 0:1],
-            masks_of(masks, slice(coarse, coarse + fine)),
-            0,
-            incoming,
-        )
-        copies = []
-        for k, pop in enumerate(incoming):
-            ready[k] = new[pop]
-            copies.append(pltpu.make_async_copy(ready.at[k], out_hbm.at[pop, 0], sent.at[k]))
-            copies[-1].start()
-        for copy in copies:
-            copy.wait()
+        for k in range(5):
+            next_main[incoming[k], 0] = own[k]
+        rim_left[1, 0:1, main_lanes] = before[3, width - 1 : width]
+        rim_right[2, 0:1, main_lanes] = after[4, 0:1]
+
+    second_step(1, 0)
+    for copy in copies:
+        copy.wait()
 
 
 def f32(*shape):
@@ -992,7 +979,7 @@
     e_cross = send(e_to_cross, 0, beyond)
     back = pl.pallas_call(
         back_kernel,
-        out_shape=f32(3, 3, width, coarse),
+        out_shape=f32(4, width, coarse),
         in_specs=[whole, whole, anywhere],
         scratch_shapes=all_tiles,
         compiler_params=params,
@@ -1027,12 +1014,12 @@
         compiler_params=params,
         name="middle_rows",
     )(tile_row, phase_row, masks, star_pre, star_main, cross, same, z_same, z_cross, tiles)
-    out_pre, out_main, kept_rows = pl.pallas_call(
+    return pl.pallas_call(
         last_kernel,
-        out_shape=(f32(*pre_pops.shape), f32(*main_pops.shape), f32(5, width, fine)),
-        in_specs=[whole] * 14 + [outside] * 2,
-        out_specs=(outside, outside, whole),
-        input_output_aliases={14: 0, 15: 1},
+        out_shape=(f32(*pre_pops.shape), f32(*main_pops.shape)),
+        in_specs=[whole] * 17 + [outside] * 2,
+        out_specs=(outside, outside),
+        input_output_aliases={17: 0, 18: 1},
         scratch_shapes=[
             pltpu.VMEM((KEPT + 5, 24, lanes), jnp.float32),
             pltpu.VMEM((KEPT + 5, 24, lanes), jnp.float32),
@@ -1065,23 +1052,12 @@
         z_cross,
         e_cross,
         e_same,
+        awaited,
+        back,
+        matrices,
         part_pre,
         part_main,
     )
-    out_main = pl.pallas_call(
-        inlet_kernel,
-        out_shape=f32(*main_pops.shape),
-        in_specs=[whole] * 5 + [outside],
-        out_specs=outside,
-        input_output_aliases={5: 0},
-        scratch_shapes=[
-            pltpu.VMEM((5, width, fine), jnp.float32),
-            pltpu.SemaphoreType.DMA((5,)),
-        ],
-        compiler_params=params,
-        name="inlet_row",
-    )(matrices, masks, awaited, back, kept_rows, out_main)
-    return out_pre, out_main
 
 
 def solution(mesh):

time: 27.8 us -> 27.5 us (0.989)
  Pallas kernels: 7.33 us -> 6.58 us
  waiting for transfers between devices: 0.2 us -> 0.66 us
    pallas_call x2 -> x1, Pallas kernels: 0.96 us -> 0.01 us  [local(): pl.pallas_call(back_kernel, out_shape=f32(4, width, coarse), in_specs=[wh...]
    ppermute x1, waiting for transfers between devices: 0.01 us -> 0.64 us  [swap_in_pairs(): return lax.ppermute(value, ('stream', 'span'), moves)]
  transfers between devices with their start and end apart: 7 -> 7, of which waited for: 1 -> 1; matrix products, arithmetic and copies ran while one was open for 0% -> 0% of each run, Pallas kernels for 16% -> 8%
where the time goes in v7:
time: 27.5 us; the launch traced here: 27.3 us
  starting transfers between devices  9.77 us (36%)
  blocking collectives  9.56 us (35%)
  Pallas kernels  6.58 us (24%)
  between operations  0.7 us (3%)
  waiting for transfers between devices  0.66 us (2%)
    all_gather x1, blocking collectives, local(): tiles = lax.all_gather(plane, 'span', axis=0, tiled=False)  9.56 us
    ppermute x6, starting transfers between devices, send(): return lax.ppermute(value, ('stream', 'span'), moves)  8.57 us
    pallas_call x1, Pallas kernels, local(): pl.pallas_call(last_kernel, out_shape=(f32(*pre_pops.shape), f32(*main_po...  2.21 us
    pallas_call x1, Pallas kernels, local(): pl.pallas_call(first_kernel, out_shape=(f32(*pre_pops.shape), f32(*main_p...  2.06 us
    pallas_call x1, Pallas kernels, local(): pl.pallas_call(middle_kernel, out_shape=(f32(POPS, rows - 2, width, coars...  1.94 us
    ppermute x1, starting transfers between devices, swap_in_pairs(): return lax.ppermute(value, ('stream', 'span'), moves)  1.2 us
    ppermute x1, waiting for transfers between devices, swap_in_pairs(): return lax.ppermute(value, ('stream', 'span'), moves)  0.64 us
  transfers between devices with their start and end apart: 7, of which 1 were waited for; matrix products, arithmetic and copies ran while one was open for 0% of the time, Pallas kernels for 8%

profile of v7, /device:TPU:0, one launch (start us, length us, event | category | flops | bytes accessed | tf_op | source)
XLA Modules:
  0.0 27.3 jit_solution(18043071722161117962)
XLA Ops:
  0.6 0.0 copy-start.1
  0.6 2.1 %collide_and_pack.1 = (f32[19,8,8,128]{3,2,1,0:T(8,128)S(1)}, f32[19,8,8,256]{3,2,1,0:T(8,128)S(1)}, f32[24,8,384]{2,1,0:T(8,128)S(1)}, f32[24,8,384]{2,1,0:T(8,128)S(1)}) custom-call(f32[19,8,8,128]{3,2,1,0:T(8,128)} %pre_hbm.1, f32[19,8,8,256]{3,2,1,0:T(8,128)} %main_hbm.1), custom_call_target="tpu_custom_call" | custom-call | tf_op jit(solution)/shard_map/collide_and_pack/pallas_call | solution.py:932
  2.7 3.4 %collective-permute-start = (f32[24,8,384]{2,1,0:T(8,128)S(1)}, f32[24,8,384]{2,1,0:T(8,128)S(1)}, u32[]{:S(2)}, u32[]{:S(2)}) collective-permute-start(f32[24,8,384]{2,1,0:T(8,128)S(1)} %get-tuple-element.22.edge_cross), channel_id=1, source_target_pairs={{0,7},{1,2},{2,1},{3,4},{4,3},{5,6},{6,5},{7,0},{8,15},{9,10},{10,... | collective-permute-start | bytes 884744 | tf_op jit(solution)/shard_map/ppermute | solution.py:913
  6.1 0.0 collective-permute-start.1
  6.1 0.0 copy-done.1
  6.1 0.0 copy-start
  6.1 0.3 %faces.1 = (f32[3,8,384]{2,1,0:T(8,128)S(1)}, f32[14,8,384]{2,1,0:T(8,128)S(1)}, f32[14,8,384]{2,1,0:T(8,128)S(1)}, f32[16,8,128]{2,1,0:T(8,128)S(1)}) custom-call(s32[1,256]{1,0:T(1,128)S(1)} %bitcast.9, f32[19,8,8,128]{3,2,1,0:T(8,128)S(1)} %get-tuple-element.19.star_pre, f32[19,8,8,256]{3,2,1,0:T(8,128)S(1)} %get-tuple-element.20.star_main), custom_call_target="tpu_custom_call" | custom-call | tf_op jit(solution)/shard_map/faces/pallas_call | solution.py:949
  6.4 0.0 copy-start.2
  6.4 3.7 %collective-permute-start.2 = (f32[14,8,384]{2,1,0:T(8,128)S(1)}, f32[14,8,384]{2,1,0:T(8,128)S(1)}, u32[]{:S(2)}, u32[]{:S(2)}) collective-permute-start(f32[14,8,384]{2,1,0:T(8,128)S(1)} %get-tuple-element.28), channel_id=1, source_target_pairs={{0,24},{1,25},{2,26},{3,27},{4,28},{5,29},{6,30},{7,31},{8,0},{9,1... | collective-permute-start | bytes 516104 | tf_op jit(solution)/shard_map/ppermute | solution.py:913
  10.1 0.0 collective-permute-start.3
  10.1 9.6 %all-gather = f32[128,8,128]{2,1,0:T(8,128)S(1)} all-gather(f32[16,8,128]{2,1,0:T(8,128)S(1)} %get-tuple-element.24), channel_id=2, replica_groups=mesh['stream'=4,'span'=8] {'span'}, dimensions={0}, use_global_device_ids=true | all-gather | bytes 589824 | tf_op jit(solution)/shard_map/all_gather | solution.py:965
  19.7 0.0 collective-permute-done.2.x_high
  19.7 0.0 collective-permute-done.3.x_low
  19.7 1.5 %collective-permute-start.4 = (f32[32,384]{1,0:T(8,128)S(1)}, f32[32,384]{1,0:T(8,128)S(1)}, u32[]{:S(2)}, u32[]{:S(2)}) collective-permute-start(f32[32,384]{1,0:T(8,128)S(1)} %get-tuple-element.30), channel_id=1, source_target_pairs={{0,7},{1,2},{2,1},{3,4},{4,3},{5,6},{6,5},{7,0},{8,15},{9,10},{10,... | collective-permute-start | bytes 147464 | tf_op jit(solution)/shard_map/ppermute | solution.py:913
  21.2 0.0 collective-permute-start.5
  21.2 0.0 copy-done
  21.3 1.2 %collective-permute-start.6 = (f32[4,8,128]{2,1,0:T(8,128)S(1)}, f32[4,8,128]{2,1,0:T(8,128)S(1)}, u32[]{:S(2)}, u32[]{:S(2)}) collective-permute-start(f32[4,8,128]{2,1,0:T(8,128)S(1)} %behind_plane.1), channel_id=1, source_target_pairs={{0,8},{1,9},{2,10},{3,11},{4,12},{5,13},{6,14},{7,15},{8,0},{9,1},... | collective-permute-start | bytes 49160 | tf_op jit(solution)/shard_map/ppermute | solution.py:920
  22.5 0.0 collective-permute-done.cross
  22.5 0.0 collective-permute-done.1.same
  22.5 0.0 copy-done.2
  22.5 1.9 %middle_rows.1 = (f32[19,6,8,128]{3,2,1,0:T(8,128)S(1)}, f32[19,6,8,256]{3,2,1,0:T(8,128)S(1)}, f32[3,5,8,256]{3,2,1,0:T(8,128)S(1)}, f32[3,9,8,128]{3,2,1,0:T(8...) custom-call(s32[1,8]{1,0:T(1,128)S(1)} %bitcast.8, ...), custom_call_target="tpu_custom_call" | custom-call | tf_op jit(solution)/shard_map/middle_rows/pallas_call | solution.py:991
  24.4 0.6 %collective-permute-done.6.back = f32[4,8,128]{2,1,0:T(8,128)S(1)} collective-permute-done((f32[4,8,128]{2,1,0:T(8,128)S(1)}, f32[4,8,128]{2,1,0:T(8,128)S(1)}, u32[]{:S(2)}, u32[]{:S(2)}) %collective-permute-start.6) | collective-permute-done | bytes 16416 | tf_op jit(solution)/shard_map/ppermute | solution.py:920
  25.1 0.0 collective-permute-done.4.e_cross
  25.1 0.0 collective-permute-done.5.e_same
  25.1 2.2 %last_rows.1 = (f32[19,8,8,128]{3,2,1,0:T(8,128)}, f32[19,8,8,256]{3,2,1,0:T(8,128)}) custom-call(f32[3,8,384]{2,1,0:T(8,128)S(1)} %get-tuple-element.21.masks, f32[19,8,8,128]{3,2,1,0:T(8,128)S(1)} %get-tuple-element.19.star_pre, f32[19,8,8,256]{3,2,1,0:T(8,128)S(1)} %get-tuple-element.20.star_main, ...), custom_call_target="tpu_custom_call", output_to_operand_aliasing={{0}: (17, {}), {1}: (18, {})} | custom-call | tf_op jit(solution)/shard_map/last_rows/pallas_call | solution.py:1017
  (2 shorter events, 0.1 us)
Async XLA Ops:
  0.6 5.5 %copy-start.1 = (s32[256]{0:T(256)S(1)}, s32[256]{0:T(256)}, u32[]{:S(2)}) copy-start(s32[256]{0:T(256)} %param.9) | copy-start | bytes 3076
  2.7 19.8 %collective-permute-start = (f32[24,8,384]{2,1,0:T(8,128)S(1)}, f32[24,8,384]{2,1,0:T(8,128)S(1)}, u32[]{:S(2)}, u32[]{:S(2)}) collective-permute-start(f32[24,8,384]{2,1,0:T(8,128)S(1)} %get-tuple-element.22.edge_cross), channel_id=1, source_target_pairs={{0,7},{1,2},{2,1},{3,4},{4,3},{5,6},{6,5},{7,0},{8,15},{9,10},{10,... | collective-permute-start | bytes 884744 | tf_op jit(solution)/shard_map/ppermute | solution.py:913
  6.1 16.3 %collective-permute-start.1 = (f32[24,8,384]{2,1,0:T(8,128)S(1)}, f32[24,8,384]{2,1,0:T(8,128)S(1)}, u32[]{:S(2)}, u32[]{:S(2)}) collective-permute-start(f32[24,8,384]{2,1,0:T(8,128)S(1)} %get-tuple-element.23.edge_same), channel_id=1, source_target_pairs={{0,1},{1,0},{2,3},{3,2},{4,5},{5,4},{6,7},{7,6},{8,9},{9,8},{10,11... | collective-permute-start | bytes 884744 | tf_op jit(solution)/shard_map/ppermute | solution.py:913
  6.1 15.1 %copy-start = (s32[8]{0:T(128)S(1)}, s32[8]{0:T(128)}, u32[]{:S(2)}) copy-start(s32[8]{0:T(128)} %param.7) | copy-start | bytes 100
  6.4 16.0 %copy-start.2 = (s32[8]{0:T(128)S(1)}, s32[8]{0:T(128)}, u32[]{:S(2)}) copy-start(s32[8]{0:T(128)} %param.8) | copy-start | bytes 100
  6.4 13.2 %collective-permute-start.2 = (f32[14,8,384]{2,1,0:T(8,128)S(1)}, f32[14,8,384]{2,1,0:T(8,128)S(1)}, u32[]{:S(2)}, u32[]{:S(2)}) collective-permute-start(f32[14,8,384]{2,1,0:T(8,128)S(1)} %get-tuple-element.28), channel_id=1, source_target_pairs={{0,24},{1,25},{2,26},{3,27},{4,28},{5,29},{6,30},{7,31},{8,0},{9,1... | collective-permute-start | bytes 516104 | tf_op jit(solution)/shard_map/ppermute | solution.py:913
  10.1 9.6 %collective-permute-start.3 = (f32[14,8,384]{2,1,0:T(8,128)S(1)}, f32[14,8,384]{2,1,0:T(8,128)S(1)}, u32[]{:S(2)}, u32[]{:S(2)}) collective-permute-start(f32[14,8,384]{2,1,0:T(8,128)S(1)} %get-tuple-element.29), channel_id=1, source_target_pairs={{0,8},{1,9},{2,10},{3,11},{4,12},{5,13},{6,14},{7,15},{8,16},{9,17... | collective-permute-start | bytes 516104 | tf_op jit(solution)/shard_map/ppermute | solution.py:913
  19.7 5.3 %collective-permute-start.4 = (f32[32,384]{1,0:T(8,128)S(1)}, f32[32,384]{1,0:T(8,128)S(1)}, u32[]{:S(2)}, u32[]{:S(2)}) collective-permute-start(f32[32,384]{1,0:T(8,128)S(1)} %get-tuple-element.30), channel_id=1, source_target_pairs={{0,7},{1,2},{2,1},{3,4},{4,3},{5,6},{6,5},{7,0},{8,15},{9,10},{10,... | collective-permute-start | bytes 147464 | tf_op jit(solution)/shard_map/ppermute | solution.py:913
  21.2 3.8 %collective-permute-start.5 = (f32[32,384]{1,0:T(8,128)S(1)}, f32[32,384]{1,0:T(8,128)S(1)}, u32[]{:S(2)}, u32[]{:S(2)}) collective-permute-start(f32[32,384]{1,0:T(8,128)S(1)} %get-tuple-element.31), channel_id=1, source_target_pairs={{0,1},{1,0},{2,3},{3,2},{4,5},{5,4},{6,7},{7,6},{8,9},{9,8},{10,11... | collective-permute-start | bytes 147464 | tf_op jit(solution)/shard_map/ppermute | solution.py:913
  21.3 3.8 %collective-permute-start.6 = (f32[4,8,128]{2,1,0:T(8,128)S(1)}, f32[4,8,128]{2,1,0:T(8,128)S(1)}, u32[]{:S(2)}, u32[]{:S(2)}) collective-permute-start(f32[4,8,128]{2,1,0:T(8,128)S(1)} %behind_plane.1), channel_id=1, source_target_pairs={{0,8},{1,9},{2,10},{3,11},{4,12},{5,13},{6,14},{7,15},{8,0},{9,1},... | collective-permute-start | bytes 49160 | tf_op jit(solution)/shard_map/ppermute | solution.py:920

commit v8 on v7

--- a/solution.py
+++ b/solution.py
@@ -598,14 +598,15 @@
             kept = (out_pre, out_main)[domain]
             for pop in range(POPS):
                 kept[pop, x_at - 2] = new[pop]
-            copies.append(
-                pltpu.make_async_copy(
-                    kept.at[:, x_at - 2],
-                    (out_pre_hbm, out_main_hbm)[domain].at[:, x_at],
-                    sent.at[domain, x_at - 2],
+            if x_at % 2 == 1:
+                copies.append(
+                    pltpu.make_async_copy(
+                        kept.at[:, x_at - 3 : x_at - 1],
+                        (out_pre_hbm, out_main_hbm)[domain].at[:, x_at - 1 : x_at + 1],
+                        sent.at[domain, x_at - 2],
+                    )
                 )
-            )
-            copies[-1].start()
+                copies[-1].start()
 
     for x_at in range(1, rows - 1):
         first_step(x_at)
@@ -838,14 +839,16 @@
             kept = (out_pre, out_main)[domain]
             for pop in range(POPS):
                 kept[pop, at_end] = new[pop]
-            copies.append(
-                pltpu.make_async_copy(
-                    kept.at[:, at_end],
-                    (out_pre_hbm, out_main_hbm)[domain].at[:, x_at],
-                    sent.at[domain, at_end],
+            if at_end % 2 == 1:
+                first = x_at - x_at % 2
+                copies.append(
+                    pltpu.make_async_copy(
+                        kept.at[:, at_end - 1 : at_end + 1],
+                        (out_pre_hbm, out_main_hbm)[domain].at[:, first : first + 2],
+                        sent.at[domain, at_end],
+                    )
                 )
-            )
-            copies[-1].start()
+                copies[-1].start()
 
     end_row(rows - 1)
     second_step(2, rows - 2)
@@ -860,7 +863,6 @@
 
     second_step(3, rows - 1)
     end_row(0)
-    second_step(0, 1)
     end_row(-1)
 
     @pl.when(is_first)
@@ -886,7 +888,8 @@
         rim_left[1, 0:1, main_lanes] = before[3, width - 1 : width]
         rim_right[2, 0:1, main_lanes] = after[4, 0:1]
 
-    second_step(1, 0)
+    second_step(0, 0)
+    second_step(1, 1)
     for copy in copies:
         copy.wait()
 

time: 27.5 us -> 27.5 us (level)
  transfers between devices with their start and end apart: 7 -> 7, of which waited for: 1 -> 1; matrix products, arithmetic and copies ran while one was open for 0% -> 0% of each run, Pallas kernels for 8% -> 9%
where the time goes in v8:
time: 27.5 us; the launch traced here: 27.3 us
  starting transfers between devices  9.77 us (36%)
  blocking collectives  9.56 us (35%)
  Pallas kernels  6.64 us (24%)
  between operations  0.7 us (3%)
  waiting for transfers between devices  0.62 us (2%)
    all_gather x1, blocking collectives, local(): tiles = lax.all_gather(plane, 'span', axis=0, tiled=False)  9.56 us
    ppermute x6, starting transfers between devices, send(): return lax.ppermute(value, ('stream', 'span'), moves)  8.57 us
    pallas_call x1, Pallas kernels, local(): pl.pallas_call(last_kernel, out_shape=(f32(*pre_pops.shape), f32(*main_po...  2.23 us
    pallas_call x1, Pallas kernels, local(): pl.pallas_call(first_kernel, out_shape=(f32(*pre_pops.shape), f32(*main_p...  2.06 us
    pallas_call x1, Pallas kernels, local(): pl.pallas_call(middle_kernel, out_shape=(f32(POPS, rows - 2, width, coars...  1.98 us
    ppermute x1, starting transfers between devices, swap_in_pairs(): return lax.ppermute(value, ('stream', 'span'), moves)  1.2 us
    ppermute x1, waiting for transfers between devices, swap_in_pairs(): return lax.ppermute(value, ('stream', 'span'), moves)  0.6 us
  transfers between devices with their start and end apart: 7, of which 1 were waited for; matrix products, arithmetic and copies ran while one was open for 0% of the time, Pallas kernels for 9%

profile of v8, /device:TPU:0, one launch (start us, length us, event | category | flops | bytes accessed | tf_op | source)
XLA Modules:
  0.0 27.3 jit_solution(18223209871804385391)
XLA Ops:
  0.6 0.0 copy-start.1
  0.6 2.1 %collide_and_pack.1 = (f32[19,8,8,128]{3,2,1,0:T(8,128)S(1)}, f32[19,8,8,256]{3,2,1,0:T(8,128)S(1)}, f32[24,8,384]{2,1,0:T(8,128)S(1)}, f32[24,8,384]{2,1,0:T(8,128)S(1)}) custom-call(f32[19,8,8,128]{3,2,1,0:T(8,128)} %pre_hbm.1, f32[19,8,8,256]{3,2,1,0:T(8,128)} %main_hbm.1), custom_call_target="tpu_custom_call" | custom-call | tf_op jit(solution)/shard_map/collide_and_pack/pallas_call | solution.py:935
  2.7 3.4 %collective-permute-start = (f32[24,8,384]{2,1,0:T(8,128)S(1)}, f32[24,8,384]{2,1,0:T(8,128)S(1)}, u32[]{:S(2)}, u32[]{:S(2)}) collective-permute-start(f32[24,8,384]{2,1,0:T(8,128)S(1)} %get-tuple-element.22.edge_cross), channel_id=1, source_target_pairs={{0,7},{1,2},{2,1},{3,4},{4,3},{5,6},{6,5},{7,0},{8,15},{9,10},{10,... | collective-permute-start | bytes 884744 | tf_op jit(solution)/shard_map/ppermute | solution.py:916
  6.1 0.0 collective-permute-start.1
  6.1 0.0 copy-done.1
  6.1 0.0 copy-start
  6.1 0.3 %faces.1 = (f32[3,8,384]{2,1,0:T(8,128)S(1)}, f32[14,8,384]{2,1,0:T(8,128)S(1)}, f32[14,8,384]{2,1,0:T(8,128)S(1)}, f32[16,8,128]{2,1,0:T(8,128)S(1)}) custom-call(s32[1,256]{1,0:T(1,128)S(1)} %bitcast.9, f32[19,8,8,128]{3,2,1,0:T(8,128)S(1)} %get-tuple-element.19.star_pre, f32[19,8,8,256]{3,2,1,0:T(8,128)S(1)} %get-tuple-element.20.star_main), custom_call_target="tpu_custom_call" | custom-call | tf_op jit(solution)/shard_map/faces/pallas_call | solution.py:952
  6.4 0.0 copy-start.2
  6.4 3.7 %collective-permute-start.2 = (f32[14,8,384]{2,1,0:T(8,128)S(1)}, f32[14,8,384]{2,1,0:T(8,128)S(1)}, u32[]{:S(2)}, u32[]{:S(2)}) collective-permute-start(f32[14,8,384]{2,1,0:T(8,128)S(1)} %get-tuple-element.28), channel_id=1, source_target_pairs={{0,24},{1,25},{2,26},{3,27},{4,28},{5,29},{6,30},{7,31},{8,0},{9,1... | collective-permute-start | bytes 516104 | tf_op jit(solution)/shard_map/ppermute | solution.py:916
  10.1 0.0 collective-permute-start.3
  10.1 9.6 %all-gather = f32[128,8,128]{2,1,0:T(8,128)S(1)} all-gather(f32[16,8,128]{2,1,0:T(8,128)S(1)} %get-tuple-element.24), channel_id=2, replica_groups=mesh['stream'=4,'span'=8] {'span'}, dimensions={0}, use_global_device_ids=true | all-gather | bytes 589824 | tf_op jit(solution)/shard_map/all_gather | solution.py:968
  19.7 0.0 collective-permute-done.2.x_high
  19.7 0.0 collective-permute-done.3.x_low
  19.7 1.5 %collective-permute-start.4 = (f32[32,384]{1,0:T(8,128)S(1)}, f32[32,384]{1,0:T(8,128)S(1)}, u32[]{:S(2)}, u32[]{:S(2)}) collective-permute-start(f32[32,384]{1,0:T(8,128)S(1)} %get-tuple-element.30), channel_id=1, source_target_pairs={{0,7},{1,2},{2,1},{3,4},{4,3},{5,6},{6,5},{7,0},{8,15},{9,10},{10,... | collective-permute-start | bytes 147464 | tf_op jit(solution)/shard_map/ppermute | solution.py:916
  21.2 0.0 collective-permute-start.5
  21.2 0.0 copy-done
  21.3 1.2 %collective-permute-start.6 = (f32[4,8,128]{2,1,0:T(8,128)S(1)}, f32[4,8,128]{2,1,0:T(8,128)S(1)}, u32[]{:S(2)}, u32[]{:S(2)}) collective-permute-start(f32[4,8,128]{2,1,0:T(8,128)S(1)} %behind_plane.1), channel_id=1, source_target_pairs={{0,8},{1,9},{2,10},{3,11},{4,12},{5,13},{6,14},{7,15},{8,0},{9,1},... | collective-permute-start | bytes 49160 | tf_op jit(solution)/shard_map/ppermute | solution.py:923
  22.5 0.0 collective-permute-done.cross
  22.5 0.0 collective-permute-done.1.same
  22.5 0.0 copy-done.2
  22.5 2.0 %middle_rows.1 = (f32[19,6,8,128]{3,2,1,0:T(8,128)S(1)}, f32[19,6,8,256]{3,2,1,0:T(8,128)S(1)}, f32[3,5,8,256]{3,2,1,0:T(8,128)S(1)}, f32[3,9,8,128]{3,2,1,0:T(8...) custom-call(s32[1,8]{1,0:T(1,128)S(1)} %bitcast.8, ...), custom_call_target="tpu_custom_call" | custom-call | tf_op jit(solution)/shard_map/middle_rows/pallas_call | solution.py:994
  24.5 0.6 %collective-permute-done.6.back = f32[4,8,128]{2,1,0:T(8,128)S(1)} collective-permute-done((f32[4,8,128]{2,1,0:T(8,128)S(1)}, f32[4,8,128]{2,1,0:T(8,128)S(1)}, u32[]{:S(2)}, u32[]{:S(2)}) %collective-permute-start.6) | collective-permute-done | bytes 16416 | tf_op jit(solution)/shard_map/ppermute | solution.py:923
  25.1 0.0 collective-permute-done.4.e_cross
  25.1 0.0 collective-permute-done.5.e_same
  25.1 2.2 %last_rows.1 = (f32[19,8,8,128]{3,2,1,0:T(8,128)}, f32[19,8,8,256]{3,2,1,0:T(8,128)}) custom-call(f32[3,8,384]{2,1,0:T(8,128)S(1)} %get-tuple-element.21.masks, f32[19,8,8,128]{3,2,1,0:T(8,128)S(1)} %get-tuple-element.19.star_pre, f32[19,8,8,256]{3,2,1,0:T(8,128)S(1)} %get-tuple-element.20.star_main, ...), custom_call_target="tpu_custom_call", output_to_operand_aliasing={{0}: (17, {}), {1}: (18, {})} | custom-call | tf_op jit(solution)/shard_map/last_rows/pallas_call | solution.py:1020
  (2 shorter events, 0.1 us)
Async XLA Ops:
  0.6 5.5 %copy-start.1 = (s32[256]{0:T(256)S(1)}, s32[256]{0:T(256)}, u32[]{:S(2)}) copy-start(s32[256]{0:T(256)} %param.9) | copy-start | bytes 3076
  2.7 19.8 %collective-permute-start = (f32[24,8,384]{2,1,0:T(8,128)S(1)}, f32[24,8,384]{2,1,0:T(8,128)S(1)}, u32[]{:S(2)}, u32[]{:S(2)}) collective-permute-start(f32[24,8,384]{2,1,0:T(8,128)S(1)} %get-tuple-element.22.edge_cross), channel_id=1, source_target_pairs={{0,7},{1,2},{2,1},{3,4},{4,3},{5,6},{6,5},{7,0},{8,15},{9,10},{10,... | collective-permute-start | bytes 884744 | tf_op jit(solution)/shard_map/ppermute | solution.py:916
  6.1 16.3 %collective-permute-start.1 = (f32[24,8,384]{2,1,0:T(8,128)S(1)}, f32[24,8,384]{2,1,0:T(8,128)S(1)}, u32[]{:S(2)}, u32[]{:S(2)}) collective-permute-start(f32[24,8,384]{2,1,0:T(8,128)S(1)} %get-tuple-element.23.edge_same), channel_id=1, source_target_pairs={{0,1},{1,0},{2,3},{3,2},{4,5},{5,4},{6,7},{7,6},{8,9},{9,8},{10,11... | collective-permute-start | bytes 884744 | tf_op jit(solution)/shard_map/ppermute | solution.py:916
  6.1 15.1 %copy-start = (s32[8]{0:T(128)S(1)}, s32[8]{0:T(128)}, u32[]{:S(2)}) copy-start(s32[8]{0:T(128)} %param.7) | copy-start | bytes 100
  6.4 16.0 %copy-start.2 = (s32[8]{0:T(128)S(1)}, s32[8]{0:T(128)}, u32[]{:S(2)}) copy-start(s32[8]{0:T(128)} %param.8) | copy-start | bytes 100
  6.4 13.2 %collective-permute-start.2 = (f32[14,8,384]{2,1,0:T(8,128)S(1)}, f32[14,8,384]{2,1,0:T(8,128)S(1)}, u32[]{:S(2)}, u32[]{:S(2)}) collective-permute-start(f32[14,8,384]{2,1,0:T(8,128)S(1)} %get-tuple-element.28), channel_id=1, source_target_pairs={{0,24},{1,25},{2,26},{3,27},{4,28},{5,29},{6,30},{7,31},{8,0},{9,1... | collective-permute-start | bytes 516104 | tf_op jit(solution)/shard_map/ppermute | solution.py:916
  10.1 9.6 %collective-permute-start.3 = (f32[14,8,384]{2,1,0:T(8,128)S(1)}, f32[14,8,384]{2,1,0:T(8,128)S(1)}, u32[]{:S(2)}, u32[]{:S(2)}) collective-permute-start(f32[14,8,384]{2,1,0:T(8,128)S(1)} %get-tuple-element.29), channel_id=1, source_target_pairs={{0,8},{1,9},{2,10},{3,11},{4,12},{5,13},{6,14},{7,15},{8,16},{9,17... | collective-permute-start | bytes 516104 | tf_op jit(solution)/shard_map/ppermute | solution.py:916
  19.7 5.3 %collective-permute-start.4 = (f32[32,384]{1,0:T(8,128)S(1)}, f32[32,384]{1,0:T(8,128)S(1)}, u32[]{:S(2)}, u32[]{:S(2)}) collective-permute-start(f32[32,384]{1,0:T(8,128)S(1)} %get-tuple-element.30), channel_id=1, source_target_pairs={{0,7},{1,2},{2,1},{3,4},{4,3},{5,6},{6,5},{7,0},{8,15},{9,10},{10,... | collective-permute-start | bytes 147464 | tf_op jit(solution)/shard_map/ppermute | solution.py:916
  21.2 3.8 %collective-permute-start.5 = (f32[32,384]{1,0:T(8,128)S(1)}, f32[32,384]{1,0:T(8,128)S(1)}, u32[]{:S(2)}, u32[]{:S(2)}) collective-permute-start(f32[32,384]{1,0:T(8,128)S(1)} %get-tuple-element.31), channel_id=1, source_target_pairs={{0,1},{1,0},{2,3},{3,2},{4,5},{5,4},{6,7},{7,6},{8,9},{9,8},{10,11... | collective-permute-start | bytes 147464 | tf_op jit(solution)/shard_map/ppermute | solution.py:916
  21.3 3.8 %collective-permute-start.6 = (f32[4,8,128]{2,1,0:T(8,128)S(1)}, f32[4,8,128]{2,1,0:T(8,128)S(1)}, u32[]{:S(2)}, u32[]{:S(2)}) collective-permute-start(f32[4,8,128]{2,1,0:T(8,128)S(1)} %behind_plane.1), channel_id=1, source_target_pairs={{0,8},{1,9},{2,10},{3,11},{4,12},{5,13},{6,14},{7,15},{8,0},{9,1},... | collective-permute-start | bytes 49160 | tf_op jit(solution)/shard_map/ppermute | solution.py:923

commit v9 on v8

--- a/solution.py
+++ b/solution.py
@@ -168,15 +168,19 @@
 
 
 def first_kernel(
+    walls_hbm,
     pre_hbm,
     main_hbm,
     star_pre,
     star_main,
     z_same,
     z_cross,
+    masks,
     pre,
     main,
+    walls,
     arrived,
+    walls_arrived,
 ):
     rows = pre.shape[1]
     coarse = pre.shape[3]
@@ -189,9 +193,13 @@
         ]
         for x_at in range(rows)
     ]
+    copy_walls = pltpu.make_async_copy(walls_hbm, walls.at[0], walls_arrived)
+    copy_walls.start()
     for row in copies:
         for copy in row:
             copy.start()
+    copy_walls.wait()
+    fill_masks(walls, masks)
     for x_at in range(rows):
         for copy in copies[x_at]:
             copy.wait()
@@ -247,9 +255,8 @@
             face[13, row : row + 1, lanes] = star[pop, x_at, z_at : z_at + 1, :]
 
 
-def face_kernel(walls, star_pre, star_main, masks, x_hi, x_lo, plane):
+def face_kernel(masks, star_pre, star_main, x_hi, x_lo, plane):
     coarse = star_pre.shape[3]
-    fill_masks(walls, masks)
     for star, lanes in zip((star_pre, star_main), lanes_of(coarse, star_main.shape[3])):
         blocked = masks_of(masks, lanes)
         fill_face(star, lanes, blocked, True, x_hi)
@@ -932,34 +939,36 @@
     tile_row, phase_row = (row.reshape(1, span_count) for row in (tile_map, layer_phase))
 
     in_hbm = lambda value: pltpu.with_memory_space_constraint(value, pltpu.HBM)
-    star_pre, star_main, z_same, z_cross = pl.pallas_call(
+    star_pre, star_main, z_same, z_cross, masks = pl.pallas_call(
         first_kernel,
         out_shape=(
             f32(*pre_pops.shape),
             f32(*main_pops.shape),
             f32(KEPT, rows, lanes),
             f32(KEPT, rows, lanes),
+            f32(3, 8, lanes),
         ),
-        in_specs=[outside, outside],
+        in_specs=[outside, outside, outside],
         scratch_shapes=[
             pltpu.VMEM(pre_pops.shape, jnp.float32),
             pltpu.VMEM(main_pops.shape, jnp.float32),
+            pltpu.VMEM((1, fine), jnp.int32),
             pltpu.SemaphoreType.DMA((2, rows)),
+            pltpu.SemaphoreType.DMA,
         ],
         compiler_params=pltpu.CompilerParams(vmem_limit_bytes=VMEM_SMALL),
         name="collide_and_pack",
-    )(in_hbm(pre_pops), in_hbm(main_pops))
-    masks, x_hi, x_lo, plane = pl.pallas_call(
+    )(in_hbm(wall_flags), in_hbm(pre_pops), in_hbm(main_pops))
+    x_hi, x_lo, plane = pl.pallas_call(
         face_kernel,
         out_shape=(
-            f32(3, 8, lanes),
             f32(FACE, width, lanes),
             f32(FACE, width, lanes),
             f32(PLANE, width, coarse),
         ),
         compiler_params=params,
         name="faces",
-    )(wall_flags.reshape(1, fine), star_pre, star_main)
+    )(masks, star_pre, star_main)
 
     same = send(z_same, 0, sibling)
     cross = send(z_cross, 0, beyond)

time: 27.5 us -> 27.9 us (1.015)
  Pallas kernels: 6.64 us -> 7.03 us
    pallas_call x1, Pallas kernels: 2.06 us -> 2.56 us  [local(): pl.pallas_call(first_kernel, out_shape=(f32(*pre_pops.shape), f32(*main_p...]
  transfers between devices with their start and end apart: 7 -> 7, of which waited for: 1 -> 1; matrix products, arithmetic and copies ran while one was open for 0% -> 0% of each run, Pallas kernels for 9% -> 8%
where the time goes in v9:
time: 27.9 us; the launch traced here: 27.7 us
  starting transfers between devices  9.87 us (35%)
  blocking collectives  9.56 us (34%)
  Pallas kernels  7.03 us (25%)
  between operations  0.69 us (2%)
  waiting for transfers between devices  0.52 us (2%)
    all_gather x1, blocking collectives, local(): tiles = lax.all_gather(plane, 'span', axis=0, tiled=False)  9.56 us
    ppermute x6, starting transfers between devices, send(): return lax.ppermute(value, ('stream', 'span'), moves)  8.57 us
    pallas_call x1, Pallas kernels, local(): pl.pallas_call(first_kernel, out_shape=(f32(*pre_pops.shape), f32(*main_p...  2.56 us
    pallas_call x1, Pallas kernels, local(): pl.pallas_call(last_kernel, out_shape=(f32(*pre_pops.shape), f32(*main_po...  2.23 us
    pallas_call x1, Pallas kernels, local(): pl.pallas_call(middle_kernel, out_shape=(f32(POPS, rows - 2, width, coars...  1.98 us
    ppermute x1, starting transfers between devices, swap_in_pairs(): return lax.ppermute(value, ('stream', 'span'), moves)  1.3 us
  transfers between devices with their start and end apart: 7, of which 1 were waited for; matrix products, arithmetic and copies ran while one was open for 0% of the time, Pallas kernels for 8%

profile of v9, /device:TPU:0, one launch (start us, length us, event | category | flops | bytes accessed | tf_op | source)
XLA Modules:
  0.0 27.7 jit_solution(7627782152359820647)
XLA Ops:
  0.6 2.6 %collide_and_pack.1 = (f32[19,8,8,128]{3,2,1,0:T(8,128)S(1)}, f32[19,8,8,256]{3,2,1,0:T(8,128)S(1)}, f32[24,8,384]{2,1,0:T(8,128)S(1)}, f32[24,8,384]{2,1,0:T(8,128)S(1)}, f32[3,8,384]{2,1,0:T(8,128)S(1)}) custom-call(s32[256]{0:T(256)} %walls_hbm.1, f32[19,8,8,128]{3,2,1,0:T(8,128)} %pre_hbm.1, f32[19,8,8,256]{3,2,1,0:T(8,128)} %main_hbm.1), custom_call_target="tpu_custom_call" | custom-call | tf_op jit(solution)/shard_map/collide_and_pack/pallas_call | solution.py:942
  3.2 3.4 %collective-permute-start = (f32[24,8,384]{2,1,0:T(8,128)S(1)}, f32[24,8,384]{2,1,0:T(8,128)S(1)}, u32[]{:S(2)}, u32[]{:S(2)}) collective-permute-start(f32[24,8,384]{2,1,0:T(8,128)S(1)} %get-tuple-element.22.edge_cross), channel_id=1, source_target_pairs={{0,7},{1,2},{2,1},{3,4},{4,3},{5,6},{6,5},{7,0},{8,15},{9,10},{10,... | collective-permute-start | bytes 884744 | tf_op jit(solution)/shard_map/ppermute | solution.py:923
  6.6 0.0 collective-permute-start.1
  6.6 0.0 copy-start
  6.6 0.2 faces.1
  6.8 0.0 copy-start.1
  6.8 3.7 %collective-permute-start.2 = (f32[14,8,384]{2,1,0:T(8,128)S(1)}, f32[14,8,384]{2,1,0:T(8,128)S(1)}, u32[]{:S(2)}, u32[]{:S(2)}) collective-permute-start(f32[14,8,384]{2,1,0:T(8,128)S(1)} %get-tuple-element.28), channel_id=1, source_target_pairs={{0,24},{1,25},{2,26},{3,27},{4,28},{5,29},{6,30},{7,31},{8,0},{9,1... | collective-permute-start | bytes 516104 | tf_op jit(solution)/shard_map/ppermute | solution.py:923
  10.5 0.0 collective-permute-start.3
  10.5 9.6 %all-gather = f32[128,8,128]{2,1,0:T(8,128)S(1)} all-gather(f32[16,8,128]{2,1,0:T(8,128)S(1)} %get-tuple-element.24), channel_id=2, replica_groups=mesh['stream'=4,'span'=8] {'span'}, dimensions={0}, use_global_device_ids=true | all-gather | bytes 589824 | tf_op jit(solution)/shard_map/all_gather | solution.py:977
  20.1 0.0 collective-permute-done.2.x_high
  20.1 0.0 collective-permute-done.3.x_low
  20.1 1.5 %collective-permute-start.4 = (f32[32,384]{1,0:T(8,128)S(1)}, f32[32,384]{1,0:T(8,128)S(1)}, u32[]{:S(2)}, u32[]{:S(2)}) collective-permute-start(f32[32,384]{1,0:T(8,128)S(1)} %get-tuple-element.30), channel_id=1, source_target_pairs={{0,7},{1,2},{2,1},{3,4},{4,3},{5,6},{6,5},{7,0},{8,15},{9,10},{10,... | collective-permute-start | bytes 147464 | tf_op jit(solution)/shard_map/ppermute | solution.py:923
  21.6 0.0 collective-permute-start.5
  21.6 0.0 copy-done
  21.6 1.3 %collective-permute-start.6 = (f32[4,8,128]{2,1,0:T(8,128)S(1)}, f32[4,8,128]{2,1,0:T(8,128)S(1)}, u32[]{:S(2)}, u32[]{:S(2)}) collective-permute-start(f32[4,8,128]{2,1,0:T(8,128)S(1)} %behind_plane.1), channel_id=1, source_target_pairs={{0,8},{1,9},{2,10},{3,11},{4,12},{5,13},{6,14},{7,15},{8,0},{9,1},... | collective-permute-start | bytes 49160 | tf_op jit(solution)/shard_map/ppermute | solution.py:930
  22.9 0.0 collective-permute-done.cross
  22.9 0.0 collective-permute-done.1.same
  23.0 0.0 copy-done.1
  23.0 2.0 %middle_rows.1 = (f32[19,6,8,128]{3,2,1,0:T(8,128)S(1)}, f32[19,6,8,256]{3,2,1,0:T(8,128)S(1)}, f32[3,5,8,256]{3,2,1,0:T(8,128)S(1)}, f32[3,9,8,128]{3,2,1,0:T(8...) custom-call(s32[1,8]{1,0:T(1,128)S(1)} %bitcast.7, ...), custom_call_target="tpu_custom_call" | custom-call | tf_op jit(solution)/shard_map/middle_rows/pallas_call | solution.py:1003
  24.9 0.5 %collective-permute-done.6.back = f32[4,8,128]{2,1,0:T(8,128)S(1)} collective-permute-done((f32[4,8,128]{2,1,0:T(8,128)S(1)}, f32[4,8,128]{2,1,0:T(8,128)S(1)}, u32[]{:S(2)}, u32[]{:S(2)}) %collective-permute-start.6) | collective-permute-done | bytes 16416 | tf_op jit(solution)/shard_map/ppermute | solution.py:930
  25.4 0.0 collective-permute-done.4.e_cross
  25.5 0.0 collective-permute-done.5.e_same
  25.5 2.2 %last_rows.1 = (f32[19,8,8,128]{3,2,1,0:T(8,128)}, f32[19,8,8,256]{3,2,1,0:T(8,128)}) custom-call(f32[3,8,384]{2,1,0:T(8,128)S(1)} %get-tuple-element.19.masks, f32[19,8,8,128]{3,2,1,0:T(8,128)S(1)} %get-tuple-element.20.star_pre, f32[19,8,8,256]{3,2,1,0:T(8,128)S(1)} %get-tuple-element.21.star_main, ...), custom_call_target="tpu_custom_call", output_to_operand_aliasing={{0}: (17, {}), {1}: (18, {})} | custom-call | tf_op jit(solution)/shard_map/last_rows/pallas_call | solution.py:1029
  (2 shorter events, 0.1 us)
Async XLA Ops:
  3.2 19.8 %collective-permute-start = (f32[24,8,384]{2,1,0:T(8,128)S(1)}, f32[24,8,384]{2,1,0:T(8,128)S(1)}, u32[]{:S(2)}, u32[]{:S(2)}) collective-permute-start(f32[24,8,384]{2,1,0:T(8,128)S(1)} %get-tuple-element.22.edge_cross), channel_id=1, source_target_pairs={{0,7},{1,2},{2,1},{3,4},{4,3},{5,6},{6,5},{7,0},{8,15},{9,10},{10,... | collective-permute-start | bytes 884744 | tf_op jit(solution)/shard_map/ppermute | solution.py:923
  6.6 16.3 %collective-permute-start.1 = (f32[24,8,384]{2,1,0:T(8,128)S(1)}, f32[24,8,384]{2,1,0:T(8,128)S(1)}, u32[]{:S(2)}, u32[]{:S(2)}) collective-permute-start(f32[24,8,384]{2,1,0:T(8,128)S(1)} %get-tuple-element.23.edge_same), channel_id=1, source_target_pairs={{0,1},{1,0},{2,3},{3,2},{4,5},{5,4},{6,7},{7,6},{8,9},{9,8},{10,11... | collective-permute-start | bytes 884744 | tf_op jit(solution)/shard_map/ppermute | solution.py:923
  6.6 15.0 %copy-start = (s32[8]{0:T(128)S(1)}, s32[8]{0:T(128)}, u32[]{:S(2)}) copy-start(s32[8]{0:T(128)} %param.7) | copy-start | bytes 100
  6.8 16.1 %copy-start.1 = (s32[8]{0:T(128)S(1)}, s32[8]{0:T(128)}, u32[]{:S(2)}) copy-start(s32[8]{0:T(128)} %param.8) | copy-start | bytes 100
  6.8 13.2 %collective-permute-start.2 = (f32[14,8,384]{2,1,0:T(8,128)S(1)}, f32[14,8,384]{2,1,0:T(8,128)S(1)}, u32[]{:S(2)}, u32[]{:S(2)}) collective-permute-start(f32[14,8,384]{2,1,0:T(8,128)S(1)} %get-tuple-element.28), channel_id=1, source_target_pairs={{0,24},{1,25},{2,26},{3,27},{4,28},{5,29},{6,30},{7,31},{8,0},{9,1... | collective-permute-start | bytes 516104 | tf_op jit(solution)/shard_map/ppermute | solution.py:923
  10.5 9.6 %collective-permute-start.3 = (f32[14,8,384]{2,1,0:T(8,128)S(1)}, f32[14,8,384]{2,1,0:T(8,128)S(1)}, u32[]{:S(2)}, u32[]{:S(2)}) collective-permute-start(f32[14,8,384]{2,1,0:T(8,128)S(1)} %get-tuple-element.29), channel_id=1, source_target_pairs={{0,8},{1,9},{2,10},{3,11},{4,12},{5,13},{6,14},{7,15},{8,16},{9,17... | collective-permute-start | bytes 516104 | tf_op jit(solution)/shard_map/ppermute | solution.py:923
  20.1 5.3 %collective-permute-start.4 = (f32[32,384]{1,0:T(8,128)S(1)}, f32[32,384]{1,0:T(8,128)S(1)}, u32[]{:S(2)}, u32[]{:S(2)}) collective-permute-start(f32[32,384]{1,0:T(8,128)S(1)} %get-tuple-element.30), channel_id=1, source_target_pairs={{0,7},{1,2},{2,1},{3,4},{4,3},{5,6},{6,5},{7,0},{8,15},{9,10},{10,... | collective-permute-start | bytes 147464 | tf_op jit(solution)/shard_map/ppermute | solution.py:923
  21.6 3.8 %collective-permute-start.5 = (f32[32,384]{1,0:T(8,128)S(1)}, f32[32,384]{1,0:T(8,128)S(1)}, u32[]{:S(2)}, u32[]{:S(2)}) collective-permute-start(f32[32,384]{1,0:T(8,128)S(1)} %get-tuple-element.31), channel_id=1, source_target_pairs={{0,1},{1,0},{2,3},{3,2},{4,5},{5,4},{6,7},{7,6},{8,9},{9,8},{10,11... | collective-permute-start | bytes 147464 | tf_op jit(solution)/shard_map/ppermute | solution.py:923
  21.6 3.8 %collective-permute-start.6 = (f32[4,8,128]{2,1,0:T(8,128)S(1)}, f32[4,8,128]{2,1,0:T(8,128)S(1)}, u32[]{:S(2)}, u32[]{:S(2)}) collective-permute-start(f32[4,8,128]{2,1,0:T(8,128)S(1)} %behind_plane.1), channel_id=1, source_target_pairs={{0,8},{1,9},{2,10},{3,11},{4,12},{5,13},{6,14},{7,15},{8,0},{9,1},... | collective-permute-start | bytes 49160 | tf_op jit(solution)/shard_map/ppermute | solution.py:930

commit v10 on v8

--- a/solution.py
+++ b/solution.py
@@ -127,6 +127,9 @@
             continue
         step_x, step_y, step_z = velocities[which_pop]
         source = base(which_pop, x_at - step_x)
+        if which_pop == 0:
+            result.append(source)
+            continue
         if step_z != 0 and sub is None:
             sub = lax.broadcasted_iota(jnp.int32, source.shape, 0)
         width = source.shape[0]
@@ -305,7 +308,8 @@
 def column_values(is_left, first, second, inner, shift, blocked):
     inward, outward = (forward_z, backward_z) if is_left else (backward_z, forward_z)
     result = []
-    for pop in range(POPS):
+    result.append(first(0))
+    for pop in range(1, POPS):
         step_x, step_y, _ = velocities[pop]
         if pop in inward:
             source = shift(second, inward.index(pop), step_x)

time: 27.5 us -> 27.5 us (level)
  no operation moved by 1% of the time
where the time goes in v10:
time: 27.5 us; the launch traced here: 27.3 us
  starting transfers between devices  9.77 us (36%)
  blocking collectives  9.56 us (35%)
  Pallas kernels  6.64 us (24%)
  between operations  0.7 us (3%)
  waiting for transfers between devices  0.62 us (2%)
    all_gather x1, blocking collectives, local(): tiles = lax.all_gather(plane, 'span', axis=0, tiled=False)  9.56 us
    ppermute x6, starting transfers between devices, send(): return lax.ppermute(value, ('stream', 'span'), moves)  8.57 us
    pallas_call x1, Pallas kernels, local(): pl.pallas_call(last_kernel, out_shape=(f32(*pre_pops.shape), f32(*main_po...  2.23 us
    pallas_call x1, Pallas kernels, local(): pl.pallas_call(first_kernel, out_shape=(f32(*pre_pops.shape), f32(*main_p...  2.06 us
    pallas_call x1, Pallas kernels, local(): pl.pallas_call(middle_kernel, out_shape=(f32(POPS, rows - 2, width, coars...  1.98 us
    ppermute x1, starting transfers between devices, swap_in_pairs(): return lax.ppermute(value, ('stream', 'span'), moves)  1.2 us
    ppermute x1, waiting for transfers between devices, swap_in_pairs(): return lax.ppermute(value, ('stream', 'span'), moves)  0.6 us
  transfers between devices with their start and end apart: 7, of which 1 were waited for; matrix products, arithmetic and copies ran while one was open for 0% of the time, Pallas kernels for 9%

profile of v10, /device:TPU:0, one launch (start us, length us, event | category | flops | bytes accessed | tf_op | source)
XLA Modules:
  0.0 27.3 jit_solution(18223209871804385391)
XLA Ops:
  0.6 0.0 copy-start.1
  0.6 2.1 %collide_and_pack.1 = (f32[19,8,8,128]{3,2,1,0:T(8,128)S(1)}, f32[19,8,8,256]{3,2,1,0:T(8,128)S(1)}, f32[24,8,384]{2,1,0:T(8,128)S(1)}, f32[24,8,384]{2,1,0:T(8,128)S(1)}) custom-call(f32[19,8,8,128]{3,2,1,0:T(8,128)} %pre_hbm.1, f32[19,8,8,256]{3,2,1,0:T(8,128)} %main_hbm.1), custom_call_target="tpu_custom_call" | custom-call | tf_op jit(solution)/shard_map/collide_and_pack/pallas_call | solution.py:939
  2.7 3.4 %collective-permute-start = (f32[24,8,384]{2,1,0:T(8,128)S(1)}, f32[24,8,384]{2,1,0:T(8,128)S(1)}, u32[]{:S(2)}, u32[]{:S(2)}) collective-permute-start(f32[24,8,384]{2,1,0:T(8,128)S(1)} %get-tuple-element.22.edge_cross), channel_id=1, source_target_pairs={{0,7},{1,2},{2,1},{3,4},{4,3},{5,6},{6,5},{7,0},{8,15},{9,10},{10,... | collective-permute-start | bytes 884744 | tf_op jit(solution)/shard_map/ppermute | solution.py:920
  6.1 0.0 collective-permute-start.1
  6.1 0.0 copy-done.1
  6.1 0.0 copy-start
  6.1 0.3 %faces.1 = (f32[3,8,384]{2,1,0:T(8,128)S(1)}, f32[14,8,384]{2,1,0:T(8,128)S(1)}, f32[14,8,384]{2,1,0:T(8,128)S(1)}, f32[16,8,128]{2,1,0:T(8,128)S(1)}) custom-call(s32[1,256]{1,0:T(1,128)S(1)} %bitcast.9, f32[19,8,8,128]{3,2,1,0:T(8,128)S(1)} %get-tuple-element.19.star_pre, f32[19,8,8,256]{3,2,1,0:T(8,128)S(1)} %get-tuple-element.20.star_main), custom_call_target="tpu_custom_call" | custom-call | tf_op jit(solution)/shard_map/faces/pallas_call | solution.py:956
  6.4 0.0 copy-start.2
  6.4 3.7 %collective-permute-start.2 = (f32[14,8,384]{2,1,0:T(8,128)S(1)}, f32[14,8,384]{2,1,0:T(8,128)S(1)}, u32[]{:S(2)}, u32[]{:S(2)}) collective-permute-start(f32[14,8,384]{2,1,0:T(8,128)S(1)} %get-tuple-element.28), channel_id=1, source_target_pairs={{0,24},{1,25},{2,26},{3,27},{4,28},{5,29},{6,30},{7,31},{8,0},{9,1... | collective-permute-start | bytes 516104 | tf_op jit(solution)/shard_map/ppermute | solution.py:920
  10.1 0.0 collective-permute-start.3
  10.1 9.6 %all-gather = f32[128,8,128]{2,1,0:T(8,128)S(1)} all-gather(f32[16,8,128]{2,1,0:T(8,128)S(1)} %get-tuple-element.24), channel_id=2, replica_groups=mesh['stream'=4,'span'=8] {'span'}, dimensions={0}, use_global_device_ids=true | all-gather | bytes 589824 | tf_op jit(solution)/shard_map/all_gather | solution.py:972
  19.7 0.0 collective-permute-done.2.x_high
  19.7 0.0 collective-permute-done.3.x_low
  19.7 1.5 %collective-permute-start.4 = (f32[32,384]{1,0:T(8,128)S(1)}, f32[32,384]{1,0:T(8,128)S(1)}, u32[]{:S(2)}, u32[]{:S(2)}) collective-permute-start(f32[32,384]{1,0:T(8,128)S(1)} %get-tuple-element.30), channel_id=1, source_target_pairs={{0,7},{1,2},{2,1},{3,4},{4,3},{5,6},{6,5},{7,0},{8,15},{9,10},{10,... | collective-permute-start | bytes 147464 | tf_op jit(solution)/shard_map/ppermute | solution.py:920
  21.2 0.0 collective-permute-start.5
  21.2 0.0 copy-done
  21.3 1.2 %collective-permute-start.6 = (f32[4,8,128]{2,1,0:T(8,128)S(1)}, f32[4,8,128]{2,1,0:T(8,128)S(1)}, u32[]{:S(2)}, u32[]{:S(2)}) collective-permute-start(f32[4,8,128]{2,1,0:T(8,128)S(1)} %behind_plane.1), channel_id=1, source_target_pairs={{0,8},{1,9},{2,10},{3,11},{4,12},{5,13},{6,14},{7,15},{8,0},{9,1},... | collective-permute-start | bytes 49160 | tf_op jit(solution)/shard_map/ppermute | solution.py:927
  22.5 0.0 collective-permute-done.cross
  22.5 0.0 collective-permute-done.1.same
  22.5 0.0 copy-done.2
  22.5 2.0 %middle_rows.1 = (f32[19,6,8,128]{3,2,1,0:T(8,128)S(1)}, f32[19,6,8,256]{3,2,1,0:T(8,128)S(1)}, f32[3,5,8,256]{3,2,1,0:T(8,128)S(1)}, f32[3,9,8,128]{3,2,1,0:T(8...) custom-call(s32[1,8]{1,0:T(1,128)S(1)} %bitcast.8, ...), custom_call_target="tpu_custom_call" | custom-call | tf_op jit(solution)/shard_map/middle_rows/pallas_call | solution.py:998
  24.5 0.6 %collective-permute-done.6.back = f32[4,8,128]{2,1,0:T(8,128)S(1)} collective-permute-done((f32[4,8,128]{2,1,0:T(8,128)S(1)}, f32[4,8,128]{2,1,0:T(8,128)S(1)}, u32[]{:S(2)}, u32[]{:S(2)}) %collective-permute-start.6) | collective-permute-done | bytes 16416 | tf_op jit(solution)/shard_map/ppermute | solution.py:927
  25.1 0.0 collective-permute-done.4.e_cross
  25.1 0.0 collective-permute-done.5.e_same
  25.1 2.2 %last_rows.1 = (f32[19,8,8,128]{3,2,1,0:T(8,128)}, f32[19,8,8,256]{3,2,1,0:T(8,128)}) custom-call(f32[3,8,384]{2,1,0:T(8,128)S(1)} %get-tuple-element.21.masks, f32[19,8,8,128]{3,2,1,0:T(8,128)S(1)} %get-tuple-element.19.star_pre, f32[19,8,8,256]{3,2,1,0:T(8,128)S(1)} %get-tuple-element.20.star_main, ...), custom_call_target="tpu_custom_call", output_to_operand_aliasing={{0}: (17, {}), {1}: (18, {})} | custom-call | tf_op jit(solution)/shard_map/last_rows/pallas_call | solution.py:1024
  (2 shorter events, 0.1 us)
Async XLA Ops:
  0.6 5.5 %copy-start.1 = (s32[256]{0:T(256)S(1)}, s32[256]{0:T(256)}, u32[]{:S(2)}) copy-start(s32[256]{0:T(256)} %param.9) | copy-start | bytes 3076
  2.7 19.8 %collective-permute-start = (f32[24,8,384]{2,1,0:T(8,128)S(1)}, f32[24,8,384]{2,1,0:T(8,128)S(1)}, u32[]{:S(2)}, u32[]{:S(2)}) collective-permute-start(f32[24,8,384]{2,1,0:T(8,128)S(1)} %get-tuple-element.22.edge_cross), channel_id=1, source_target_pairs={{0,7},{1,2},{2,1},{3,4},{4,3},{5,6},{6,5},{7,0},{8,15},{9,10},{10,... | collective-permute-start | bytes 884744 | tf_op jit(solution)/shard_map/ppermute | solution.py:920
  6.1 16.3 %collective-permute-start.1 = (f32[24,8,384]{2,1,0:T(8,128)S(1)}, f32[24,8,384]{2,1,0:T(8,128)S(1)}, u32[]{:S(2)}, u32[]{:S(2)}) collective-permute-start(f32[24,8,384]{2,1,0:T(8,128)S(1)} %get-tuple-element.23.edge_same), channel_id=1, source_target_pairs={{0,1},{1,0},{2,3},{3,2},{4,5},{5,4},{6,7},{7,6},{8,9},{9,8},{10,11... | collective-permute-start | bytes 884744 | tf_op jit(solution)/shard_map/ppermute | solution.py:920
  6.1 15.1 %copy-start = (s32[8]{0:T(128)S(1)}, s32[8]{0:T(128)}, u32[]{:S(2)}) copy-start(s32[8]{0:T(128)} %param.7) | copy-start | bytes 100
  6.4 16.0 %copy-start.2 = (s32[8]{0:T(128)S(1)}, s32[8]{0:T(128)}, u32[]{:S(2)}) copy-start(s32[8]{0:T(128)} %param.8) | copy-start | bytes 100
  6.4 13.2 %collective-permute-start.2 = (f32[14,8,384]{2,1,0:T(8,128)S(1)}, f32[14,8,384]{2,1,0:T(8,128)S(1)}, u32[]{:S(2)}, u32[]{:S(2)}) collective-permute-start(f32[14,8,384]{2,1,0:T(8,128)S(1)} %get-tuple-element.28), channel_id=1, source_target_pairs={{0,24},{1,25},{2,26},{3,27},{4,28},{5,29},{6,30},{7,31},{8,0},{9,1... | collective-permute-start | bytes 516104 | tf_op jit(solution)/shard_map/ppermute | solution.py:920
  10.1 9.6 %collective-permute-start.3 = (f32[14,8,384]{2,1,0:T(8,128)S(1)}, f32[14,8,384]{2,1,0:T(8,128)S(1)}, u32[]{:S(2)}, u32[]{:S(2)}) collective-permute-start(f32[14,8,384]{2,1,0:T(8,128)S(1)} %get-tuple-element.29), channel_id=1, source_target_pairs={{0,8},{1,9},{2,10},{3,11},{4,12},{5,13},{6,14},{7,15},{8,16},{9,17... | collective-permute-start | bytes 516104 | tf_op jit(solution)/shard_map/ppermute | solution.py:920
  19.7 5.3 %collective-permute-start.4 = (f32[32,384]{1,0:T(8,128)S(1)}, f32[32,384]{1,0:T(8,128)S(1)}, u32[]{:S(2)}, u32[]{:S(2)}) collective-permute-start(f32[32,384]{1,0:T(8,128)S(1)} %get-tuple-element.30), channel_id=1, source_target_pairs={{0,7},{1,2},{2,1},{3,4},{4,3},{5,6},{6,5},{7,0},{8,15},{9,10},{10,... | collective-permute-start | bytes 147464 | tf_op jit(solution)/shard_map/ppermute | solution.py:920
  21.2 3.8 %collective-permute-start.5 = (f32[32,384]{1,0:T(8,128)S(1)}, f32[32,384]{1,0:T(8,128)S(1)}, u32[]{:S(2)}, u32[]{:S(2)}) collective-permute-start(f32[32,384]{1,0:T(8,128)S(1)} %get-tuple-element.31), channel_id=1, source_target_pairs={{0,1},{1,0},{2,3},{3,2},{4,5},{5,4},{6,7},{7,6},{8,9},{9,8},{10,11... | collective-permute-start | bytes 147464 | tf_op jit(solution)/shard_map/ppermute | solution.py:920
  21.3 3.8 %collective-permute-start.6 = (f32[4,8,128]{2,1,0:T(8,128)S(1)}, f32[4,8,128]{2,1,0:T(8,128)S(1)}, u32[]{:S(2)}, u32[]{:S(2)}) collective-permute-start(f32[4,8,128]{2,1,0:T(8,128)S(1)} %behind_plane.1), channel_id=1, source_target_pairs={{0,8},{1,9},{2,10},{3,11},{4,12},{5,13},{6,14},{7,15},{8,0},{9,1},... | collective-permute-start | bytes 49160 | tf_op jit(solution)/shard_map/ppermute | solution.py:927
